TPU v7x, 32 devices: a whole 2x2x4 slice. The times are simulated.
32 devices in a mesh: seq: 8 (over z, y), mat: 4 (over x, core).
Axes of the slice: x: 2, y: 2, z: 4, core: 2. Of those that a mesh axis runs over, the one named last changes fastest.
Arguments:
- token_ids: int32 [2, 4, 1024], P(None, 'mat'), may hold values from 0 to 50256
- expert_route: int32 [2, 4, 1024, 1], P(None, 'mat', 'seq'), may hold values from 0 to 7; in each aligned block of 128 rows (0 to 127, 128 to 255, ..., all dimensions but the last counted through in order) at most 32 rows name the same one
- doc_lengths: int32 [2, 4, 3], P(None, 'mat'), may hold values from 1 to 960, 1024 in all within a row
- loss_slots: int32 [2, 4, 256], P(None, 'mat', 'seq'), may hold values from 0 to 1023, as said below
- loss_weight: int32 [2, 4, 256], P(None, 'mat'), may hold values from 0 to 1
- target_ids: int32 [2, 4, 256], P(None, 'mat'), may hold values from 0 to 50256
- embedding: float32 [50304, 768], P('seq', 'mat')
- embedding_mom: float32 [50304, 768], P('seq', 'mat'), may hold values from -2.9802322e-07 to 2.9802322e-07
- embedding_sq: float32 [50304, 768], P('seq', 'mat'), may hold values from 5.1895214e-15 to 4.1915364e-14
- in_project: float32 [768, 3072], P(None, 'mat'), may hold values from -0.21875 to 0.21875
- in_project_mom: float32 [768, 3072], P(None, 'mat'), may hold values from -2.861023e-06 to 2.861023e-06
- out_project: float32 [1536, 768], P('mat'), may hold values from -0.15625 to 0.15625
- out_project_mom: float32 [1536, 768], P('mat'), may hold values from -2.861023e-06 to 2.861023e-06
- expert_up: float32 [8, 768, 3072], P('seq', None, 'mat'), may hold values from -0.21875 to 0.21875
- expert_up_mom: float32 [8, 768, 3072], P('seq', None, 'mat'), may hold values from -2.861023e-06 to 2.861023e-06
- expert_down: float32 [8, 3072, 768], P('seq', 'mat'), may hold values from -0.109375 to 0.109375
- expert_down_mom: float32 [8, 3072, 768], P('seq', 'mat'), may hold values from -2.861023e-06 to 2.861023e-06
- x_project: float32 [1536, 80], P('mat'), may hold values from -0.15625 to 0.15625
- x_project_mom: float32 [1536, 80], P('mat'), may hold values from -2.9802322e-07 to 2.9802322e-07
- x_project_sq: float32 [1536, 80], P('mat'), may hold values from 5.1895214e-15 to 4.1915364e-14
- step_project: float32 [48, 1536], P(None, 'mat'), may hold values from -0.875 to 0.875
- step_project_mom: float32 [48, 1536], P(None, 'mat'), may hold values from -2.9802322e-07 to 2.9802322e-07
- step_project_sq: float32 [48, 1536], P(None, 'mat'), may hold values from 5.1895214e-15 to 4.1915364e-14
- router_weight: float32 [768, 8], P('mat'), may hold values from -0.15625 to 0.15625
- router_mom: float32 [768, 8], P('mat'), may hold values from -2.9802322e-07 to 2.9802322e-07
- router_sq: float32 [768, 8], P('mat'), may hold values from 5.1895214e-15 to 4.1915364e-14
- channel_param: float32 [23, 1536], P(None, 'mat')
- channel_mom: float32 [23, 1536], P(None, 'mat'), may hold values from -1.1920929e-06 to 1.1920929e-06
- channel_sq: float32 [23, 1536], P(None, 'mat'), may hold values from 7.983879e-14 to 6.7862973e-13
- norm_gains: float32 [3, 768], P(None, 'mat')
- gains_mom: float32 [3, 768], P(None, 'mat'), may hold values from -1.1920929e-06 to 1.1920929e-06
- gains_sq: float32 [3, 768], P(None, 'mat'), may hold values from 7.983879e-14 to 6.7862973e-13
Outputs:
- loss_total: float32 [], replicated
- loss_count: float32 [], replicated
- grad_norm: float32 [], replicated
- row_loss: float32 [2, 4, 256], P(None, 'mat', 'seq')
- new_embedding: float32 [50304, 768], P('seq', 'mat')
- new_embedding_mom: float32 [50304, 768], P('seq', 'mat')
- new_embedding_sq: float32 [50304, 768], P('seq', 'mat')
- new_in_project: float32 [768, 3072], P(None, 'mat')
- new_in_project_mom: float32 [768, 3072], P(None, 'mat')
- new_out_project: float32 [1536, 768], P('mat')
- new_out_project_mom: float32 [1536, 768], P('mat')
- new_expert_up: float32 [8, 768, 3072], P('seq', None, 'mat')
- new_expert_up_mom: float32 [8, 768, 3072], P('seq', None, 'mat')
- new_expert_down: float32 [8, 3072, 768], P('seq', 'mat')
- new_expert_down_mom: float32 [8, 3072, 768], P('seq', 'mat')
- new_x_project: float32 [1536, 80], P('mat')
- new_x_project_mom: float32 [1536, 80], P('mat')
- new_x_project_sq: float32 [1536, 80], P('mat')
- new_step_project: float32 [48, 1536], P(None, 'mat')
- new_step_project_mom: float32 [48, 1536], P(None, 'mat')
- new_step_project_sq: float32 [48, 1536], P(None, 'mat')
- new_router: float32 [768, 8], P('mat')
- new_router_mom: float32 [768, 8], P('mat')
- new_router_sq: float32 [768, 8], P('mat')
- new_channel: float32 [23, 1536], P(None, 'mat')
- new_channel_mom: float32 [23, 1536], P(None, 'mat')
- new_channel_sq: float32 [23, 1536], P(None, 'mat')
- new_gains: float32 [3, 768], P(None, 'mat')
- new_gains_mom: float32 [3, 768], P(None, 'mat')
- new_gains_sq: float32 [3, 768], P(None, 'mat')
Inputs may be any that keep to these rules, and one draw needn't show every extreme that they name: `loss_slots`: each aligned block of 32 slots names different positions inside the matching block of 128 positions. `expert_route`: in each aligned block of 128 positions of a row (the positions of one device) no expert is named more than 32 times. `doc_lengths`: each row's lengths sum to 1024.
All inputs are finite; a program needn't handle non-finite values.
Results may differ from a plain program's by a relative error of at most 0.025.
The roundings to bfloat16 on the way count: a program that leaves them out, or rounds other values in their place, can miss the bound.
Values may be sent and summed in bfloat16 or wider, within the bound.
A program may use at most 512 MiB of HBM per device.

v0:
```python
import math

import jax
import jax.numpy as jnp
from jax import lax
from jax.sharding import PartitionSpec as P

D = 768
DI = 1536
FF = 3072
VOCAB_REAL = 50257
CONV = 4
ORTHO_STEPS = 5
STEP_COUNT = 10


HIGH = lax.Precision.HIGHEST
CLIP_NORM = 0.004
COEF_A = 3.4445
COEF_B = -4.775
COEF_C = 2.0315
MOMENTUM = 0.95
LR_MUON = 0.2
DECAY_MUON = 0.01
BETA_ONE = 0.9
BETA_TWO = 0.95
ADAM_EPS = 1e-08


def carried_in(part, axis, combine, identity, reverse):
    count = lax.axis_size(axis)
    place = lax.axis_index(axis)
    ahead = count - 1 - place if reverse else place
    gathered = jax.tree.map(lambda a: lax.all_gather(a, axis), part)
    state = jax.tree.map(lambda a, e: jnp.zeros_like(a) + jnp.asarray(e, a.dtype), part, identity)

    def one(lap, state):
        source = count - 1 - lap if reverse else lap
        return combine(
            state, jax.tree.map(lambda a: lax.dynamic_index_in_dim(a, source, 0, False), gathered)
        )

    return lax.fori_loop(0, ahead, one, state)


def from_behind(value, axis, steps):
    count = lax.axis_size(axis)
    leading, last = (max(0, -steps), min(count, count - steps))
    return lax.ppermute(value, axis, [(source, source + steps) for source in range(leading, last)])


def combined_all(part, axis, combine):
    gathered = jax.tree.map(lambda a: lax.all_gather(a, axis), part)

    def take(source):
        return jax.tree.map(lambda a: lax.dynamic_index_in_dim(a, source, 0, False), gathered)

    return lax.fori_loop(
        1, lax.axis_size(axis), lambda source, state: combine(state, take(source)), take(0)
    )


def apply_weight(low_left, weight):
    if weight.ndim == 3:
        return jnp.einsum("erk,ekn->ern", low_left, weight, preferred_element_type=jnp.float32)
    return jnp.dot(low_left, weight, preferred_element_type=jnp.float32)


def product_plain(left, weight):
    return apply_weight(left.astype(jnp.bfloat16), weight)


def product_keep(left, weight, holder):
    low_left = left.astype(jnp.bfloat16)
    return (apply_weight(low_left, weight), (low_left, weight))


def product_back(kept, grad):
    low_left, weight = kept
    low_grad = grad.astype(jnp.bfloat16)
    if weight.ndim == 3:
        left_grad = jnp.einsum("ern,ekn->erk", low_grad, weight, preferred_element_type=jnp.float32)
        weight_grad = jnp.einsum(
            "erk,ern->ekn", low_left, low_grad, preferred_element_type=jnp.float32
        )
    else:
        left_grad = lax.dot_general(
            low_grad, weight, (((1,), (1,)), ((), ())), preferred_element_type=jnp.float32
        )
        weight_grad = lax.dot_general(
            low_left, low_grad, (((0,), (0,)), ((), ())), preferred_element_type=jnp.float32
        )
    return (left_grad, jnp.zeros_like(weight), weight_grad)


def product(left, weight, holder):

    def inner_product(left_in, weight_in, holder_in):
        return product_plain(left_in, weight_in)

    wrapped = jax.custom_vjp(inner_product)
    wrapped.defvjp(product_keep, product_back)
    return wrapped(left, weight, holder)


def normalize(values, gain):
    return values * lax.rsqrt(jnp.mean(values * values, axis=-1, keepdims=True) + 1e-05) * gain


def empty_like(weight):
    return jnp.zeros(weight.shape, jnp.float32)


def link_states(earlier, later):
    return (earlier[0] * later[0], later[0] * earlier[1] + later[1])


def carry_states(decay, state, backward):
    return carried_in(
        (decay, state), "seq", link_states, (jnp.ones_like(decay), jnp.zeros_like(state)), backward
    )[1]


def move_rows(values, offset):
    return from_behind(values, "seq", offset)


def send_experts(values):
    return lax.all_to_all(values, "seq", split_axis=0, concat_axis=0, tiled=True)


def return_experts(values):
    return lax.all_to_all(values, "seq", split_axis=0, concat_axis=0, tiled=True)


def expert_layout(values, local_experts, capacity):
    sources, _, width = values.shape
    return (
        values.reshape(sources, local_experts, capacity, width)
        .transpose(1, 0, 2, 3)
        .reshape(local_experts, sources * capacity, width)
    )


def token_layout(values, sources, capacity):
    local_experts, _, width = values.shape
    return (
        values.reshape(local_experts, sources, capacity, width)
        .transpose(1, 0, 2, 3)
        .reshape(sources, local_experts * capacity, width)
    )


def merge_stats(first_part, second_part):
    largest = jnp.maximum(first_part[0], second_part[0])
    summed = first_part[1] * jnp.exp(first_part[0] - largest) + second_part[1] * jnp.exp(
        second_part[0] - largest
    )
    return (largest, summed, first_part[2] + second_part[2])


def sum_copies(g_in, g_out, g_x, g_step, g_route, g_chan, g_gain):
    return lax.psum((g_in, g_out, g_x, g_step, g_route, g_chan, g_gain), "seq")


def sum_shards(g_table, g_in, g_out, g_up, g_down, g_x, g_step, g_route, g_chan, g_gain):
    return (
        lax.psum_scatter(g_table, "mat", scatter_dimension=1, tiled=True),
        lax.psum_scatter(g_in, "mat", scatter_dimension=1, tiled=True),
        lax.psum_scatter(g_out, "mat", scatter_dimension=0, tiled=True),
        lax.psum_scatter(g_up, "mat", scatter_dimension=2, tiled=True),
        lax.psum_scatter(g_down, "mat", scatter_dimension=1, tiled=True),
        lax.psum_scatter(g_x, "mat", scatter_dimension=0, tiled=True),
        lax.psum_scatter(g_step, "mat", scatter_dimension=1, tiled=True),
        lax.psum_scatter(g_route, "mat", scatter_dimension=0, tiled=True),
        lax.psum_scatter(g_chan, "mat", scatter_dimension=1, tiled=True),
        lax.psum_scatter(g_gain, "mat", scatter_dimension=1, tiled=True),
    )


def micro_step(weights, ids, route, lengths, slots, weight_mask, targets, loss_all):
    table, w_in, w_out, w_up, w_down, w_x, w_step, w_route, chan_low, gains_low = weights
    channel = chan_low.astype(jnp.float32)
    gains = gains_low.astype(jnp.float32)
    seq_index = lax.axis_index("seq")
    seq_count = lax.axis_size("seq")
    tokens = route.shape[0]
    dmodel = w_in.shape[0]
    inner = w_in.shape[1] // 2
    vocab_part = table.shape[0]
    first_pos = seq_index * tokens
    vocab_start = seq_index * vocab_part
    ext_pos = first_pos - (CONV - 1) + jnp.arange(tokens + CONV - 1, dtype=jnp.int32)
    bounds = jnp.cumsum(lengths)
    ext_doc = jnp.sum((ext_pos[:, None] >= bounds[None, :-1]).astype(jnp.int32), axis=1)
    ext_doc = jnp.where(ext_pos >= 0, ext_doc, -1)
    starts = jnp.concatenate([jnp.zeros((1,), jnp.int32), bounds[:-1]])
    keeping = 1.0 - jnp.any(ext_pos[CONV - 1 :, None] == starts[None, :], axis=1).astype(
        jnp.float32
    )
    alive = jnp.cumprod(keeping)
    own_doc = ext_doc[CONV - 1 :]
    sameness = [
        (ext_doc[tap_index : tap_index + tokens] == own_doc).astype(jnp.float32)
        for tap_index in range(CONV)
    ]
    local_ids = ids - vocab_start
    inside = (local_ids >= 0) & (local_ids < vocab_part)
    picked = jnp.take(table, jnp.clip(local_ids, 0, vocab_part - 1), axis=0)
    resid = lax.psum_scatter(
        jnp.where(inside[:, None], picked.astype(jnp.float32), 0.0).astype(jnp.bfloat16),
        "seq",
        scatter_dimension=0,
        tiled=True,
    ).astype(jnp.float32)

    def mixer_entry(gain, holder, resid_in):
        return product(normalize(resid_in, gain), w_in, holder)

    halves, back_entry = jax.vjp(mixer_entry, gains[0], empty_like(w_in), resid)
    raw_half = halves[:, :inner]
    gate_half = halves[:, inner:]
    edge_rows = move_rows(raw_half[tokens - (CONV - 1) :], 1)
    padded = jnp.concatenate([edge_rows, raw_half], axis=0)

    def mixer_core(chan_in, holder_x, holder_step, padded_in):
        convolved = chan_in[CONV] + jnp.zeros((tokens, inner), jnp.float32)
        for tap_index in range(CONV):
            convolved = (
                convolved
                + chan_in[tap_index]
                * padded_in[tap_index : tap_index + tokens]
                * sameness[tap_index][:, None]
            )
        activated = jax.nn.silu(convolved)
        projected = product(activated, w_x, holder_x)
        rank_width = w_step.shape[0]
        states = (projected.shape[1] - rank_width) // 2
        inject = projected[:, rank_width : rank_width + states]
        readout = projected[:, rank_width + states :]
        step_size = jax.nn.softplus(
            product(projected[:, :rank_width], w_step, holder_step) + chan_in[CONV + 1]
        )
        rate = -jnp.exp(chan_in[CONV + 3 :])

        def advance(state, item):
            x_item, step_item, inject_item, read_item, keep_item = item
            state = (
                jnp.exp(rate * step_item[None, :]) * keep_item * state
                + inject_item[:, None] * (step_item * x_item)[None, :]
            )
            return (state, jnp.dot(read_item, state, precision=HIGH))

        state_end, scanned = lax.scan(
            advance,
            jnp.zeros((states, inner), jnp.float32),
            (activated, step_size, inject, readout, keeping),
            unroll=8,
        )
        cumulative = jnp.cumsum(step_size, axis=0)
        decay_total = jnp.exp(rate * cumulative[-1][None, :]) * alive[-1]
        return (scanned, activated, readout, cumulative, decay_total, state_end)

    core_out, back_core = jax.vjp(mixer_core, channel, empty_like(w_x), empty_like(w_step), padded)
    scanned, activated, readout, cumulative, decay_total, state_end = core_out
    state_start = carry_states(decay_total, state_end, False)

    def mixer_exit(
        chan_in,
        holder,
        scanned_in,
        activated_in,
        gate_in,
        readout_in,
        cumulative_in,
        start_in,
        resid_in,
    ):
        rate = -jnp.exp(chan_in[CONV + 3 :])
        decay = jnp.exp(rate[None, :, :] * cumulative_in[:, None, :]) * alive[:, None, None]
        carried = jnp.einsum("tn,tnd->td", readout_in, decay * start_in[None, :, :], precision=HIGH)
        mixed = (scanned_in + carried + chan_in[CONV + 2] * activated_in) * jax.nn.silu(gate_in)
        return resid_in + product(mixed, w_out, holder)

    resid_mid, back_exit = jax.vjp(
        mixer_exit,
        channel,
        empty_like(w_out),
        scanned,
        activated,
        gate_half,
        readout,
        cumulative,
        state_start,
        resid,
    )
    experts = w_route.shape[1]
    capacity = max(2, 2 * tokens // experts)
    chosen = route[:, None] == jnp.arange(experts, dtype=jnp.int32)[None, :]

    def router_piece(gain, holder, resid_in):
        normed = normalize(resid_in, gain)
        scores = product(normed, w_route, holder)
        return (normed, jax.nn.sigmoid(jnp.sum(jnp.where(chosen, scores, 0.0), axis=1)))

    (normed, gate), back_router = jax.vjp(router_piece, gains[1], empty_like(w_route), resid_mid)
    onehot = chosen.astype(jnp.int32)
    ranking = jnp.sum(jnp.cumsum(onehot, axis=0) * onehot, axis=1) - 1
    placed = route * capacity + ranking
    sender = (placed[None, :] == jnp.arange(experts * capacity, dtype=jnp.int32)[:, None]).astype(
        jnp.bfloat16
    )
    outgoing = jnp.dot(
        sender, normed.astype(jnp.bfloat16), preferred_element_type=jnp.float32
    ).astype(jnp.bfloat16)
    arrived = send_experts(outgoing.reshape(seq_count, -1, dmodel))
    local_experts = w_up.shape[0]
    taken = expert_layout(arrived, local_experts, capacity)

    def expert_piece(holder_up, holder_down, taken_in):
        hidden = jax.nn.gelu(product(taken_in, w_up, holder_up), approximate=False)
        return product(hidden, w_down, holder_down)

    result, back_expert = jax.vjp(
        expert_piece, empty_like(w_up), empty_like(w_down), taken.astype(jnp.float32)
    )
    returned = return_experts(token_layout(result.astype(jnp.bfloat16), seq_count, capacity))
    combined = lax.dot_general(
        sender,
        returned.reshape(experts * capacity, dmodel),
        (((0,), (0,)), ((), ())),
        preferred_element_type=jnp.float32,
    )

    def mixture_piece(gate_in, combined_in, resid_in):
        return resid_in + gate_in[:, None] * combined_in

    resid_out, back_mixture = jax.vjp(mixture_piece, gate, combined, resid_mid)

    def final_piece(gain, resid_in):
        return normalize(resid_in, gain)

    final_hidden, back_final = jax.vjp(final_piece, gains[2], resid_out)
    own_count = slots.shape[0]
    local_rows = slots - first_pos
    picked_rows = jnp.take(final_hidden, local_rows, axis=0).astype(jnp.bfloat16)
    every_row = lax.all_gather(picked_rows, "seq", axis=0, tiled=True)
    logits = lax.dot_general(
        every_row, table, (((1,), (1,)), ((), ())), preferred_element_type=jnp.float32
    )
    column = vocab_start + jnp.arange(vocab_part, dtype=jnp.int32)
    valid = column < VOCAB_REAL
    masked = jnp.where(valid[None, :], logits, -1e30)
    largest = jnp.max(masked, axis=1)
    expsum = jnp.sum(jnp.exp(masked - largest[:, None]), axis=1)
    hitting = column[None, :] == targets[:, None]
    target_logit = jnp.sum(jnp.where(hitting, logits, 0.0), axis=1)
    top_all, sum_all, target_all = combined_all((largest, expsum, target_logit), "seq", merge_stats)
    lse = top_all + jnp.log(sum_all)
    counted = weight_mask.astype(jnp.float32)
    unweighted = lse - target_all
    row_loss = unweighted * counted
    loss_here = jnp.sum(lax.dynamic_slice_in_dim(row_loss, seq_index * own_count, own_count))
    count_here = jnp.sum(lax.dynamic_slice_in_dim(counted, seq_index * own_count, own_count))
    rows_here = lax.dynamic_slice_in_dim(unweighted, seq_index * own_count, own_count)
    probability = jnp.where(valid[None, :], jnp.exp(masked - lse[:, None]), 0.0)
    logit_grad = (
        (counted / loss_all)[:, None] * (probability - hitting.astype(jnp.float32))
    ).astype(jnp.bfloat16)
    table_grad = lax.dot_general(
        logit_grad, every_row, (((0,), (0,)), ((), ())), preferred_element_type=jnp.float32
    )
    block = lax.slice_in_dim(logit_grad, 0, own_count * lax.axis_size("seq"), axis=0)
    picked_grad = lax.psum_scatter(
        jnp.dot(block, table, preferred_element_type=jnp.float32),
        "seq",
        scatter_dimension=0,
        tiled=True,
    )
    final_grad = jnp.zeros((tokens, dmodel), jnp.float32).at[local_rows].add(picked_grad)
    gain_two, resid_out_grad = back_final(final_grad)
    gate_grad, combined_grad, resid_mid_grad = back_mixture(resid_out_grad)
    back_rows = jnp.dot(
        sender, combined_grad.astype(jnp.bfloat16), preferred_element_type=jnp.float32
    ).astype(jnp.bfloat16)
    arrived_grad = expert_layout(
        send_experts(back_rows.reshape(seq_count, -1, dmodel)), local_experts, capacity
    )
    up_grad, down_grad, taken_grad = back_expert(arrived_grad.astype(jnp.float32))
    returned_grad = return_experts(
        token_layout(taken_grad.astype(jnp.bfloat16), seq_count, capacity)
    )
    normed_grad = lax.dot_general(
        sender,
        returned_grad.reshape(experts * capacity, dmodel),
        (((0,), (0,)), ((), ())),
        preferred_element_type=jnp.float32,
    )
    gain_one, route_grad, resid_mid_more = back_router((normed_grad, gate_grad))
    resid_mid_grad = resid_mid_grad + resid_mid_more
    (
        chan_exit,
        out_grad,
        scanned_grad,
        activated_grad,
        gate_half_grad,
        readout_grad,
        cumulative_grad,
        start_grad,
        resid_grad,
    ) = back_exit(resid_mid_grad)
    later_grad = carry_states(decay_total, start_grad, True)
    chan_core, x_grad, step_grad, padded_grad = back_core(
        (
            scanned_grad,
            activated_grad,
            readout_grad,
            cumulative_grad,
            later_grad * state_start,
            later_grad,
        )
    )
    edge_grad = move_rows(padded_grad[: CONV - 1], -1)
    raw_grad = padded_grad[CONV - 1 :].at[tokens - (CONV - 1) :].add(edge_grad)
    gain_zero, in_grad, resid_more = back_entry(jnp.concatenate([raw_grad, gate_half_grad], axis=1))
    first_grad = (resid_grad + resid_more).astype(jnp.bfloat16)
    every_grad = lax.all_gather(first_grad, "seq", axis=0, tiled=True)
    local_ids = ids - vocab_start
    target_rows = jnp.where((local_ids >= 0) & (local_ids < vocab_part), local_ids, vocab_part)
    table_grad = table_grad.at[target_rows].add(every_grad.astype(jnp.float32), mode="drop")
    gain_grads = jnp.stack([gain_zero, gain_one, gain_two])
    grads = (
        table_grad,
        in_grad,
        out_grad,
        up_grad,
        down_grad,
        x_grad,
        step_grad,
        route_grad,
        chan_exit + chan_core,
        gain_grads,
    )
    return (grads, loss_here, count_here, rows_here)


def orthogonalize(views):
    current = list(views)
    for sweep in range(ORTHO_STEPS):
        rounded = [view.astype(jnp.bfloat16) for view in current]
        parts = [
            jnp.einsum(
                "...mk,...jk->...mj", piece, piece, preferred_element_type=jnp.float32
            ).astype(jnp.bfloat16)
            for piece in rounded
        ]
        grams = list(
            (
                lax.psum(parts[0], "mat").astype(jnp.float32),
                lax.psum(parts[1], "mat").astype(jnp.float32),
                lax.psum(parts[2], "mat").astype(jnp.float32),
                lax.psum(parts[3], "mat").astype(jnp.float32),
            )
        )
        if sweep == 0:
            factors = [
                (1.0 / (jnp.sqrt(jnp.trace(gram, axis1=-2, axis2=-1)) + 1e-07))[..., None, None]
                for gram in grams
            ]
            current = [
                piece.astype(jnp.float32) * factor for piece, factor in zip(rounded, factors)
            ]
            grams = [gram * factor * factor for gram, factor in zip(grams, factors)]
        current = [
            COEF_A * matrix
            + jnp.matmul(
                COEF_B * gram + COEF_C * jnp.matmul(gram, gram, precision=HIGH),
                matrix,
                precision=HIGH,
            )
            for matrix, gram in zip(current, grams)
        ]
    return current


def adamw_update(weight, mean, square, grad, rate, decay):
    mean = BETA_ONE * mean + (1.0 - BETA_ONE) * grad
    square = BETA_TWO * square + (1.0 - BETA_TWO) * grad * grad
    ratio = (
        mean
        / (1.0 - BETA_ONE**STEP_COUNT)
        / (jnp.sqrt(square / (1.0 - BETA_TWO**STEP_COUNT)) + ADAM_EPS)
    )
    return (weight * (1.0 - rate * decay) - rate * ratio, mean, square)


def local(
    token_ids,
    expert_route,
    doc_lengths,
    loss_slots,
    loss_weight,
    target_ids,
    embedding,
    embedding_mom,
    embedding_sq,
    in_project,
    in_project_mom,
    out_project,
    out_project_mom,
    expert_up,
    expert_up_mom,
    expert_down,
    expert_down_mom,
    x_project,
    x_project_mom,
    x_project_sq,
    step_project,
    step_project_mom,
    step_project_sq,
    router_weight,
    router_mom,
    router_sq,
    channel_param,
    channel_mom,
    channel_sq,
    norm_gains,
    gains_mom,
    gains_sq,
):
    gathered = (
        lax.all_gather(embedding.astype(jnp.bfloat16), "mat", axis=1, tiled=True),
        lax.all_gather(in_project.astype(jnp.bfloat16), "mat", axis=1, tiled=True),
        lax.all_gather(out_project.astype(jnp.bfloat16), "mat", axis=0, tiled=True),
        lax.all_gather(expert_up.astype(jnp.bfloat16), "mat", axis=2, tiled=True),
        lax.all_gather(expert_down.astype(jnp.bfloat16), "mat", axis=1, tiled=True),
        lax.all_gather(x_project.astype(jnp.bfloat16), "mat", axis=0, tiled=True),
        lax.all_gather(step_project.astype(jnp.bfloat16), "mat", axis=1, tiled=True),
        lax.all_gather(router_weight.astype(jnp.bfloat16), "mat", axis=0, tiled=True),
        lax.all_gather(channel_param.astype(jnp.bfloat16), "mat", axis=1, tiled=True),
        lax.all_gather(norm_gains.astype(jnp.bfloat16), "mat", axis=1, tiled=True),
    )
    micro_count = token_ids.shape[0]
    loss_all = micro_count * lax.axis_size("mat") * loss_weight.shape[2]
    summed = None
    loss_part = jnp.zeros((), jnp.float32)
    count_part = jnp.zeros((), jnp.float32)
    row_parts = []
    for micro_index in range(micro_count):
        grads, loss_here, count_here, rows_here = micro_step(
            gathered,
            token_ids[micro_index, 0],
            expert_route[micro_index, 0, :, 0],
            doc_lengths[micro_index, 0],
            loss_slots[micro_index, 0],
            loss_weight[micro_index, 0],
            target_ids[micro_index, 0],
            loss_all,
        )
        summed = (
            grads
            if summed is None
            else tuple((older + newer for older, newer in zip(summed, grads)))
        )
        loss_part = loss_part + loss_here
        count_part = count_part + count_here
        row_parts.append(rows_here)
    row_loss = jnp.stack(row_parts)[:, None, :]
    copies = sum_copies(summed[1], summed[2], summed[5], summed[6], summed[7], summed[8], summed[9])
    shards = sum_shards(
        summed[0],
        copies[0],
        copies[1],
        summed[3],
        summed[4],
        copies[2],
        copies[3],
        copies[4],
        copies[5],
        copies[6],
    )
    seq_count = lax.axis_size("seq")
    owned = (
        jnp.sum(shards[0] * shards[0])
        + jnp.sum(shards[3] * shards[3])
        + jnp.sum(shards[4] * shards[4])
    )
    shared = jnp.zeros((), jnp.float32)
    for index in (1, 2, 5, 6, 7, 8, 9):
        shared = shared + jnp.sum(shards[index] * shards[index])
    squares, loss_total, loss_count = lax.psum(
        (owned + shared / seq_count, loss_part, count_part), ("seq", "mat")
    )
    grad_norm = jnp.sqrt(squares)
    scale = jnp.minimum(1.0, CLIP_NORM / (grad_norm + 1e-06))
    clipped = tuple((grad * scale for grad in shards))
    mom_in = MOMENTUM * in_project_mom + clipped[1]
    mom_out = MOMENTUM * out_project_mom + clipped[2]
    mom_up = MOMENTUM * expert_up_mom + clipped[3]
    mom_down = MOMENTUM * expert_down_mom + clipped[4]
    ortho = orthogonalize((mom_in, mom_out.T, mom_up, jnp.swapaxes(mom_down, 1, 2)))
    shrink = 1.0 - LR_MUON * DECAY_MUON
    new_in = in_project * shrink - LR_MUON * 0.2 * math.sqrt(max(D, 2 * DI)) * ortho[0]
    new_out = out_project * shrink - LR_MUON * 0.2 * math.sqrt(max(D, DI)) * ortho[1].T
    new_up = expert_up * shrink - LR_MUON * 0.2 * math.sqrt(max(D, FF)) * ortho[2]
    new_down = expert_down * shrink - LR_MUON * 0.2 * math.sqrt(max(D, FF)) * jnp.swapaxes(
        ortho[3], 1, 2
    )
    table_new = adamw_update(embedding, embedding_mom, embedding_sq, clipped[0], 0.05, 0.1)
    x_new = adamw_update(x_project, x_project_mom, x_project_sq, clipped[5], 0.06, 0.1)
    step_new = adamw_update(step_project, step_project_mom, step_project_sq, clipped[6], 0.06, 0.1)
    route_new = adamw_update(router_weight, router_mom, router_sq, clipped[7], 0.06, 0.1)
    chan_new = adamw_update(channel_param, channel_mom, channel_sq, clipped[8], 1.0, 0.0)
    gains_new = adamw_update(norm_gains, gains_mom, gains_sq, clipped[9], 0.4, 0.0)
    return (
        loss_total,
        loss_count,
        grad_norm,
        row_loss,
        table_new[0],
        table_new[1],
        table_new[2],
        new_in,
        mom_in,
        new_out,
        mom_out,
        new_up,
        mom_up,
        new_down,
        mom_down,
        x_new[0],
        x_new[1],
        x_new[2],
        step_new[0],
        step_new[1],
        step_new[2],
        route_new[0],
        route_new[1],
        route_new[2],
        chan_new[0],
        chan_new[1],
        chan_new[2],
        gains_new[0],
        gains_new[1],
        gains_new[2],
    )


def solution(mesh):
    in_specs = (
        P(None, "mat", None),
        P(None, "mat", "seq", None),
        P(None, "mat", None),
        P(None, "mat", "seq"),
        P(None, "mat", None),
        P(None, "mat", None),
        P("seq", "mat"),
        P("seq", "mat"),
        P("seq", "mat"),
        P(None, "mat"),
        P(None, "mat"),
        P("mat", None),
        P("mat", None),
        P("seq", None, "mat"),
        P("seq", None, "mat"),
        P("seq", "mat", None),
        P("seq", "mat", None),
        P("mat", None),
        P("mat", None),
        P("mat", None),
        P(None, "mat"),
        P(None, "mat"),
        P(None, "mat"),
        P("mat", None),
        P("mat", None),
        P("mat", None),
        P(None, "mat"),
        P(None, "mat"),
        P(None, "mat"),
        P(None, "mat"),
        P(None, "mat"),
        P(None, "mat"),
    )
    out_specs = (
        P(),
        P(),
        P(),
        P(None, "mat", "seq"),
        P("seq", "mat"),
        P("seq", "mat"),
        P("seq", "mat"),
        P(None, "mat"),
        P(None, "mat"),
        P("mat", None),
        P("mat", None),
        P("seq", None, "mat"),
        P("seq", None, "mat"),
        P("seq", "mat", None),
        P("seq", "mat", None),
        P("mat", None),
        P("mat", None),
        P("mat", None),
        P(None, "mat"),
        P(None, "mat"),
        P(None, "mat"),
        P("mat", None),
        P("mat", None),
        P("mat", None),
        P(None, "mat"),
        P(None, "mat"),
        P(None, "mat"),
        P(None, "mat"),
        P(None, "mat"),
        P(None, "mat"),
    )
    return jax.shard_map(local, mesh=mesh, in_specs=in_specs, out_specs=out_specs, check_vma=False)
```

profile of v0, /device:TPU:0, one launch (start us, length us, event | category | flops | bytes accessed | tf_op | source)
XLA Modules:
  0.0 4612.9 jit_solution(17768630943053459729)
XLA Ops:
  12.1 68.6 %all-gather.28.cloned.1.call-done = bf16[6288,768]{0,1:T(8,128)(2,1)} async-done(((bf16[6288,192]{0,1:T(8,128)(2,1)}), bf16[6288,768]{0,1:T(8,128)(2,1)}) %all-gather.28.cloned.1.call-update) | async-done | bytes 9658384 | tf_op jit(solution)/shard_map/all_gather | solution.py:532
  174.1 37.6 all-gather.30.cloned.1.call-done
  218.4 62.3 %reduce-scatter.21.cloned.1.call-done = bf16[128,768]{1,0:T(8,128)(2,1)} async-done(((bf16[1024,768]{1,0:T(8,128)(2,1)}), bf16[128,768]{1,0:T(8,128)(2,1)}) %reduce-scatter.21.cloned.1.call-update) | async-done | bytes 196624 | tf_op jit(solution)/shard_map/reduce_scatter | solution.py:210
  337.5 408.8 %while.203 = (s32[]{:T(128)}, f32[16,1536]{1,0:T(8,128)S(1)}, f32[16,8,1536]{2,1,0:T(8,128)}, f32[16,8,1,1536]{3,2,1,0:T(1,128)}, f32[16,8,16,1536]{3,2,1,0:T(8,...) while((s32[]{:T(128)}, f32[16,1536]{1,0:T(8,128)S(1)}, ...), condition=%wide.region_28.32_spmd.clone, body=%wide.region_27.31_spmd.clone.sunk | while | flops 3784708 | bytes 13864079 | solution.py:254
  746.3 34.5 all-gather.6
  780.8 34.0 all-gather.5
  844.8 407.7 %while.202 = (s32[]{:T(128)}, f32[16,1536]{1,0:T(8,128)S(1)}, f32[16,8,1536]{2,1,0:T(8,128)}, f32[16,8,1,1536]{3,2,1,0:T(1,128)}, f32[16,8,16,1536]{3,2,1,0:T(8,...) while((s32[]{:T(128)}, f32[16,1536]{1,0:T(8,128)S(1)}, ...), condition=%wide.region_6.9_spmd.clone, body=%wide.region_5.8_spmd.clone.sunk | while | flops 3784708 | bytes 13864079 | solution.py:254
  1252.5 39.7 all-gather.1
  1292.2 33.9 all-gather
  1439.7 33.2 all_gather.128
  1476.1 31.4 all_gather.139
  1660.6 47.7 %reduce-scatter.27.cloned.1.call-done = f32[32,768]{1,0:T(8,128)} async-done(((f32[256,768]{1,0:T(8,128)}), f32[32,768]{1,0:T(8,128)}) %reduce-scatter.27.cloned.1.call-update) | async-done | bytes 98320 | tf_op jit(solution)/shard_map/reduce_scatter | solution.py:374
  1709.6 64.4 %reduce-scatter.25.cloned.1.call-done = f32[32,768]{1,0:T(8,128)} async-done(((f32[256,768]{1,0:T(8,128)}), f32[32,768]{1,0:T(8,128)}) %reduce-scatter.25.cloned.1.call-update) | async-done | bytes 98320 | tf_op jit(solution)/shard_map/reduce_scatter | solution.py:374
  1874.9 32.5 all-gather.10
  1917.4 471.8 %while.204 = (s32[]{:T(128)}, f32[16,1536]{1,0:T(8,128)S(1)}, f32[16,1536]{1,0:T(8,128)S(1)}, f32[16,8,1536]{2,1,0:T(8,128)}, f32[16,8,1536]{2,1,0:T(8,128)}, /*...) while((s32[]{:T(128)}, f32[16,1536]{1,0:T(8,128)S(1)}, ...), condition=%wide.region_81.85_spmd.clone, body=%wide.region_56.84_spmd.clone.sunk | while | flops 5197707 | bytes 8050511 | solution.py:254
  2389.2 32.2 all-gather.11
  2431.4 512.1 %while.205 = (s32[]{:T(128)}, f32[16,1536]{1,0:T(8,128)}, f32[16,1536]{1,0:T(8,128)S(1)}, f32[16,8,1536]{2,1,0:T(8,128)}, f32[16,8,1536]{2,1,0:T(8,128)}, /*inde...) while((s32[]{:T(128)}, f32[16,1536]{1,0:T(8,128)}, ...), condition=%wide.region_119.123_spmd.clone, body=%wide.region_94.122_spmd.clone.sunk | while | flops 5197707 | bytes 8050511 | solution.py:254
  3113.9 81.1 %reduce-scatter.33.cloned.1.call-done = f32[768,768]{0,1:T(8,128)} async-done(((f32[768,3072]{0,1:T(8,128)}), f32[768,768]{0,1:T(8,128)}) %reduce-scatter.33.cloned.1.call-update) | async-done | bytes 2359312 | tf_op jit(solution)/shard_map/reduce_scatter | solution.py:169
  3217.9 23.9 all-gather.38.cloned.1.call-done
  3241.8 45.6 all-gather.40.cloned.1.call-done
  3287.4 28.5 scatter_custom_fusion.2
  3356.3 38.3 all-reduce.35
  3396.4 40.9 reduce-scatter.31.cloned.1.call-done
  3440.2 78.1 %reduce-scatter.29.cloned.1.call-done = f32[1,768,768]{2,1,0:T(8,128)} async-done(((f32[1,768,3072]{2,1,0:T(8,128)}), f32[1,768,768]{2,1,0:T(8,128)}) %reduce-scatter.29.cloned.1.call-update) | async-done | bytes 2359312 | tf_op jit(solution)/shard_map/reduce_scatter | solution.py:171
  3521.2 146.5 %all-reduce.49.cloned.1.call-done = (f32[768,768]{0,1:T(8,128)}, f32[384,768]{1,0:T(8,128)}, f32[384,80]{0,1:T(8,128)}, f32[48,384]{1,0:T(8,128)}) async-done(((f32[768,768]{0,1:T(8,128)}, f32[384,768]{1,0:T(8,128)}, f32[384,80]{0,1:T(8,128)}, f32[48,384]{1,0:T(8,128)}), (f32[768,768]{0,1:T(8,128)}, f32[384,768]{1,0:T(8,128)}, f32[384,80]{0,1:T(8,128)}, f32[48,384]{1,0:T(8,128)})) %all-reduce.49.cloned.1.call-update) | async-done | bytes 3735568 | tf_op jit(solution)/shard_map/psum | solution.py:163
  3678.7 135.3 %reduce-scatter.43.cloned.1.call-done = f32[192,6288]{1,0:T(8,128)} async-done(((f32[768,6288]{1,0:T(8,128)}), f32[192,6288]{1,0:T(8,128)}) %reduce-scatter.43.cloned.1.call-update) | async-done | bytes 4829200
  3830.5 39.3 all-reduce.34
  3886.6 95.4 %all-reduce.59.cloned.1.call-done = (bf16[768,768]{0,1:T(8,128)(2,1)}, bf16[768,768]{0,1:T(8,128)(2,1)}, bf16[1,768,768]{1,2,0:T(8,128)(2,1)}, bf16[1,768,768]{1,2,0:T(8,128)(2,1)}) async-done(((bf16[768,768]{0,1:T(8,128)(2,1)}, bf16[768,768]{0,1:T(8,128)(2,1)}, bf16[1,768,768]{1,2,0:T(8,128)(2,1)}, bf16[1,768,768]{1,2,0:T(8,128)(2,1)}), (bf16[768,768]{0,1:T(8,128)(2,1)}, bf16[768,768]{0,1:T(8,128)(2,1)}, ...) | async-done | bytes 4718608 | tf_op jit(solution)/shard_map/psum | solution.py:459
  4054.0 94.8 %all-reduce.57.cloned.1.call-done = (bf16[768,768]{0,1:T(8,128)(2,1)}, bf16[768,768]{0,1:T(8,128)(2,1)}, bf16[1,768,768]{1,2,0:T(8,128)(2,1)}, bf16[1,768,768]{1,2,0:T(8,128)(2,1)}) async-done(((bf16[768,768]{0,1:T(8,128)(2,1)}, bf16[768,768]{0,1:T(8,128)(2,1)}, bf16[1,768,768]{1,2,0:T(8,128)(2,1)}, bf16[1,768,768]{1,2,0:T(8,128)(2,1)}), (bf16[768,768]{0,1:T(8,128)(2,1)}, bf16[768,768]{0,1:T(8,128)(2,1)}, ...) | async-done | bytes 4718608 | tf_op jit(solution)/shard_map/psum | solution.py:459
  4191.3 94.8 %all-reduce.55.cloned.1.call-done = (bf16[768,768]{0,1:T(8,128)(2,1)}, bf16[768,768]{0,1:T(8,128)(2,1)}, bf16[1,768,768]{1,2,0:T(8,128)(2,1)}, bf16[1,768,768]{1,2,0:T(8,128)(2,1)}) async-done(((bf16[768,768]{0,1:T(8,128)(2,1)}, bf16[768,768]{0,1:T(8,128)(2,1)}, bf16[1,768,768]{1,2,0:T(8,128)(2,1)}, bf16[1,768,768]{1,2,0:T(8,128)(2,1)}), (bf16[768,768]{0,1:T(8,128)(2,1)}, bf16[768,768]{0,1:T(8,128)(2,1)}, ...) | async-done | bytes 4718608 | tf_op jit(solution)/shard_map/psum | solution.py:459
  4350.6 71.7 %all-reduce.53.cloned.1.call-done = (bf16[768,768]{0,1:T(8,128)(2,1)}, bf16[768,768]{0,1:T(8,128)(2,1)}, bf16[1,768,768]{1,2,0:T(8,128)(2,1)}, bf16[1,768,768]{1,2,0:T(8,128)(2,1)}) async-done(((bf16[768,768]{0,1:T(8,128)(2,1)}, bf16[768,768]{0,1:T(8,128)(2,1)}, bf16[1,768,768]{1,2,0:T(8,128)(2,1)}, bf16[1,768,768]{1,2,0:T(8,128)(2,1)}), (bf16[768,768]{0,1:T(8,128)(2,1)}, bf16[768,768]{0,1:T(8,128)(2,1)}, ...) | async-done | bytes 4718608 | tf_op jit(solution)/shard_map/psum | solution.py:459
  4511.4 47.3 %all-reduce.51.cloned.1.call-done = (bf16[768,768]{0,1:T(8,128)(2,1)}, bf16[768,768]{0,1:T(8,128)(2,1)}, bf16[1,768,768]{1,2,0:T(8,128)(2,1)}, bf16[1,768,768]{1,2,0:T(8,128)(2,1)}) async-done(((bf16[768,768]{0,1:T(8,128)(2,1)}, bf16[768,768]{0,1:T(8,128)(2,1)}, bf16[1,768,768]{1,2,0:T(8,128)(2,1)}, bf16[1,768,768]{1,2,0:T(8,128)(2,1)}), (bf16[768,768]{0,1:T(8,128)(2,1)}, bf16[768,768]{0,1:T(8,128)(2,1)}, ...) | async-done | bytes 4718608 | tf_op jit(solution)/shard_map/psum | solution.py:459
  (4129 shorter events, 2970.9 us)
Async XLA Ops:
  7.2 73.5 %all-gather.28.cloned.1.call-start = ((), (), s32[]{:S(2)}) async-start(), calls=%async_computation.22 | async-start | bytes 12288000 | tf_op jit(solution)/shard_map/all_gather | solution.py:532
  11.4 161.6 %reduce-scatter.23.cloned.1.call-start = ((), (), s32[]{:S(2)}) async-start(), calls=%async_computation.28 | async-start | bytes 1769472 | tf_op jit(solution)/shard_map/reduce_scatter | solution.py:210
  108.0 103.6 %all-gather.30.cloned.1.call-start = ((), (), s32[]{:S(2)}) async-start(), calls=%async_computation.24 | async-start | bytes 5898240 | tf_op jit(solution)/shard_map/all_gather | solution.py:533
  109.2 171.5 %reduce-scatter.21.cloned.1.call-start = ((), (), s32[]{:S(2)}) async-start(), calls=%async_computation.23 | async-start | bytes 1769472 | tf_op jit(solution)/shard_map/reduce_scatter | solution.py:210
  120.5 1227.8 %all-gather.32.cloned.1.call-start = ((), (), s32[]{:S(2)}) async-start(), calls=%async_computation.25 | async-start | bytes 2949120 | tf_op jit(solution)/shard_map/all_gather | solution.py:534
  121.5 1258.1 %all-gather.34.cloned.1.call-start = ((), (), s32[]{:S(2)}) async-start(), calls=%async_computation.26 | async-start | bytes 5898240 | tf_op jit(solution)/shard_map/all_gather | solution.py:535
  124.6 1266.3 %all-gather.36.cloned.1.call-start = ((), (), s32[]{:S(2)}) async-start(), calls=%async_computation.27 | async-start | bytes 5898240 | tf_op jit(solution)/shard_map/all_gather | solution.py:536
  215.0 74.5 %collective-permute-start.1 = (f32[3,1536]{1,0:T(4,128)S(1)}, f32[3,1536]{1,0:T(4,128)S(1)}, u32[]{:S(2)}, u32[]{:S(2)}) collective-permute-start(f32[3,1536]{1,0:T(4,128)S(1)} %slice.2872), channel_id=1, source_target_pairs={{0,4},{4,8},{8,12},{12,16},{16,20},{20,24},{24,28},{1,5},{5,9},{9,... | collective-permute-start | bytes 55304 | tf_op jit(solution)/shard_map/ppermute | solution.py:49
  1353.6 22.5 all-to-all-start.2
  1376.1 19.7 all-to-all-start
  1395.8 20.3 all-to-all-start.3
  1422.1 286.2 %reduce-scatter.27.cloned.1.call-start = ((), (), s32[]{:S(2)}) async-start(), calls=%async_computation.31 | async-start | bytes 884736 | tf_op jit(solution)/shard_map/reduce_scatter | solution.py:374
  1647.6 126.4 %reduce-scatter.25.cloned.1.call-start = ((), (), s32[]{:S(2)}) async-start(), calls=%async_computation.29 | async-start | bytes 884736 | tf_op jit(solution)/shard_map/reduce_scatter | solution.py:374
  1811.2 17.8 all-to-all-start.7
  1835.2 1258.5 %reduce-scatter.39.cloned.1.call-start = ((), (), s32[]{:S(2)}) async-start(), calls=%async_computation.38 | async-start | bytes 368640 | tf_op jit(solution)/shard_map/reduce_scatter | solution.py:174
  3020.5 73.2 %reduce-scatter.37.cloned.1.call-start = ((), (), s32[]{:S(2)}) async-start(), calls=%async_computation.37 | async-start | bytes 614400 | tf_op jit(solution)/shard_map/reduce_scatter | solution.py:173
  3023.4 90.4 %reduce-scatter.35.cloned.1.call-start = ((), (), s32[]{:S(2)}) async-start(), calls=%async_computation.36 | async-start | bytes 5898240 | tf_op jit(solution)/shard_map/reduce_scatter | solution.py:170
  3028.5 166.4 %reduce-scatter.33.cloned.1.call-start = ((), (), s32[]{:S(2)}) async-start(), calls=%async_computation.35 | async-start | bytes 11796480 | tf_op jit(solution)/shard_map/reduce_scatter | solution.py:169
  3055.6 186.2 %all-gather.38.cloned.1.call-start = ((), (), s32[]{:S(2)}) async-start(), calls=%async_computation.30 | async-start | bytes 1769472 | tf_op jit(solution)/shard_map/all_gather | solution.py:427
  3065.2 222.2 %all-gather.40.cloned.1.call-start = ((), (), s32[]{:S(2)}) async-start(), calls=%async_computation.32 | async-start | bytes 1769472 | tf_op jit(solution)/shard_map/all_gather | solution.py:427
  3065.8 275.2 %reduce-scatter.45.cloned.1.call-start = ((), (), s32[]{:S(2)}) async-start(), calls=%async_computation.41 | async-start | bytes 491520
  3067.3 274.6 %reduce-scatter.47.cloned.1.call-start = ((), (), s32[]{:S(2)}) async-start(), calls=%async_computation.42 | async-start | bytes 491520
  3074.1 282.2 %reduce-scatter.41.cloned.1.call-start = ((), (), s32[]{:S(2)}) async-start(), calls=%async_computation.39 | async-start | bytes 184320 | tf_op jit(solution)/shard_map/reduce_scatter | solution.py:176
  3075.0 362.3 %reduce-scatter.31.cloned.1.call-start = ((), (), s32[]{:S(2)}) async-start(), calls=%async_computation.34 | async-start | bytes 11796480 | tf_op jit(solution)/shard_map/reduce_scatter | solution.py:172
  3084.4 433.9 %reduce-scatter.29.cloned.1.call-start = ((), (), s32[]{:S(2)}) async-start(), calls=%async_computation.33 | async-start | bytes 11796480 | tf_op jit(solution)/shard_map/reduce_scatter | solution.py:171
  3093.0 574.7 %all-reduce.49.cloned.1.call-start = ((), (), s32[]{:S(2)}) async-start(), calls=%async_computation.43 | async-start | bytes 7471104 | tf_op jit(solution)/shard_map/psum | solution.py:163
  3195.0 619.0 %reduce-scatter.43.cloned.1.call-start = ((), (), s32[]{:S(2)}) async-start(), calls=%async_computation.40 | async-start | bytes 24576000
  3335.7 646.3 %all-reduce.59.cloned.1.call-start = ((), (), s32[]{:S(2)}) async-start(), calls=%async_computation.48 | async-start | bytes 9437184 | tf_op jit(solution)/shard_map/psum | solution.py:459
  3886.4 262.5 %all-reduce.57.cloned.1.call-start = ((), (), s32[]{:S(2)}) async-start(), calls=%async_computation.47 | async-start | bytes 9437184 | tf_op jit(solution)/shard_map/psum | solution.py:459
  4054.0 232.2 %all-reduce.55.cloned.1.call-start = ((), (), s32[]{:S(2)}) async-start(), calls=%async_computation.46 | async-start | bytes 9437184 | tf_op jit(solution)/shard_map/psum | solution.py:459
  4191.3 230.9 %all-reduce.53.cloned.1.call-start = ((), (), s32[]{:S(2)}) async-start(), calls=%async_computation.45 | async-start | bytes 9437184 | tf_op jit(solution)/shard_map/psum | solution.py:459
  4327.4 231.3 %all-reduce.51.cloned.1.call-start = ((), (), s32[]{:S(2)}) async-start(), calls=%async_computation.44 | async-start | bytes 9437184 | tf_op jit(solution)/shard_map/psum | solution.py:459
  (346 other events, 12712.0 us)
Sparse Core Ops, SparseCore 0:
  11.5 69.1 all-gather.27
  108.1 64.8 reduce-scatter.22
  175.2 36.3 all-gather.29
  215.9 64.8 reduce-scatter.20
  282.7 22.9 all-gather.31
  307.7 37.4 all-gather.33
  347.3 37.4 all-gather.35
  1647.7 60.5 reduce-scatter.26
  1712.5 61.4 reduce-scatter.24
  3020.6 17.4 reduce-scatter.38
  3041.4 21.4 reduce-scatter.36
  3066.0 47.7 reduce-scatter.34
  3116.4 78.4 reduce-scatter.32
  3197.6 44.1 all-gather.37
  3244.4 42.9 all-gather.39
  3290.3 19.6 reduce-scatter.44
  3312.9 20.8 reduce-scatter.46
  3336.7 19.6 reduce-scatter.40
  3358.9 78.4 reduce-scatter.30
  3439.8 78.4 reduce-scatter.28
  3522.2 145.4 all-reduce.48
  3670.3 143.5 reduce-scatter.42
  3886.5 95.4 all-reduce.58
  4054.1 94.7 all-reduce.56
  4191.4 94.7 all-reduce.54
  4327.5 94.7 all-reduce.52
  4463.9 94.7 all-reduce.50
where the time goes:
time: 4680 us; the launch traced here: 4610 us
  waiting for transfers between devices  1310 us (28%)
  other arithmetic  1080 us (23%)
  local copies, waits for them, and re-layouts  826 us (18%)
  matrix products  809 us (17%)
  blocking collectives  479 us (10%)
  starting transfers between devices  59.8 us (1%)
    psum x5, waiting for transfers between devices, orthogonalize(): lax.psum(parts[0], 'mat').astype(jnp.float32)  404 us
    while x448, other arithmetic  351 us
    dot_general x512, matrix products, advance(): return (state, jnp.dot(read_item, state, precision=HIGH))  339 us
    reduce_sum x32, other arithmetic, advance(): rate * step_item[None, :]  226 us
    all_gather x6, blocking collectives, carried_in(): gathered = jax.tree.map(lambda a: lax.all_gather(a, axis), part)  207 us
    dynamic_update_slice x288, local copies, waits for them, and re-layouts, mixer_core(): lax.scan(advance, jnp.zeros((states, inner), jnp.float32), (activated, st...  204 us
    psum x1, waiting for transfers between devices, sum_copies(): return lax.psum((g_in, g_out, g_x, g_step, g_route, g_chan, g_gain), 'seq')  147 us
    slice x160, local copies, waits for them, and re-layouts, mixer_core(): lax.scan(advance, jnp.zeros((states, inner), jnp.float32), (activated, st...  141 us

commit v1 on v0

v1 whole, which is shorter than its diff:
```python
import functools
import math

import jax
import jax.numpy as jnp
from jax import lax
from jax.experimental import pallas as pl
from jax.experimental.pallas import tpu as pltpu
from jax.sharding import PartitionSpec as P

D = 768
DI = 1536
FF = 3072
VOCAB_REAL = 50257
CONV = 4
ORTHO_STEPS = 5
STEP_COUNT = 10
STATES = 16
RANK = 48

CLIP_NORM = 0.004
COEF_A = 3.4445
COEF_B = -4.775
COEF_C = 2.0315
MOMENTUM = 0.95
LR_MUON = 0.2
DECAY_MUON = 0.01
BETA_ONE = 0.9
BETA_TWO = 0.95
ADAM_EPS = 1e-08
F32 = jnp.float32
BF16 = jnp.bfloat16
LANES = 512
UNROLL = 8
TILE = 256
CUT = 256
VOCAB_TILE = 640
UP_PLACE, IN_PLACE, DOWN_PLACE, OUT_PLACE = 0, 1, 2, 3
TOTAL_ROWS = 8
MESH = pl.DeviceIdType.MESH


def dot(left, right, left_dim, right_dim, **kw):
    return lax.dot_general(
        left, right, (((left_dim,), (right_dim,)), ((), ())), preferred_element_type=F32, **kw
    )


def spread(values, width):
    return jnp.concatenate([values] * (width // 128), axis=1)


def end_kernel(keep, dt, act, inject, rate, out):
    micro = pl.program_id(0)
    tokens, width = dt.shape[1], dt.shape[2]
    rates = rate[...]

    def block(step, state):
        for inner in range(UNROLL):
            t = step * UNROLL + inner
            d = dt[0, pl.ds(t, 1), :]
            w = d * act[0, pl.ds(t, 1), :]
            state = jnp.exp(rates * d) * keep[micro, t] * state + spread(inject[0, t], width) * w
        return state

    state = lax.fori_loop(0, tokens // UNROLL, block, jnp.zeros((STATES, width), F32))
    out[...] = state.astype(BF16)


def forward_kernel(
    place, keep, dt, act, inject, readout, rate, ends, totals, y_out, h_out, start_out
):
    micro = pl.program_id(0)
    micros = pl.num_programs(0)
    tokens, width = dt.shape[1], dt.shape[2]
    rates = rate[...]
    me = place[0]

    def fold(source, state):
        total = totals[source, pl.ds(micro, 1), :]
        alive = totals[source, pl.ds(micros + micro, 1), :]
        return jnp.exp(rates * total) * alive * state + ends[source].astype(F32)

    state = lax.fori_loop(0, me, fold, jnp.zeros((STATES, width), F32))
    start_out[0] = state

    def block(step, state):
        for inner in range(UNROLL):
            t = step * UNROLL + inner
            d = dt[0, pl.ds(t, 1), :]
            w = d * act[0, pl.ds(t, 1), :]
            state = jnp.exp(rates * d) * keep[micro, t] * state + spread(inject[0, t], width) * w
            h_out[0, t] = state
            y_out[0, pl.ds(t, 1), :] = jnp.sum(
                spread(readout[0, t], width) * state, axis=0, keepdims=True
            )
        return state

    lax.fori_loop(0, tokens // UNROLL, block, state)


def start_kernel(keep, dt, dy, readout, rate, out):
    micro = pl.program_id(0)
    tokens, width = dt.shape[1], dt.shape[2]
    rates = rate[...]

    def block(step, state):
        for inner in range(UNROLL):
            t = tokens - 1 - (step * UNROLL + inner)
            d = dt[0, pl.ds(t, 1), :]
            state = state + spread(readout[0, t], width) * dy[0, pl.ds(t, 1), :]
            state = jnp.exp(rates * d) * keep[micro, t] * state
        return state

    state = lax.fori_loop(0, tokens // UNROLL, block, jnp.zeros((STATES, width), F32))
    out[...] = state.astype(BF16)


def backward_kernel(
    place,
    keep,
    dt,
    act,
    dy,
    inject,
    readout,
    rate,
    totals,
    starts,
    start,
    hs,
    ddt_out,
    da_out,
    db_out,
    dc_out,
    drate_out,
):
    micro = pl.program_id(0)
    micros = pl.num_programs(0)
    group = pl.program_id(1)
    tokens, width = dt.shape[1], dt.shape[2]
    rates = rate[...]
    me = place[0]
    count = totals.shape[0]

    def fold(lap, state):
        source = count - 1 - lap
        total = totals[source, pl.ds(micro, 1), :]
        alive = totals[source, pl.ds(micros + micro, 1), :]
        return jnp.exp(rates * total) * alive * state + starts[source].astype(F32)

    grad = lax.fori_loop(0, count - 1 - me, fold, jnp.zeros((STATES, width), F32))

    @pl.when(group == 0)
    def _():
        db_out[...] = jnp.zeros_like(db_out)
        dc_out[...] = jnp.zeros_like(dc_out)

    def gather_lanes(values):
        total = values[:, 0:128]
        for tile in range(1, width // 128):
            total = total + values[:, tile * 128 : (tile + 1) * 128]
        return total

    def one(t, before, carry):
        grad, drate, state = carry
        d = dt[0, pl.ds(t, 1), :]
        x = act[0, pl.ds(t, 1), :]
        g_y = dy[0, pl.ds(t, 1), :]
        w = d * x
        grad = grad + spread(readout[0, t], width) * g_y
        db_out[0, t] += gather_lanes(grad * w)
        dc_out[0, t] += gather_lanes(state * g_y)
        dw = jnp.sum(grad * spread(inject[0, t], width), axis=0, keepdims=True)
        grad = jnp.exp(rates * d) * keep[micro, t] * grad
        effect = grad * before
        drate = drate + effect * d
        ddt_out[0, pl.ds(t, 1), :] = (
            jnp.sum(effect * rates, axis=0, keepdims=True) + dw * x
        )
        da_out[0, pl.ds(t, 1), :] = dw * d
        return grad, drate, before

    def block(step, carry):
        for inner in range(UNROLL):
            t = tokens - 1 - (step * UNROLL + inner)
            carry = one(t, hs[0, t - 1], carry)
        return carry

    carry = (grad, jnp.zeros((STATES, width), F32), hs[0, tokens - 1])
    carry = lax.fori_loop(0, tokens // UNROLL - 1, block, carry)
    for t in range(UNROLL - 1, -1, -1):
        carry = one(t, hs[0, t - 1] if t else start[0], carry)
    drate_out[0] = carry[1]


def specs(tokens, seq_count):
    rows = pl.BlockSpec((1, tokens, LANES), lambda m, g: (m, 0, g))
    wide = pl.BlockSpec((1, tokens, STATES, 128), lambda m, g: (m, 0, 0, 0))
    rate = pl.BlockSpec((STATES, LANES), lambda m, g: (0, g))
    state = pl.BlockSpec((1, STATES, LANES), lambda m, g: (m, 0, g))
    edge = pl.BlockSpec((STATES, LANES), lambda m, g: (m, g))
    edges = pl.BlockSpec((seq_count, STATES, LANES), lambda m, g: (0, m, g))
    totals = pl.BlockSpec((seq_count, TOTAL_ROWS, LANES), lambda m, g: (0, 0, g))
    every = pl.BlockSpec((1, tokens, STATES, LANES), lambda m, g: (m, 0, 0, g))
    scalars = pl.BlockSpec(memory_space=pltpu.SMEM)
    return rows, wide, rate, state, edge, edges, totals, every, scalars


def kernel_params():
    return pltpu.CompilerParams(vmem_limit_bytes=48 * 1024 * 1024)


def scan_end(keep, dt, act, inject, rate):
    micros, tokens, inner = dt.shape
    rows, wide, rated, _, edge, _, _, _, scalars = specs(tokens, 1)
    return pl.pallas_call(
        end_kernel,
        grid=(micros, inner // LANES),
        in_specs=[scalars, rows, rows, wide, rated],
        out_specs=edge,
        out_shape=jax.ShapeDtypeStruct((micros * STATES, inner), BF16),
        compiler_params=kernel_params(),
        name="scan_end",
    )(keep, dt, act, inject, rate)


def scan_forward(place, keep, dt, act, inject, readout, rate, ends_all, totals_all):
    micros, tokens, inner = dt.shape
    rows, wide, rated, state, _, edges, totals, every, scalars = specs(tokens, ends_all.shape[0])
    return pl.pallas_call(
        forward_kernel,
        grid=(micros, inner // LANES),
        in_specs=[scalars, scalars, rows, rows, wide, wide, rated, edges, totals],
        out_specs=[rows, every, state],
        out_shape=[
            jax.ShapeDtypeStruct((micros, tokens, inner), F32),
            jax.ShapeDtypeStruct((micros, tokens, STATES, inner), F32),
            jax.ShapeDtypeStruct((micros, STATES, inner), F32),
        ],
        compiler_params=kernel_params(),
        name="scan_forward",
    )(place, keep, dt, act, inject, readout, rate, ends_all, totals_all)


def scan_start(keep, dt, dy, readout, rate, ahead):
    micros, tokens, inner = dt.shape
    rows, wide, rated, _, edge, _, _, _, scalars = specs(tokens, 1)
    unread = pl.BlockSpec(memory_space=pl.ANY)

    def body(keep, dt, dy, readout, rate, *rest):
        start_kernel(keep, dt, dy, readout, rate, rest[-1])

    return pl.pallas_call(
        body,
        grid=(micros, inner // LANES),
        in_specs=[scalars, rows, rows, wide, rated] + [unread] * len(ahead),
        out_specs=edge,
        out_shape=jax.ShapeDtypeStruct((micros * STATES, inner), BF16),
        compiler_params=kernel_params(),
        name="scan_start",
    )(keep, dt, dy, readout, rate, *ahead)


def scan_backward(
    place, keep, dt, act, dy, inject, readout, rate, totals_all, starts_all, start, hs, ahead
):
    micros, tokens, inner = dt.shape
    rows, wide, rated, state, _, edges, totals, every, scalars = specs(tokens, totals_all.shape[0])
    unread = pl.BlockSpec(memory_space=pl.ANY)

    def body(*refs):
        backward_kernel(*refs[:12], *refs[12 + len(ahead) :])

    return pl.pallas_call(
        body,
        grid=(micros, inner // LANES),
        in_specs=[
            scalars, scalars, rows, rows, rows, wide, wide, rated, totals, edges, state, every,
        ]
        + [unread] * len(ahead),
        out_specs=[rows, rows, wide, wide, state],
        out_shape=[
            jax.ShapeDtypeStruct((micros, tokens, inner), F32),
            jax.ShapeDtypeStruct((micros, tokens, inner), F32),
            jax.ShapeDtypeStruct((micros, tokens, STATES, 128), F32),
            jax.ShapeDtypeStruct((micros, tokens, STATES, 128), F32),
            jax.ShapeDtypeStruct((micros, STATES, inner), F32),
        ],
        compiler_params=kernel_params(),
        name="scan_backward",
    )(place, keep, dt, act, dy, inject, readout, rate, totals_all, starts_all, start, hs, *ahead)


def exchange_kernel(groups, gathers, ahead, through, *refs):
    arrays = len(groups)
    inputs, outputs = refs[:arrays], refs[arrays + ahead : 2 * arrays + ahead]
    sends, receives, own_sem = refs[2 * arrays + ahead + through :]

    def place_of(axes):
        if len(axes) == 1:
            return lax.axis_size(axes[0]), lax.axis_index(axes[0]), lambda peer: {axes[0]: peer}
        width = lax.axis_size(axes[1])
        return (
            lax.axis_size(axes[0]) * width,
            lax.axis_index(axes[0]) * width + lax.axis_index(axes[1]),
            lambda peer: {axes[0]: peer // width, axes[1]: peer % width},
        )

    def source(index, peer):
        return inputs[index] if gathers[index] else inputs[index].at[peer]

    def copy(index, device, peer, block):
        return pltpu.make_async_remote_copy(
            src_ref=source(index, peer),
            dst_ref=outputs[index].at[block],
            send_sem=sends.at[index, peer],
            recv_sem=receives.at[index, block],
            device_id=device(peer),
            device_id_type=MESH,
        )

    barrier = pltpu.get_barrier_semaphore()
    total = 0
    for axes in sorted(set(groups)):
        peers, me, device = place_of(axes)

        def greet(lap, _):
            pl.semaphore_signal(
                barrier, inc=1, device_id=device((me + lap) % peers), device_id_type=MESH
            )
            return _

        lax.fori_loop(1, peers, greet, 0)
        total += peers - 1
    own = []
    for index, axes in enumerate(groups):
        me = place_of(axes)[1]
        own.append(
            pltpu.make_async_copy(source(index, me), outputs[index].at[me], own_sem.at[index])
        )
        own[-1].start()
    pl.semaphore_wait(barrier, total)
    for index, axes in enumerate(groups):
        peers, me, device = place_of(axes)

        def begin(lap, _):
            copy(index, device, (me + lap) % peers, me).start()
            return _

        lax.fori_loop(1, peers, begin, 0)
    for index, axes in enumerate(groups):
        peers, me, device = place_of(axes)
        own[index].wait()

        def end(lap, _):
            before = (me + peers - lap) % peers
            copy(index, device, before, before).wait_recv()
            copy(index, device, (me + lap) % peers, me).wait_send()
            return _

        lax.fori_loop(1, peers, end, 0)


def exchange(
    values, gathers, identity, axes=("seq",), space=pltpu.VMEM, ahead=(), riders=(), through=()
):
    groups = [axes] * len(values) + [("mat",)] * len(riders)
    gathers = list(gathers) + [False] * len(riders)
    peers = [math.prod(lax.axis_size(axis) for axis in group) for group in groups]
    place = pl.BlockSpec(memory_space=space)
    unread = pl.BlockSpec(memory_space=pl.ANY)
    places = [place] * len(values) + [unread] * len(riders)
    values = list(values) + list(riders)
    shapes = [
        jax.ShapeDtypeStruct(((count,) if gather else ()) + value.shape, value.dtype)
        for value, gather, count in zip(values, gathers, peers)
    ]
    arrays = len(values)
    ahead = list(ahead) + list(through)
    first = arrays + len(ahead) - len(through)
    shapes += [jax.ShapeDtypeStruct(value.shape, value.dtype) for value in through]
    return pl.pallas_call(
        functools.partial(exchange_kernel, tuple(groups), tuple(gathers), len(ahead), len(through)),
        out_shape=shapes,
        in_specs=places + [unread] * len(ahead),
        out_specs=places + [unread] * len(through),
        input_output_aliases={first + index: arrays + index for index in range(len(through))},
        scratch_shapes=[
            pltpu.SemaphoreType.DMA((arrays, max(peers))),
            pltpu.SemaphoreType.DMA((arrays, max(peers))),
            pltpu.SemaphoreType.DMA((arrays,)),
        ],
        compiler_params=pltpu.CompilerParams(collective_id=identity, has_side_effects=True),
        name="exchange",
    )(*values, *ahead)


def hold(values, ahead):
    unread = pl.BlockSpec(memory_space=pl.ANY)
    return pl.pallas_call(
        lambda *refs: None,
        out_shape=[jax.ShapeDtypeStruct(value.shape, value.dtype) for value in values],
        in_specs=[unread] * (len(values) + 1),
        out_specs=[unread] * len(values),
        input_output_aliases={index: index for index in range(len(values))},
        name="hold",
    )(*values, ahead)


class Line:
    SEMAPHORES = 6

    def __init__(self, inputs, outputs, semaphores):
        self.inputs, self.outputs = inputs, outputs
        self.sends, self.receives = semaphores[0::2], semaphores[1::2]
        self.outers = lax.axis_size("seq") // 2
        me = lax.axis_index("seq")
        self.outer, self.inner = me // 2, me % 2
        self.later = self.outer + 1 < self.outers
        self.earlier = self.outer > 0

    def block(self, outer):
        return outer * 2 + self.inner

    def across(self, outer):
        return outer * 2 + 1 - self.inner

    def target(self, way):
        step = (2, -2, 1 - 2 * self.inner)[way]
        return {"seq": self.outer * 2 + self.inner + step}

    def pieces(self):
        for index, source in enumerate(self.inputs):
            for piece in range(source.shape[0]):
                yield index, piece

    def copy(self, way, index, outer, piece, place, first=False):
        source = self.outputs[index].at[place, piece]
        return pltpu.make_async_remote_copy(
            src_ref=self.inputs[index].at[piece] if first else source,
            dst_ref=self.outputs[index].at[place, piece],
            send_sem=self.sends[way].at[index, outer, piece],
            recv_sem=self.receives[way].at[index, outer, piece],
            device_id=self.target(way),
            device_id_type=MESH,
        )

    def ways(self):
        return ((0, self.later), (1, self.earlier))

    def greet(self, barrier):
        for way, exists in self.ways():

            @pl.when(exists)
            def _():
                pl.semaphore_signal(
                    barrier, inc=1, device_id=self.target(way), device_id_type=MESH
                )

        pl.semaphore_signal(barrier, inc=1, device_id=self.target(2), device_id_type=MESH)
        return 1 + self.later.astype(jnp.int32) + self.earlier.astype(jnp.int32)

    def begin(self):
        mine = self.block(self.outer)
        for index, piece in self.pieces():
            for way, exists in self.ways():

                @pl.when(exists)
                def _():
                    self.copy(way, index, self.outer, piece, mine, True).start()

            self.copy(2, index, self.outer, piece, mine, True).start()

    def forward(self, lap):
        for index, piece in self.pieces():
            for way, exists in self.ways():
                outer = self.outer + (-lap, lap)[way]
                place = self.block(outer)

                @pl.when(jnp.logical_and(outer >= 0, outer < self.outers))
                def _():
                    self.copy(way, index, outer, piece, place).wait_recv()

                    @pl.when(exists)
                    def _():
                        self.copy(way, index, outer, piece, place).start()

                    self.copy(2, index, outer, piece, place).start()

    def take(self, outer):
        for index, piece in self.pieces():
            self.copy(2, index, outer, piece, self.across(outer)).wait_recv()

    def each(self, lap, use):
        for way in range(2):
            outer = self.outer + (-lap, lap)[way]

            @pl.when(jnp.logical_and(outer >= 0, outer < self.outers))
            def _():
                use(self.block(outer))
                self.take(outer)
                use(self.across(outer))

    def end(self):
        def one(outer, _):
            for index, piece in self.pieces():
                place = self.block(outer)

                @pl.when(jnp.logical_and(self.later, outer <= self.outer))
                def _():
                    self.copy(0, index, outer, piece, place).wait_send()

                @pl.when(jnp.logical_and(self.earlier, outer >= self.outer))
                def _():
                    self.copy(1, index, outer, piece, place).wait_send()

                self.copy(2, index, outer, piece, place).wait_send()
            return 0

        lax.fori_loop(0, self.outers, one, 0)


def line_semaphores(values):
    shape = (len(values), lax.axis_size("seq") // 2, max(value.shape[0] for value in values))
    return [pltpu.SemaphoreType.DMA(shape)] * Line.SEMAPHORES


def gather_kernel(arrays, ahead, relays, *refs):
    inputs = refs[:arrays]
    outputs = refs[arrays + ahead : 2 * arrays + ahead]
    wholes = refs[2 * arrays + ahead : 2 * arrays + ahead + len(relays)]
    rest = refs[2 * arrays + ahead + len(relays) :]
    line = Line(inputs, outputs, rest[: Line.SEMAPHORES])
    own_sem, relay_sends, relay_receives, relay_own = rest[Line.SEMAPHORES :]
    mats, here = lax.axis_size("mat"), lax.axis_index("mat")
    me = lax.axis_index("seq")

    def relayed(relay, block, origin):
        index, place = relays[relay]
        return pltpu.make_async_remote_copy(
            src_ref=outputs[index].at[block],
            dst_ref=wholes[relay].at[origin, block],
            send_sem=relay_sends.at[relay, block],
            recv_sem=relay_receives.at[relay, origin, block],
            device_id={"mat": place},
            device_id_type=MESH,
        )

    def kept(relay, block):
        index, place = relays[relay]
        return pltpu.make_async_copy(
            outputs[index].at[block], wholes[relay].at[place, block], relay_own.at[relay, block]
        )

    def relay_all(block):
        for relay, (_, place) in enumerate(relays):

            @pl.when(here != place)
            def _():
                relayed(relay, block, here).start()

            @pl.when(here == place)
            def _():
                kept(relay, block).start()

    def relay_end(block, _):
        for relay, (_, place) in enumerate(relays):

            @pl.when(here != place)
            def _():
                relayed(relay, block, here).wait_send()

            @pl.when(here == place)
            def _():
                kept(relay, block).wait()
                for origin in range(mats):
                    if origin != place:
                        relayed(relay, block, origin).wait_recv()

        return 0

    barrier = pltpu.get_barrier_semaphore()
    greeted = line.greet(barrier)
    if relays:

        def greet_mat(lap, _):
            pl.semaphore_signal(
                barrier, inc=1, device_id={"mat": (here + lap) % mats}, device_id_type=MESH
            )
            return 0

        lax.fori_loop(1, mats, greet_mat, 0)
        greeted = greeted + mats - 1
    own = [
        pltpu.make_async_copy(inputs[index], outputs[index].at[me], own_sem.at[index])
        for index in range(arrays)
    ]
    for copy in own:
        copy.start()
    pl.semaphore_wait(barrier, greeted)
    line.begin()
    for copy in own:
        copy.wait()
    relay_all(me)

    def step(lap, _):
        line.forward(lap)

        @pl.when(lap > 1)
        def _():
            line.each(lap - 1, relay_all)

        return 0

    lax.fori_loop(1, line.outers, step, 0)
    line.take(line.outer)
    relay_all(line.across(line.outer))
    line.each(line.outers - 1, relay_all)
    line.end()
    if relays:
        lax.fori_loop(0, lax.axis_size("seq"), relay_end, 0)


def gather_seq(values, identity, space=pltpu.VMEM, ahead=(), relays=()):
    peers = lax.axis_size("seq")
    mats = lax.axis_size("mat")
    plain = [value.shape for value in values]
    values = [
        value.reshape((2, -1) + value.shape[1:]) if value.shape[0] % 32 == 0 else value[None]
        for value in values
    ]
    shapes = [jax.ShapeDtypeStruct((peers,) + value.shape, value.dtype) for value in values]
    shapes += [
        jax.ShapeDtypeStruct((mats, peers) + values[index].shape, values[index].dtype)
        for index, _ in relays
    ]
    place = pl.BlockSpec(memory_space=space)
    unread = pl.BlockSpec(memory_space=pl.ANY)
    arrays = len(values)
    results = pl.pallas_call(
        functools.partial(gather_kernel, arrays, len(ahead), tuple(relays)),
        out_shape=shapes,
        in_specs=[place] * arrays + [unread] * len(ahead),
        out_specs=[place] * arrays + [unread] * len(relays),
        scratch_shapes=line_semaphores(values)
        + [
            pltpu.SemaphoreType.DMA((arrays,)),
            pltpu.SemaphoreType.DMA((max(1, len(relays)), peers)),
            pltpu.SemaphoreType.DMA((max(1, len(relays)), mats, peers)),
            pltpu.SemaphoreType.DMA((max(1, len(relays)), peers)),
        ],
        compiler_params=pltpu.CompilerParams(collective_id=identity, has_side_effects=True),
        name="gather_seq",
    )(*values, *ahead)
    gathered = [result.reshape((peers,) + shape) for result, shape in zip(results, plain)]
    relayed = [
        result.reshape((mats, peers) + plain[index])
        for result, (index, _) in zip(results[arrays:], relays)
    ]
    return gathered + relayed


def lookup_kernel(
    ids, table, small, out, smalls, found, give, got, keep, taken, passes, arrivals, sends,
    receives, small_sends, small_receives, small_own,
):
    outers, mats = taken.shape[0], taken.shape[1]
    me = lax.axis_index("seq")
    here = lax.axis_index("mat")
    outer, inner = me // 2, me % 2
    partner = {"seq": outer * 2 + 1 - inner}
    tokens = 256
    lanes = lax.broadcasted_iota(jnp.int32, (128, 128), 1)

    def device(to_outer, to_mat):
        return {"seq": to_outer * 2 + inner, "mat": to_mat}

    def hand(lap, place):
        return pltpu.make_async_remote_copy(
            src_ref=give.at[lap, place],
            dst_ref=got.at[lap, place],
            send_sem=passes.at[lap, place],
            recv_sem=arrivals.at[lap, place],
            device_id=partner,
            device_id_type=MESH,
        )

    def send(to_outer, to_mat, from_outer, from_mat):
        return pltpu.make_async_remote_copy(
            src_ref=keep.at[to_outer, to_mat],
            dst_ref=taken.at[from_outer, from_mat],
            send_sem=sends.at[to_outer, to_mat],
            recv_sem=receives.at[from_outer, from_mat],
            device_id=device(to_outer, to_mat),
            device_id_type=MESH,
        )

    def share(to_mat, from_mat):
        return pltpu.make_async_remote_copy(
            src_ref=small,
            dst_ref=smalls.at[from_mat],
            send_sem=small_sends.at[to_mat],
            recv_sem=small_receives.at[from_mat],
            device_id={"mat": to_mat},
            device_id_type=MESH,
        )

    own_small = pltpu.make_async_copy(small, smalls.at[here], small_own)
    own_small.start()
    barrier = pltpu.get_barrier_semaphore()

    def greet(lap, _):
        pl.semaphore_signal(
            barrier,
            inc=1,
            device_id=device((outer + lap // mats) % outers, (here + lap % mats) % mats),
            device_id_type=MESH,
        )
        return _

    pl.semaphore_signal(barrier, inc=1, device_id=partner, device_id_type=MESH)
    lax.fori_loop(1, outers * mats, greet, 0)
    pl.semaphore_wait(barrier, outers * mats)

    def share_start(lap, _):
        share((here + lap) % mats, here).start()
        return 0

    lax.fori_loop(1, mats, share_start, 0)

    def find(block):
        def rows(index, _):
            for step in range(8):
                row = index * 8 + step
                entry = ids[block * mats * tokens + row]
                found[pl.ds(row, 1), :] = table[pl.ds(entry, 1), :]
            return 0

        lax.fori_loop(0, mats * tokens // 8, rows, 0)

    def store(target):
        for place in range(mats):
            base = place * tokens
            target[place, 0:tokens, :] = found[base : base + tokens, 0:128].astype(BF16)
            low = found[base : base + 128, 128:256]
            high = pltpu.roll(found[base + 128 : base + tokens, 128:256], 64, 1)
            target[place, tokens : tokens + 128, :] = jnp.where(lanes < 64, low, high).astype(BF16)

    def outer_of(lap):
        return (outer + 1 + lap) % outers

    def hand_over(lap):
        find(outer_of(lap) * 2 + 1 - inner)
        store(give.at[lap])
        for place in range(mats):
            hand(lap, place).start()

    def compute(lap, _):
        to_outer = outer_of(lap)

        @pl.when(lap + 1 < outers)
        def _():
            hand_over(lap + 1)

        find(to_outer * 2 + inner)
        store(keep.at[to_outer])
        for place in range(mats):
            hand(lap, place).wait_recv()
            keep[to_outer, place] = keep[to_outer, place] + got[lap, place]
            own = jnp.logical_and(to_outer == outer, place == here)

            @pl.when(jnp.logical_not(own))
            def _():
                send(to_outer, place, outer, here).start()

            @pl.when(own)
            def _():
                taken[outer, here] = keep[to_outer, place]

        return 0

    hand_over(0)
    lax.fori_loop(0, outers, compute, 0)

    def finish(lap, _):
        to_outer, to_mat = (outer + lap // mats) % outers, (here + lap % mats) % mats
        send(to_outer, to_mat, to_outer, to_mat).wait_recv()
        send(to_outer, to_mat, outer, here).wait_send()
        return _

    lax.fori_loop(1, outers * mats, finish, 0)

    def end(lap, _):
        for place in range(mats):
            hand(lap, place).wait_send()
        return 0

    lax.fori_loop(0, outers, end, 0)

    def share_end(lap, _):
        before = (here + mats - lap) % mats
        share(before, before).wait_recv()
        share((here + lap) % mats, here).wait_send()
        return 0

    lax.fori_loop(1, mats, share_end, 0)
    own_small.wait()
    for place in range(mats):

        def gather(source, total):
            return total + taken[source, place].astype(F32)

        out[place] = lax.fori_loop(0, outers, gather, jnp.zeros((384, 128), F32)).astype(BF16)


def lookup(ids, table, small, identity):
    outers, mats = lax.axis_size("seq") // 2, lax.axis_size("mat")
    entries, part = table.shape
    padded = (entries // 8 + 1) * 8
    table = table.astype(BF16).astype(F32)
    table = jnp.pad(table, ((0, padded - entries), (0, 256 - part)))
    ids = jnp.where((ids >= 0) & (ids < entries), ids, entries)
    vmem = pl.BlockSpec(memory_space=pltpu.VMEM)
    blocks = pltpu.VMEM((outers, mats, 384, 128), BF16)
    return pl.pallas_call(
        lookup_kernel,
        out_shape=[
            jax.ShapeDtypeStruct((mats, 384, 128), BF16),
            jax.ShapeDtypeStruct((mats,) + small.shape, BF16),
        ],
        in_specs=[pl.BlockSpec(memory_space=pltpu.SMEM), vmem, vmem],
        out_specs=[vmem, vmem],
        scratch_shapes=[
            pltpu.VMEM((mats * 256, 256), F32),
            blocks,
            blocks,
            blocks,
            blocks,
            *[pltpu.SemaphoreType.DMA((outers, mats))] * 4,
            pltpu.SemaphoreType.DMA((mats,)),
            pltpu.SemaphoreType.DMA((mats,)),
            pltpu.SemaphoreType.DMA,
        ],
        compiler_params=pltpu.CompilerParams(
            collective_id=identity, has_side_effects=True, vmem_limit_bytes=56 * 1024 * 1024
        ),
        name="lookup",
    )(ids, table, small)


def scatter_rows_kernel(
    entries, ids, rows, others, first_rider, second_rider, out, squares, whole, buffer, *rest
):
    line = Line([rows], [buffer], rest[: Line.SEMAPHORES])
    rider_sends, rider_receives, rider_own = rest[Line.SEMAPHORES :]
    places = lax.axis_size("mat")
    here = lax.axis_index("mat")
    riders = ((first_rider, UP_PLACE), (second_rider, DOWN_PLACE))

    def ride(rider, origin):
        source, place = riders[rider]
        return pltpu.make_async_remote_copy(
            src_ref=source,
            dst_ref=whole.at[origin],
            send_sem=rider_sends.at[rider],
            recv_sem=rider_receives.at[origin],
            device_id={"mat": place},
            device_id_type=MESH,
        )

    def stay(rider):
        source, place = riders[rider]
        return pltpu.make_async_copy(source, whole.at[place], rider_own)

    mats = rows.shape[0]
    lanes = lax.broadcasted_iota(jnp.int32, (128, 128), 1)

    def add(block, source):
        parts = []
        for place in range(mats):
            tail = source[place, 256:384, :].astype(F32)
            low = jnp.where(lanes < 64, tail, 0.0)
            high = jnp.where(lanes < 64, pltpu.roll(tail, 64, 1), 0.0)
            tails = jnp.concatenate([low, high], axis=0).astype(BF16)
            parts.append(jnp.concatenate([source[place, 0:256, :], tails], axis=1))
        values = jnp.concatenate(parts, axis=0)
        names = jnp.concatenate(
            [ids[pl.ds(block * 2 * mats + half, 1), :] for half in range(2 * mats)], axis=1
        )
        group = lax.shift_right_arithmetic(names, 7)
        spot = lax.broadcasted_iota(jnp.int32, (128, names.shape[1]), 0)
        hits = jnp.where(spot == jnp.bitwise_and(names, 127), 1.0, 0.0).astype(BF16)

        def piece(index, _):
            first = pl.multiple_of(index * VOCAB_TILE, VOCAB_TILE)
            masked = []
            for step in range(VOCAB_TILE // 128):
                chosen = jnp.where(group == index * (VOCAB_TILE // 128) + step, 1.0, 0.0)
                masked.append(hits * chosen.astype(BF16))
            out[pl.ds(first, VOCAB_TILE), :] += dot(
                jnp.concatenate(masked, axis=0), values, 1, 0
            )
            return 0

        lax.fori_loop(0, out.shape[0] // VOCAB_TILE, piece, 0)

    barrier = pltpu.get_barrier_semaphore()
    greeted = line.greet(barrier)

    def greet_mat(lap, _):
        pl.semaphore_signal(
            barrier, inc=1, device_id={"mat": (here + lap) % places}, device_id_type=MESH
        )
        return _

    lax.fori_loop(1, places, greet_mat, 0)
    out[...] = jnp.zeros_like(out)
    pl.semaphore_wait(barrier, greeted + places - 1)
    line.begin()
    for rider, (_, place) in enumerate(riders):

        @pl.when(here != place)
        def _():
            ride(rider, here).start()

        @pl.when(here == place)
        def _():
            stay(rider).start()

    def use(block):
        add(block, buffer.at[block])

    add(line.block(line.outer), rows)

    def step(lap, _):
        line.forward(lap)

        @pl.when(lap == 1)
        def _():
            line.take(line.outer)
            use(line.across(line.outer))

        @pl.when(lap > 1)
        def _():
            line.each(lap - 1, use)

        return 0

    lax.fori_loop(1, line.outers, step, 0)
    line.each(line.outers - 1, use)
    line.end()
    for rider, (_, place) in enumerate(riders):

        @pl.when(here != place)
        def _():
            ride(rider, here).wait_send()

        @pl.when(here == place)
        def _():
            stay(rider).wait()
            for origin in range(places):
                if origin != place:
                    ride(rider, origin).wait_recv()

    part = others.shape[0]

    def finish(index, total):
        cut = pl.ds(pl.multiple_of(index * VOCAB_TILE, VOCAB_TILE), VOCAB_TILE)
        more = others[:, cut].astype(F32).T
        more = jnp.concatenate([more, jnp.zeros((VOCAB_TILE, 256 - part), F32)], axis=1)
        values = out[cut, :] + more
        out[cut, :] = values
        entry = lax.broadcasted_iota(jnp.int32, values.shape, 0) + index * VOCAB_TILE
        values = jnp.where(entry < entries, values, 0.0)
        return total + jnp.sum(values * values, axis=0, keepdims=True)

    total = lax.fori_loop(0, out.shape[0] // VOCAB_TILE, finish, jnp.zeros((1, 256), F32))
    squares[...] = jnp.broadcast_to(total, (8, 256))


def scatter_rows(ids, rows, others, entries, identity, riders):
    peers = lax.axis_size("seq")
    mats = lax.axis_size("mat")
    padded = -(-entries // VOCAB_TILE) * VOCAB_TILE
    unread = pl.BlockSpec(memory_space=pl.ANY)
    place = pl.BlockSpec(memory_space=pltpu.VMEM)
    return pl.pallas_call(
        functools.partial(scatter_rows_kernel, entries),
        out_shape=[
            jax.ShapeDtypeStruct((padded, 256), F32),
            jax.ShapeDtypeStruct((8, 256), F32),
            jax.ShapeDtypeStruct((mats,) + riders[0].shape, BF16),
        ],
        in_specs=[place, place, place, unread, unread],
        out_specs=[place, place, unread],
        scratch_shapes=[
            pltpu.VMEM((peers,) + rows.shape, BF16),
            *line_semaphores([rows]),
            pltpu.SemaphoreType.DMA((2,)),
            pltpu.SemaphoreType.DMA((mats,)),
            pltpu.SemaphoreType.DMA,
        ],
        compiler_params=pltpu.CompilerParams(
            collective_id=identity, has_side_effects=True, vmem_limit_bytes=48 * 1024 * 1024
        ),
        name="scatter_rows",
    )(ids, rows, jnp.pad(others, ((0, 0), (0, padded - entries))), *riders)


def swap_seq(value, identity, ahead=()):
    return exchange([value], [False], identity, ahead=ahead)[0]


def move_rows(value, steps):
    count = lax.axis_size("seq")
    leading, last = (max(0, -steps), min(count, count - steps))
    return lax.ppermute(value, "seq", [(source, source + steps) for source in range(leading, last)])


def normalize(values, gain):
    scale = lax.rsqrt(jnp.mean(values * values, axis=-1, keepdims=True) + 1e-05)
    hat = values * scale
    return hat * gain, hat, scale


def normalize_back(hat, scale, gain, grad):
    gain_grad = jnp.sum(grad * hat, axis=0)
    hat_grad = grad * gain
    return gain_grad, scale * (hat_grad - hat * jnp.mean(hat_grad * hat, axis=-1, keepdims=True))


def silu_back(values):
    sig = jax.nn.sigmoid(values)
    return sig * (1.0 + values * (1.0 - sig))


def padded_rows(flat):
    size = flat.shape[-1]
    room = -(-size // 16384) * 16384 - size
    flat = jnp.pad(flat, [(0, 0)] * (flat.ndim - 1) + [(0, room)])
    return flat.reshape(flat.shape[:-1] + (-1, 1024))


def pack_small(parts):
    return padded_rows(jnp.concatenate([part.astype(BF16).reshape(-1) for part in parts]))


def unpack_small(every, parts):
    every = every.reshape(every.shape[0], -1)
    result, offset = [], 0
    for part in parts:
        size = part.size
        result.append(every[:, offset : offset + size].reshape((-1,) + part.shape))
        offset += size
    return result


def columns(stacked):
    count, rows, width = stacked.shape
    return stacked.transpose(1, 0, 2).reshape(rows, count * width)


def step_grads(weights, moments, embedded, route, lengths, slots, weight_mask, targets, loss_all):
    table, w_in, w_out, w_up, w_down, w_x, w_step, w_route, chan_low, gains_low = weights
    channel = chan_low.astype(F32)
    gains = gains_low.astype(F32)
    me = lax.axis_index("seq")
    count = lax.axis_size("seq")
    micros, tokens = route.shape
    inner = w_in.shape[1] // 2
    vocab_part = table.shape[0]
    first_pos = me * tokens
    vocab_start = me * vocab_part
    ext_pos = first_pos - (CONV - 1) + jnp.arange(tokens + CONV - 1, dtype=jnp.int32)
    bounds = jnp.cumsum(lengths, axis=1)
    ext_doc = jnp.sum((ext_pos[None, :, None] >= bounds[:, None, :-1]).astype(jnp.int32), axis=2)
    ext_doc = jnp.where(ext_pos[None] >= 0, ext_doc, -1)
    starts = jnp.concatenate([jnp.zeros((micros, 1), jnp.int32), bounds[:, :-1]], axis=1)
    keeping = 1.0 - jnp.any(
        ext_pos[None, CONV - 1 :, None] == starts[:, None, :], axis=2
    ).astype(F32)
    own_doc = ext_doc[:, CONV - 1 :]
    same = [
        (ext_doc[:, tap : tap + tokens] == own_doc).astype(F32)[:, :, None] for tap in range(CONV)
    ]
    place = me.astype(jnp.int32).reshape(1)

    x0 = embedded.astype(F32)

    u, hat0, scale0 = normalize(x0, gains[0])
    u_low = u.astype(BF16)
    xz = dot(u_low, w_in, 1, 0).reshape(micros, tokens, 2 * inner)
    raw, z = xz[:, :, :inner], xz[:, :, inner:]
    edge = move_rows(raw[:, tokens - (CONV - 1) :], 1)
    padded = jnp.concatenate([edge, raw], axis=1)
    conv = channel[CONV] + jnp.zeros((micros, tokens, inner), F32)
    for tap in range(CONV):
        conv = conv + channel[tap] * padded[:, tap : tap + tokens] * same[tap]
    act = jax.nn.silu(conv)
    act_low = act.reshape(-1, inner).astype(BF16)
    projected = dot(act_low, w_x, 1, 0)
    rank_low = projected[:, :RANK].astype(BF16)
    pre = dot(rank_low, w_step, 1, 0).reshape(micros, tokens, inner) + channel[CONV + 1]
    dt = jax.nn.softplus(pre)
    rate = -jnp.exp(channel[CONV + 3 :])
    wide = projected.reshape(micros, tokens, -1)[:, :, :, None]
    wide_shape = (micros, tokens, STATES, 128)
    inject = jnp.broadcast_to(wide[:, :, RANK : RANK + STATES], wide_shape)
    readout = jnp.broadcast_to(wide[:, :, RANK + STATES :], wide_shape)
    totals = jnp.concatenate(
        [
            jnp.sum(dt, axis=1),
            jnp.broadcast_to(jnp.prod(keeping, axis=1)[:, None], (micros, inner)),
            jnp.zeros((TOTAL_ROWS - 2 * micros, inner), F32),
        ]
    )
    ends_all, totals_all = gather_seq(
        [scan_end(keeping, dt, act, inject, rate), totals], 1
    )
    y, hs, start = scan_forward(
        place, keeping, dt, act, inject, readout, rate, ends_all, totals_all
    )
    skip = channel[CONV + 2]
    z_silu = jax.nn.silu(z)
    core = y + skip * act
    mixed_low = (core * z_silu).reshape(-1, inner).astype(BF16)
    x1 = x0 + dot(mixed_low, w_out, 1, 0)

    experts = w_route.shape[1]
    capacity = max(2, 2 * tokens // experts)
    local_experts = w_up.shape[0]
    s, hat1, scale1 = normalize(x1, gains[1])
    s_low = s.astype(BF16)
    scores = dot(s_low, w_route, 1, 0)
    chosen = route.reshape(-1)[:, None] == jnp.arange(experts, dtype=jnp.int32)[None, :]
    gate = jax.nn.sigmoid(jnp.sum(jnp.where(chosen, scores, 0.0), axis=1))
    onehot = chosen.astype(jnp.int32).reshape(micros, tokens, experts)
    ranking = jnp.sum(jnp.cumsum(onehot, axis=1) * onehot, axis=2) - 1
    placed = route * capacity + ranking
    all_slots = experts * capacity
    sender = (
        placed[:, None, :] == jnp.arange(all_slots, dtype=jnp.int32)[None, :, None]
    ).astype(BF16)

    moved = []

    def swap_seq(value, identity, ahead=(), riders=(), through=()):
        result = exchange(
            [value], [False], identity, ahead=ahead, riders=riders, through=through
        )
        moved.extend(result[1:])
        return result[0]

    def to_experts(rows, identity, ahead=(), riders=()):
        sent = jnp.einsum(
            "mst,mtd->msd", sender, rows.reshape(micros, tokens, D), preferred_element_type=F32
        ).astype(BF16)
        sent = sent.reshape(micros, count, -1, D).transpose(1, 0, 2, 3).reshape(count, -1, D)
        arrived = swap_seq(sent, identity, ahead, riders).reshape(count, micros, local_experts, capacity, D)
        return arrived.transpose(2, 0, 1, 3, 4).reshape(local_experts, -1, D)

    def from_experts(rows, identity, ahead=(), riders=(), through=()):
        rows = rows.reshape(local_experts, count, micros, capacity, D).transpose(1, 2, 0, 3, 4)
        back = swap_seq(rows.reshape(count, -1, D), identity, ahead, riders, through)
        back = back.reshape(count, micros, -1, D)
        back = back.transpose(1, 0, 2, 3).reshape(micros, all_slots, D)
        return jnp.einsum("mst,msd->mtd", sender, back, preferred_element_type=F32).reshape(-1, D)

    taken = to_experts(s_low, 2, (), [moments[0]])
    hidden_pre = jnp.einsum("erk,ekn->ern", taken, w_up, preferred_element_type=F32)
    gelu = functools.partial(jax.nn.gelu, approximate=False)
    hidden_low = gelu(hidden_pre).astype(BF16)
    result = jnp.einsum("erk,ekn->ern", hidden_low, w_down, preferred_element_type=F32)
    combined = from_experts(result.astype(BF16), 3, (), [moments[1]])
    x2 = x1 + gate[:, None] * combined

    final, hat2, scale2 = normalize(x2, gains[2])
    own_count = slots.shape[1]
    local_rows = slots - first_pos
    select = (
        local_rows[:, :, None] == jnp.arange(tokens, dtype=jnp.int32)[None, None, :]
    ).astype(BF16)
    picked_rows = jnp.einsum(
        "mst,mtd->msd",
        select,
        final.astype(BF16).reshape(micros, tokens, D),
        preferred_element_type=F32,
    ).astype(BF16)
    rows = gather_seq([picked_rows.reshape(-1, D)], 4)[0].reshape(count * micros * own_count, D)

    def by_device(values):
        return values.reshape(micros, count, own_count).transpose(1, 0, 2).reshape(-1)

    targets = by_device(targets)
    counted = by_device(weight_mask).astype(F32)
    logits = dot(rows, table, 1, 1)
    column = vocab_start + jnp.arange(vocab_part, dtype=jnp.int32)
    valid = column < VOCAB_REAL
    masked = jnp.where(valid[None, :], logits, -1e30)
    largest = jnp.max(masked, axis=1)
    expsum = jnp.sum(jnp.exp(masked - largest[:, None]), axis=1)
    hitting = column[None, :] == targets[:, None]
    target_logit = jnp.sum(jnp.where(hitting, logits, 0.0), axis=1)
    stats = exchange(
        [jnp.stack([largest, expsum, target_logit] + [jnp.zeros_like(largest)] * 5)], [True], 5
    )[0]
    top = jnp.max(stats[:, 0], axis=0)
    lse = top + jnp.log(jnp.sum(stats[:, 1] * jnp.exp(stats[:, 0] - top[None]), axis=0))
    unweighted = lse - jnp.sum(stats[:, 2], axis=0)

    def own(values):
        return lax.dynamic_index_in_dim(
            values.reshape(count, micros, own_count), me, 0, keepdims=False
        )

    rows_here = own(unweighted)
    counted_here = own(counted)
    loss_here = jnp.sum(rows_here * counted_here)
    count_here = jnp.sum(counted_here)
    probability = jnp.where(valid[None, :], jnp.exp(masked - lse[:, None]), 0.0)
    logit_grad = (
        (counted / loss_all)[:, None] * (probability - hitting.astype(F32))
    ).astype(BF16)
    rows_grad = swap_seq(
        dot(logit_grad, table, 1, 0).astype(BF16).reshape(count, -1, D), 6, (), [moments[2]]
    )
    rows_grad = jnp.sum(rows_grad.astype(F32), axis=0).reshape(micros, own_count, D)
    table_grad = dot(rows, logit_grad, 0, 0).astype(BF16)
    final_grad = jnp.einsum(
        "mst,msd->mtd",
        select.astype(F32),
        rows_grad,
        precision=lax.Precision.HIGHEST,
        preferred_element_type=F32,
    ).reshape(-1, D)
    gain_two, x2_grad = normalize_back(hat2, scale2, gains[2], final_grad)

    gate_grad = jnp.sum(x2_grad * combined, axis=1)
    out_grad = to_experts((gate[:, None] * x2_grad).astype(BF16), 7, [table_grad])
    hidden_grad = jnp.einsum("ern,ekn->erk", out_grad, w_down, preferred_element_type=F32)
    down_grad = jnp.einsum("erk,ern->ekn", hidden_low, out_grad, preferred_element_type=F32)
    _, gelu_back = jax.vjp(gelu, hidden_pre)
    pre_grad = gelu_back(hidden_grad)[0].astype(BF16)
    up_grad = jnp.einsum("erk,ern->ekn", taken, pre_grad, preferred_element_type=F32)
    taken_grad = jnp.einsum("ern,ekn->erk", pre_grad, w_up, preferred_element_type=F32)
    s_table = scatter_mat(table_grad, 0)
    up_grad, down_grad = hold([up_grad.astype(BF16), down_grad.astype(BF16)], s_table)
    s_grad = from_experts(taken_grad.astype(BF16), 8, [up_grad, down_grad])
    s_up = scatter_mat(up_grad, 2)
    s_down = scatter_mat(down_grad, 1)
    score_grad = jnp.where(chosen, (gate_grad * gate * (1.0 - gate))[:, None], 0.0).astype(BF16)
    route_grad = dot(s_low, score_grad, 0, 0)
    s_grad = s_grad + dot(score_grad, w_route, 1, 1)
    gain_one, more = normalize_back(hat1, scale1, gains[1], s_grad)
    x1_grad = x2_grad + more

    x1_grad_low = x1_grad.astype(BF16)
    mixed_grad = dot(x1_grad_low, w_out, 1, 1).reshape(micros, tokens, inner)
    out_weight_grad = dot(mixed_low, x1_grad_low, 0, 0)
    y_grad = mixed_grad * z_silu
    z_grad = mixed_grad * core * silu_back(z)
    out_weight_grad = out_weight_grad.astype(BF16)
    s_out = scatter_mat(out_weight_grad, 0)
    starts_all = gather_seq(
        [scan_start(keeping, dt, y_grad, readout, rate, [out_weight_grad])], 9
    )[0]
    dt_grad, act_grad, inject_grad, readout_grad, rate_grad = scan_backward(
        place, keeping, dt, act, y_grad, inject, readout, rate, totals_all, starts_all, start, hs,
        [],
    )
    skip_grad = jnp.sum(y_grad * act, axis=(0, 1))
    act_grad = act_grad + y_grad * skip
    pre_dt = dt_grad * jax.nn.sigmoid(pre)
    pre_dt_low = pre_dt.reshape(-1, inner).astype(BF16)
    step_weight_grad = dot(rank_low, pre_dt_low, 0, 0)
    projected_grad = jnp.concatenate(
        [
            dot(pre_dt_low, w_step, 1, 1),
            jnp.sum(inject_grad, axis=3).reshape(-1, STATES),
            jnp.sum(readout_grad, axis=3).reshape(-1, STATES),
        ],
        axis=1,
    ).astype(BF16)
    x_weight_grad = dot(act_low, projected_grad, 0, 0)
    act_grad = act_grad + dot(projected_grad, w_x, 1, 1).reshape(micros, tokens, inner)
    conv_grad = act_grad * silu_back(conv)
    chan_rows = [
        jnp.sum(conv_grad * padded[:, tap : tap + tokens] * same[tap], axis=(0, 1))
        for tap in range(CONV)
    ]
    chan_rows += [jnp.sum(conv_grad, axis=(0, 1)), jnp.sum(pre_dt, axis=(0, 1)), skip_grad]
    chan_grad = jnp.concatenate(
        [jnp.stack(chan_rows), jnp.sum(rate_grad, axis=0) * rate], axis=0
    )
    padded_grad = jnp.zeros((micros, tokens + CONV - 1, inner), F32)
    for tap in range(CONV):
        padded_grad = padded_grad + jnp.pad(
            channel[tap] * conv_grad * same[tap], ((0, 0), (tap, CONV - 1 - tap), (0, 0))
        )
    edge_grad = move_rows(padded_grad[:, : CONV - 1], -1)
    raw_grad = padded_grad[:, CONV - 1 :] + jnp.pad(
        edge_grad, ((0, 0), (tokens - (CONV - 1), 0), (0, 0))
    )
    xz_grad = jnp.concatenate([raw_grad, z_grad], axis=2).reshape(-1, 2 * inner).astype(BF16)
    in_grad = dot(u_low, xz_grad, 0, 0)
    gain_zero, more = normalize_back(hat0, scale0, gains[0], dot(xz_grad, w_in, 1, 1))
    x0_grad = (x1_grad + more).astype(BF16)
    grads = (
        s_table,
        scatter_mat(in_grad, 1),
        s_out,
        s_up,
        s_down,
        x_weight_grad,
        step_weight_grad,
        route_grad,
        chan_grad,
        jnp.stack([gain_zero, gain_one, gain_two]),
    )
    return grads, moved, x0_grad, loss_here, count_here, rows_here


def scatter_mat(grad, dim):
    return lax.psum_scatter(grad.astype(BF16), "mat", scatter_dimension=dim, tiled=True)


def ortho_kernel(
    place, scale, moment_a, moment_b, moment_c, experts, inward, outward, out,
    current, rounded, gram, low, poly, slope, trace,
):
    blocks, size, _ = experts.shape
    tile = TILE
    tiles = size // tile
    cuts = size // CUT
    row = lax.broadcasted_iota(jnp.int32, (tile, size), 0)
    column = lax.broadcasted_iota(jnp.int32, (tile, size), 1)
    turned = jnp.logical_or(place[0] == DOWN_PLACE, place[0] == OUT_PLACE)

    def band(index):
        return pl.ds(pl.multiple_of(index * tile, tile), tile)

    def load(block, index, moment, grad, turn):
        values = MOMENTUM * moment.astype(F32) + scale[0] * grad.astype(F32)
        values = values.astype(BF16).astype(F32)
        trace[...] += jnp.sum(values * values, axis=0, keepdims=True)
        if turn:
            values = values.T
            current[block, :, pl.ds(index * CUT, CUT)] = values
            rounded[0, block, :, pl.ds(index * CUT, CUT)] = values.astype(BF16)
        else:
            current[block, pl.ds(index * CUT, CUT), :] = values
            rounded[0, block, pl.ds(index * CUT, CUT), :] = values.astype(BF16)

    moments = (moment_a, moment_b, moment_c)
    trace[...] = jnp.zeros_like(trace)

    def load_block(block, _):
        for index in range(cuts):
            rows = pl.ds(index * CUT, CUT)

            @pl.when(place[0] == UP_PLACE)
            def _():
                load(block, index, moments[index][block], experts[block, rows, :], False)

            @pl.when(place[0] == DOWN_PLACE)
            def _():
                load(block, index, moments[index][block], experts[block, rows, :], True)

            @pl.when(place[0] == IN_PLACE)
            def _():
                load(block, index, moments[index][block], inward[block, rows, :], False)

            @pl.when(place[0] == OUT_PLACE)
            def _():
                room = outward.shape[1] - index * CUT
                if room >= CUT:
                    grad = outward[block, rows, :].astype(F32)
                elif room > 0:
                    grad = outward[block, pl.ds(index * CUT, room), :].astype(F32)
                    grad = jnp.concatenate([grad, jnp.zeros((CUT - room, size), F32)], axis=0)
                else:
                    grad = jnp.zeros((CUT, size), F32)
                load(block, index, moments[index][block], grad, True)

        return 0

    lax.fori_loop(0, blocks, load_block, 0)
    total = jnp.sum(trace[...])
    factor = 1.0 / (jnp.sqrt(total + jnp.zeros((8, 128), F32)) + 1e-07)[0:1, 0:1]

    def sweep(step, gain):
        now = step % 2

        def make_gram(index, diagonal):
            total = jnp.zeros((tile, size), F32)
            for block in range(blocks):
                total = total + dot(
                    rounded[now, block, band(index), :], rounded[now, block], 1, 1
                )
            total = total * gain
            mask = column == row + index * tile
            gram[band(index), :] = total
            low[band(index), :] = jnp.where(mask, 0.0, total).astype(BF16)
            return diagonal + jnp.sum(jnp.where(mask, total, 0.0), axis=0, keepdims=True)

        diagonal = lax.fori_loop(0, tiles, make_gram, jnp.zeros((1, size), F32))

        def make_poly(index, _):
            mask = column == row + index * tile
            values = gram[band(index), :]
            own = jnp.sum(jnp.where(mask, values, 0.0), axis=1, keepdims=True)
            rest = jnp.where(mask, own * own, (own + diagonal) * values)
            total = COEF_B * values + COEF_C * (dot(low[band(index), :], low[...], 1, 0) + rest)
            poly[band(index), :] = jnp.where(mask, 0.0, total).astype(BF16)
            part = jnp.sum(jnp.where(mask, total, 0.0), axis=1, keepdims=True)
            slope[band(index), :] = jnp.broadcast_to(part + COEF_A, (tile, 128))
            return _

        lax.fori_loop(0, tiles, make_poly, 0)

        def advance(lap, _):
            block, index = lap // tiles, lap % tiles
            scaled = spread(slope[band(index), :], size) * current[block, band(index), :]
            values = scaled + dot(poly[band(index), :], rounded[now, block], 1, 0)
            current[block, band(index), :] = values
            rounded[1 - now, block, band(index), :] = values.astype(BF16)
            return _

        def advance_first(lap, _):
            block, index = lap // tiles, lap % tiles
            scaled = spread(slope[band(index), :], size) * current[block, band(index), :]
            product = dot(poly[band(index), :], rounded[now, block], 1, 0)
            values = (scaled + product) * factor
            current[block, band(index), :] = values
            rounded[1 - now, block, band(index), :] = values.astype(BF16)
            return _

        @pl.when(step == 0)
        def _():
            lax.fori_loop(0, blocks * tiles, advance_first, 0)

        @pl.when(step > 0)
        def _():
            lax.fori_loop(0, blocks * tiles, advance, 0)

        return jnp.ones_like(gain)

    lax.fori_loop(0, ORTHO_STEPS, sweep, factor * factor)

    def store(block, _):
        @pl.when(turned)
        def _():
            for index in range(cuts):
                cut = pl.ds(index * CUT, CUT)
                out[block, :, cut] = current[block, cut, :].T.astype(BF16)

        @pl.when(jnp.logical_not(turned))
        def _():
            for index in range(cuts):
                cut = pl.ds(index * CUT, CUT)
                out[block, cut, :] = current[block, cut, :].astype(BF16)

        return 0

    lax.fori_loop(0, blocks, store, 0)


def orthogonalize(scale, moments, experts, inward, outward):
    blocks, size, width = experts.shape
    vmem = pl.BlockSpec(memory_space=pltpu.VMEM)
    smem = pl.BlockSpec(memory_space=pltpu.SMEM)
    place = lax.axis_index("mat").astype(jnp.int32).reshape(1)
    return pl.pallas_call(
        ortho_kernel,
        out_shape=jax.ShapeDtypeStruct(experts.shape, BF16),
        in_specs=[smem, smem] + [vmem] * 6,
        out_specs=vmem,
        scratch_shapes=[
            pltpu.VMEM((blocks, size, width), F32),
            pltpu.VMEM((2, blocks, size, width), BF16),
            pltpu.VMEM((size, size), F32),
            pltpu.VMEM((size, size), BF16),
            pltpu.VMEM((size, size), BF16),
            pltpu.VMEM((size, 128), F32),
            pltpu.VMEM((1, size), F32),
        ],
        compiler_params=pltpu.CompilerParams(vmem_limit_bytes=56 * 1024 * 1024),
        name="orthogonalize",
    )(place, scale.reshape(1), *moments, experts, inward, outward)


def adamw_update(weight, mean, square, grad, rate, decay):
    mean = BETA_ONE * mean + (1.0 - BETA_ONE) * grad
    square = BETA_TWO * square + (1.0 - BETA_TWO) * grad * grad
    ratio = (
        mean
        / (1.0 - BETA_ONE**STEP_COUNT)
        / (jnp.sqrt(square / (1.0 - BETA_TWO**STEP_COUNT)) + ADAM_EPS)
    )
    return (weight * (1.0 - rate * decay) - rate * ratio, mean, square)


def table_kernel(scale, grad, weight, mean, square, _ahead, new_weight, new_mean, new_square):
    part = weight.shape[0]
    turned = grad[...].T[:part] * scale[0]
    results = adamw_update(weight[...], mean[...], square[...], turned, 0.05, 0.1)
    new_weight[...], new_mean[...], new_square[...] = results


def update_table(scale, grad, weight, mean, square, ahead):
    part, entries = weight.shape
    flat = pl.BlockSpec((part, VOCAB_TILE), lambda i: (0, i))
    return pl.pallas_call(
        table_kernel,
        grid=(-(-entries // VOCAB_TILE),),
        in_specs=[
            pl.BlockSpec(memory_space=pltpu.SMEM),
            pl.BlockSpec((VOCAB_TILE, 256), lambda i: (i, 0)),
            flat,
            flat,
            flat,
            pl.BlockSpec(memory_space=pl.ANY),
        ],
        out_specs=[flat] * 3,
        out_shape=[jax.ShapeDtypeStruct(weight.shape, F32)] * 3,
        compiler_params=kernel_params(),
        cost_estimate=pl.CostEstimate(
            flops=20 * entries * 256,
            bytes_accessed=7 * entries * 256 * 4,
            transcendentals=2 * entries * 256,
        ),
        name="update_table",
    )(scale.reshape(1), grad, weight, mean, square, ahead)


def local(
    token_ids,
    expert_route,
    doc_lengths,
    loss_slots,
    loss_weight,
    target_ids,
    embedding,
    embedding_mom,
    embedding_sq,
    in_project,
    in_project_mom,
    out_project,
    out_project_mom,
    expert_up,
    expert_up_mom,
    expert_down,
    expert_down_mom,
    x_project,
    x_project_mom,
    x_project_sq,
    step_project,
    step_project_mom,
    step_project_sq,
    router_weight,
    router_mom,
    router_sq,
    channel_param,
    channel_mom,
    channel_sq,
    norm_gains,
    gains_mom,
    gains_sq,
):
    micros = token_ids.shape[0]
    mats = lax.axis_size("mat")
    seq_count = lax.axis_size("seq")
    tokens = expert_route.shape[2]
    vocab_part, part = embedding.shape
    ids = exchange([token_ids.reshape(-1, 128)], [True], 12, ("mat",))[0]
    ids = ids.reshape(mats, micros, seq_count, tokens)
    ids = ids.transpose(2, 0, 1, 3).reshape(-1) - lax.axis_index("seq") * vocab_part
    parts = [x_project, step_project, router_weight, channel_param, norm_gains]
    found, small = lookup(ids, embedding, pack_small(parts), 10)
    found, w_table, w_out, w_up, w_down = lax.optimization_barrier(
        (
            found,
            embedding.astype(BF16),
            out_project.astype(BF16),
            expert_up.astype(BF16),
            expert_down.astype(BF16),
        )
    )
    small = unpack_small(small, parts)
    weights = (
        lax.all_gather(w_table, "mat", axis=1, tiled=True),
        lax.all_gather(in_project.astype(BF16), "mat", axis=1, tiled=True),
        lax.all_gather(w_out, "mat", axis=0, tiled=True),
        lax.all_gather(w_up, "mat", axis=2, tiled=True),
        lax.all_gather(w_down, "mat", axis=1, tiled=True),
        small[0].reshape(-1, small[0].shape[2]),
        columns(small[1]),
        small[2].reshape(-1, small[2].shape[2]),
        columns(small[3]),
        columns(small[4]),
    )
    half = micros * tokens // 2
    tails = found[:, 2 * half :].reshape(mats, half, 2, part - 128).transpose(0, 2, 1, 3)
    heads = found[:, : 2 * half].reshape(mats, 2, half, 128)
    embedded = jnp.concatenate([heads, tails], axis=3).transpose(1, 2, 0, 3)
    embedded = embedded.reshape(micros * tokens, mats * part)
    loss_all = micros * lax.axis_size("mat") * loss_weight.shape[2]
    moments = jnp.stack(
        [
            expert_up_mom[0],
            in_project_mom,
            expert_down_mom[0],
            jnp.pad(out_project_mom, ((0, D - out_project_mom.shape[0]), (0, 0))),
        ]
    ).astype(BF16)
    grads, moved, x0_grad, loss_part, count_part, rows_here = step_grads(
        weights,
        jnp.split(moments, 3, axis=1),
        embedded,
        expert_route[:, 0, :, 0],
        doc_lengths[:, 0],
        loss_slots[:, 0],
        loss_weight[:, 0],
        target_ids[:, 0],
        loss_all,
    )
    row_loss = rows_here[:, None, :]
    s_table, s_in, s_out, s_up, s_down, g_x, g_step, g_route, g_chan, g_gain = grads
    pieces = (
        g_x.reshape(mats, -1),
        g_step.reshape(g_step.shape[0], mats, -1).transpose(1, 0, 2).reshape(mats, -1),
        g_route.reshape(mats, -1),
        g_chan.reshape(g_chan.shape[0], mats, -1).transpose(1, 0, 2).reshape(mats, -1),
        g_gain.reshape(g_gain.shape[0], mats, -1).transpose(1, 0, 2).reshape(mats, -1),
    )
    packed = jnp.concatenate(pieces, axis=1)
    unit = seq_count * 2048
    packed = jnp.pad(packed, ((0, 0), (0, -packed.shape[1] % unit)))
    packed = packed.astype(BF16).reshape(mats, -1, 128)
    x0_parts = x0_grad.reshape(2, -1, mats, part).transpose(2, 0, 1, 3)
    x0_heads = x0_parts[..., :128].reshape(mats, -1, 128)
    x0_tails = jnp.concatenate([x0_parts[:, 0, :, 128:], x0_parts[:, 1, :, 128:]], axis=2)
    x0_rows = 3 * micros * tokens // 2
    mixed = lax.all_to_all(
        jnp.concatenate([x0_heads, x0_tails, packed], axis=1),
        "mat",
        split_axis=0,
        concat_axis=0,
        tiled=True,
    )
    packed = jnp.sum(mixed[:, x0_rows:].astype(F32), axis=0).astype(BF16)
    g_table, table_squares, whole_experts = scatter_rows(
        ids.reshape(-1, 128),
        mixed[:, :x0_rows],
        s_table,
        vocab_part,
        13,
        [s_up[0], s_down[0]],
    )
    s_in, s_out, packed = exchange(
        [
            s_in.reshape(seq_count, -1, D),
            s_out.reshape(seq_count, -1, D),
            packed.reshape(seq_count, -1, 128),
        ],
        [False, False, False],
        14,
        ahead=[g_table],
    )
    s_in = jnp.sum(s_in.astype(F32), axis=0)
    s_out = jnp.sum(s_out.astype(F32), axis=0)
    packed = jnp.sum(packed.astype(F32), axis=0)
    s_up = s_up.astype(F32)
    s_down = s_down.astype(F32)
    squares = sum(jnp.sum(g * g) for g in (s_up, s_down, s_in, s_out, packed))
    squares = squares + jnp.sum(table_squares[0])
    tallies = jnp.stack([squares, loss_part, count_part])
    tallies = jnp.broadcast_to(jnp.pad(tallies, (0, 5))[:, None], (8, 128))
    g_in, g_out, packed, totals, whole_in, whole_out = gather_seq(
        [s_in.astype(BF16), s_out.astype(BF16), packed, tallies],
        15,
        relays=[(0, IN_PLACE), (1, OUT_PLACE)],
    )
    g_in = g_in.reshape(-1, D).astype(F32)
    g_out = g_out.reshape(-1, D).astype(F32)
    totals = exchange([jnp.sum(totals, axis=0)], [True], 11, ("mat",))[0]
    totals = jnp.sum(totals[:, :, 0], axis=0)
    packed = packed.reshape(-1)
    shards, offset = [], 0
    for piece, like in zip(
        pieces, (x_project, step_project, router_weight, channel_param, norm_gains)
    ):
        shards.append(packed[offset : offset + piece.shape[1]].reshape(like.shape))
        offset += piece.shape[1]
    squares, loss_total, loss_count = totals[0], totals[1], totals[2]
    grad_norm = jnp.sqrt(squares)
    scale = jnp.minimum(1.0, CLIP_NORM / (grad_norm + 1e-06))
    mom_in = MOMENTUM * in_project_mom + g_in * scale
    mom_out = MOMENTUM * out_project_mom + g_out * scale
    mom_up = MOMENTUM * expert_up_mom + s_up * scale
    mom_down = MOMENTUM * expert_down_mom + s_down * scale
    ortho = orthogonalize(
        scale,
        moved,
        whole_experts,
        whole_in.reshape(mats, D, -1),
        whole_out.reshape(mats, -1, D),
    )
    table_new = update_table(
        scale, g_table, embedding.T, embedding_mom.T, embedding_sq.T, ortho
    )
    table_new = [values.T for values in table_new]
    ortho = lax.all_to_all(ortho, "mat", split_axis=0, concat_axis=0, tiled=True).astype(F32)
    shrink = 1.0 - LR_MUON * DECAY_MUON
    new_up = expert_up * shrink - LR_MUON * 0.2 * math.sqrt(max(D, FF)) * ortho[UP_PLACE][None]
    new_in = in_project * shrink - LR_MUON * 0.2 * math.sqrt(max(D, 2 * DI)) * ortho[IN_PLACE]
    new_down = (
        expert_down * shrink - LR_MUON * 0.2 * math.sqrt(max(D, FF)) * ortho[DOWN_PLACE][None]
    )
    new_out = (
        out_project * shrink
        - LR_MUON * 0.2 * math.sqrt(max(D, DI)) * ortho[OUT_PLACE, : out_project.shape[0]]
    )
    x_new = adamw_update(x_project, x_project_mom, x_project_sq, shards[0] * scale, 0.06, 0.1)
    step_new = adamw_update(
        step_project, step_project_mom, step_project_sq, shards[1] * scale, 0.06, 0.1
    )
    route_new = adamw_update(router_weight, router_mom, router_sq, shards[2] * scale, 0.06, 0.1)
    chan_new = adamw_update(channel_param, channel_mom, channel_sq, shards[3] * scale, 1.0, 0.0)
    gains_new = adamw_update(norm_gains, gains_mom, gains_sq, shards[4] * scale, 0.4, 0.0)
    return (
        loss_total,
        loss_count,
        grad_norm,
        row_loss,
        *table_new,
        new_in,
        mom_in,
        new_out,
        mom_out,
        new_up,
        mom_up,
        new_down,
        mom_down,
        *x_new,
        *step_new,
        *route_new,
        *chan_new,
        *gains_new,
    )


def solution(mesh):
    in_specs = (
        P(None, "mat", None),
        P(None, "mat", "seq", None),
        P(None, "mat", None),
        P(None, "mat", "seq"),
        P(None, "mat", None),
        P(None, "mat", None),
        P("seq", "mat"),
        P("seq", "mat"),
        P("seq", "mat"),
        P(None, "mat"),
        P(None, "mat"),
        P("mat", None),
        P("mat", None),
        P("seq", None, "mat"),
        P("seq", None, "mat"),
        P("seq", "mat", None),
        P("seq", "mat", None),
        P("mat", None),
        P("mat", None),
        P("mat", None),
        P(None, "mat"),
        P(None, "mat"),
        P(None, "mat"),
        P("mat", None),
        P("mat", None),
        P("mat", None),
        P(None, "mat"),
        P(None, "mat"),
        P(None, "mat"),
        P(None, "mat"),
        P(None, "mat"),
        P(None, "mat"),
    )
    out_specs = (
        P(),
        P(),
        P(),
        P(None, "mat", "seq"),
        P("seq", "mat"),
        P("seq", "mat"),
        P("seq", "mat"),
        P(None, "mat"),
        P(None, "mat"),
        P("mat", None),
        P("mat", None),
        P("seq", None, "mat"),
        P("seq", None, "mat"),
        P("seq", "mat", None),
        P("seq", "mat", None),
        P("mat", None),
        P("mat", None),
        P("mat", None),
        P(None, "mat"),
        P(None, "mat"),
        P(None, "mat"),
        P("mat", None),
        P("mat", None),
        P("mat", None),
        P(None, "mat"),
        P(None, "mat"),
        P(None, "mat"),
        P(None, "mat"),
        P(None, "mat"),
        P(None, "mat"),
    )
    return jax.shard_map(local, mesh=mesh, in_specs=in_specs, out_specs=out_specs, check_vma=False)
```

time: 4680 us -> 986 us (0.21); the launches traced: 4610 us -> 982 us
  waiting for transfers between devices: 1310 us -> 30.8 us
  other arithmetic: 1080 us -> 100 us
  local copies, waits for them, and re-layouts: 826 us -> 98.5 us
  matrix products: 809 us -> 121 us
  Pallas kernels: 0 us -> 583 us
  blocking collectives: 479 us -> 0 us
    dot_general x632 -> x30, matrix products: 809 us -> 121 us  [the longest x18 65.1 us: dot(): lax.dot_general(left, right, (((left_dim,), (right_dim,)), ((), ())), pre...]
    pallas_call x0 -> x22, Pallas kernels: none -> 583 us  [the longest x9 209 us: exchange(): pl.pallas_call(functools.partial(exchange_kernel, tuple(groups), tuple(ga...]
    psum x6 -> x0, waiting for transfers between devices: 551 us -> none  [the longest x5 404 us: orthogonalize(): lax.psum(parts[0], 'mat').astype(jnp.float32)]
    reduce_scatter x11 -> x5, waiting for transfers between devices: 418 us -> 0.52 us  [scatter_mat(): lax.psum_scatter(grad.astype(BF16), 'mat', scatter_dimension=dim, tiled=T...]
    all_gather x19 -> x0, blocking collectives: 402 us -> none  [the longest x6 207 us: carried_in(): gathered = jax.tree.map(lambda a: lax.all_gather(a, axis), part)]
    while x448 -> x0, other arithmetic: 351 us -> none
    reduce_sum x190 -> x29, other arithmetic: 356 us -> 33.7 us  [the longest x5 8.21 us: local(): squares = sum((jnp.sum(g * g) for g in (s_up, s_down, s_in, s_out, packed)))]
    dynamic_update_slice x288 -> x0, local copies, waits for them, and re-layouts: 204 us -> none  [mixer_core(): lax.scan(advance, jnp.zeros((states, inner), jnp.float32), (activated, st...]
where the time goes in v1:
time: 986 us; the launch traced here: 982 us
  Pallas kernels  583 us (59%)
  matrix products  121 us (12%)
  other arithmetic  100 us (10%)
  local copies, waits for them, and re-layouts  98.5 us (10%)
  waiting for transfers between devices  30.8 us (3%)
  starting transfers between devices  25.1 us (3%)
  between operations  22.6 us (2%)
    pallas_call x9, Pallas kernels, exchange(): pl.pallas_call(functools.partial(exchange_kernel, tuple(groups), tuple(ga...  209 us
    pallas_call x4, Pallas kernels, gather_seq(): pl.pallas_call(functools.partial(gather_kernel, arrays, len(ahead), tuple...  97 us
    pallas_call x1, Pallas kernels, orthogonalize(): pl.pallas_call(ortho_kernel, out_shape=jax.ShapeDtypeStruct(experts.shape...  77.9 us
    dot_general x18, matrix products, dot(): lax.dot_general(left, right, (((left_dim,), (right_dim,)), ((), ())), pre...  65.1 us
    pallas_call x1, Pallas kernels, scatter_rows(): pl.pallas_call(functools.partial(scatter_rows_kernel, entries), out_shape...  64 us
    pallas_call x1, Pallas kernels, lookup(): pl.pallas_call(lookup_kernel, out_shape=[jax.ShapeDtypeStruct((mats, 384,...  55.4 us
    unnamed x337, local copies, waits for them, and re-layouts  45.1 us
    pallas_call x1, Pallas kernels, scan_backward(): pl.pallas_call(body, grid=(micros, inner // LANES), in_specs=[scalars, sc...  30.7 us
  transfers between devices with their start and end apart: 14, of which 3 were waited for; matrix products, arithmetic and copies ran while one was open for 23% of the time, Pallas kernels for 41%

profile of v1, /device:TPU:0, one launch (start us, length us, event | category | flops | bytes accessed | tf_op | source)
XLA Modules:
  0.0 982.0 jit_solution(15133003254986385773)
XLA Ops:
  37.4 55.4 %lookup.1 = (bf16[4,384,128]{2,1,0:T(8,128)(2,1)}, bf16[4,64,1024]{2,1,0:T(8,128)(2,1)}) custom-call(s32[8192]{0:T(1024)} %and_select_fusion.ids, f32[6296,256]{1,0:T(8,128)} %pad_convert_fusion.table, bf16[64,1024]{1,0:T(8,128)(2,1)} %reshape.665.small), custom_call_target="tpu_custom_call" | custom-call | tf_op jit(solution)/shard_map/lookup/pallas_call | solution.py:826
  118.9 13.6 %collective-permute-start = (f32[2,3,1536]{2,1,0:T(4,128)}, f32[2,3,1536]{2,1,0:T(4,128)}, u32[]{:S(2)}, u32[]{:S(2)}) collective-permute-start(f32[2,3,1536]{2,1,0:T(4,128)} %slice.263), channel_id=1, source_target_pairs={{0,4},{4,8},{8,12},{12,16},{16,20},{20,24},{24,28},{1,5},{5,9},{9,... | collective-permute-start | bytes 110600 | tf_op jit(solution)/shard_map/ppermute | solution.py:1018
  161.6 8.0 scan_end.1
  171.0 22.9 %gather_seq.4 = (bf16[8,2,16,1536]{3,2,1,0:T(8,128)(2,1)}, f32[8,1,8,1536]{3,2,1,0:T(8,128)}) custom-call(bf16[2,16,1536]{2,1,0:T(8,128)(2,1)} %bitcast.330, f32[1,8,1536]{2,1,0:T(8,128)} %maximum_bitcast_fusion.refs_1_), custom_call_target="tpu_custom_call" | custom-call | tf_op jit(solution)/shard_map/gather_seq/pallas_call | solution.py:641
  195.8 17.8 %scan_forward.1 = (f32[2,128,1536]{2,1,0:T(8,128)S(1)}, f32[2,128,16,1536]{3,2,1,0:T(8,128)}, f32[2,16,1536]{2,1,0:T(8,128)S(1)}) custom-call(s32[1]{0:T(128)} %bitcast.11.place.refs_0_, f32[2,128]{1,0:T(2,128)S(1)} %get-tuple-element.384.keep.refs_1_, f32[2,128,1536]{2,1,0:T(8,128)S(1)} %get-tuple-element.363.dt.refs_2_, ...), custom_call_target="tpu_custom_call" | custom-call | tf_op jit(solution)/shard_map/scan_forward/pallas_call | solution.py:231
  222.4 40.3 %exchange.10 = (bf16[8,64,768]{2,1,0:T(8,128)(2,1)}, bf16[4,256,768]{2,1,0:T(8,128)(2,1)}) custom-call(bf16[8,64,768]{2,1,0:T(8,128)(2,1)} %bitcast.349, bf16[4,256,768]{2,1,0:T(8,128)(2,1)} %get-tuple-element.355.refs_1_), custom_call_target="tpu_custom_call" | custom-call | tf_op jit(solution)/shard_map/exchange/pallas_call | solution.py:383
  262.8 18.8 %multiply_convert_fusion = (bf16[512,3072]{1,0:T(8,128)(2,1)}, f32[512,3072]{1,0:T(8,128)}, f32[512,3072]{1,0:T(8,128)}) fusion(bf16[512,768]{1,0:T(8,128)(2,1)} %bitcast.423, bf16[1,768,3072]{2,1,0:T(8,128)(2,1)} %all-gather.10.cloned.1.call-done), kind=kOutput, calls=%fused_computation.12 | convolution fusion | flops 2518155264 | bytes 21233664 | tf_op jit(solution)/shard_map/erk,ekn->ern/dot_general | solution.py:1171
  288.5 23.0 %exchange.11 = (bf16[8,64,768]{2,1,0:T(8,128)(2,1)}, bf16[4,256,768]{2,1,0:T(8,128)(2,1)}) custom-call(bf16[8,64,768]{2,1,0:T(8,128)(2,1)} %bitcast.385, bf16[4,256,768]{2,1,0:T(8,128)(2,1)} %get-tuple-element.354.refs_1_), custom_call_target="tpu_custom_call" | custom-call | tf_op jit(solution)/shard_map/exchange/pallas_call | solution.py:383
  316.7 18.7 %gather_seq.5 = bf16[8,2,32,768]{3,2,1,0:T(8,128)(2,1)} custom-call(bf16[2,32,768]{2,1,0:T(8,128)(2,1)} %convolution_convert_fusion.10.refs_0_), custom_call_target="tpu_custom_call" | custom-call | tf_op jit(solution)/shard_map/gather_seq/pallas_call | solution.py:641
  335.4 9.3 select_reduce_fusion
  351.2 8.2 exchange.12
  361.1 7.9 fusion.3
  371.7 7.9 convolution_convert_fusion.refs_1_
  380.0 11.2 %convolution_convert_fusion.8 = bf16[512,768]{1,0:T(8,128)(2,1)} fusion(bf16[512,6288]{0,1:T(8,128)(2,1)} %copy-done.55, bf16[6288,768]{0,1:T(8,128)(2,1)} %all-gather.14.cloned.1.call-done), kind=kOutput, calls=%fused_computation.103 | convolution fusion | flops 4945477632 | bytes 16883712 | tf_op jit(solution)/shard_map/dot_general | solution.py:44
  391.2 30.5 %exchange.13 = (bf16[8,64,768]{2,1,0:T(8,128)(2,1)}, bf16[4,256,768]{2,1,0:T(8,128)(2,1)}) custom-call(bf16[8,64,768]{2,1,0:T(8,128)(2,1)} %bitcast.384, bf16[4,256,768]{2,1,0:T(8,128)(2,1)} %get-tuple-element.353.refs_1_), custom_call_target="tpu_custom_call" | custom-call | tf_op jit(solution)/shard_map/exchange/pallas_call | solution.py:383
  426.9 18.0 %exchange.14 = bf16[8,64,768]{2,1,0:T(8,128)(2,1)} custom-call(bf16[8,64,768]{2,1,0:T(8,128)(2,1)} %bitcast.347, bf16[768,6288]{1,0:T(8,128)(2,1)} %convolution_convert_fusion.refs_1_), custom_call_target="tpu_custom_call" | custom-call | tf_op jit(solution)/shard_map/exchange/pallas_call | solution.py:383
  444.9 7.0 fusion.21.refs_1_
  451.9 8.5 add_convert_fusion
  475.8 7.9 fusion.41
  483.7 22.1 %exchange.15 = bf16[8,64,768]{2,1,0:T(8,128)(2,1)} custom-call(bf16[8,64,768]{2,1,0:T(8,128)(2,1)} %bitcast.387, bf16[1,768,3072]{2,1,0:T(8,128)(2,1)} %get-tuple-element.83.refs_1_, bf16[1,3072,768]{2,1,0:T(8,128)(2,1)} %get-tuple-element.84.refs_2_), custom_call_target="tpu_custom_call" | custom-call | tf_op jit(solution)/shard_map/exchange/pallas_call | solution.py:383
  517.0 7.6 scan_start.1
  525.3 22.0 %gather_seq.6 = bf16[8,2,16,1536]{3,2,1,0:T(8,128)(2,1)} custom-call(bf16[2,16,1536]{2,1,0:T(8,128)(2,1)} %bitcast.329), custom_call_target="tpu_custom_call" | custom-call | tf_op jit(solution)/shard_map/gather_seq/pallas_call | solution.py:641
  548.5 30.7 %scan_backward.1 = (f32[2,128,1536]{2,1,0:T(8,128)S(1)}, f32[2,128,1536]{2,1,0:T(8,128)S(1)}, f32[2,128,16,128]{3,2,1,0:T(8,128)}, f32[2,128,16,128]{3,2,1,0:T(8,128)}, f32[2,16,1536]{2,1,0:T(8,128)S(1)}) custom-call(s32[1]{0:T(128)} %bitcast.11.place.refs_0_, f32[2,128]{1,0:T(2,128)S(1)} %get-tuple-element.384.keep.refs_1_, f32[2,128,1536]{2,1,0:T(8,128)} %copy-done.4, ...), custom_call_target="tpu_custom_call" | custom-call | tf_op jit(solution)/shard_map/scan_backward/pallas_call | solution.py:275
  588.3 7.0 fusion.116
  631.8 8.5 all-to-all-done
  650.4 64.0 %scatter_rows.1 = (f32[6400,256]{1,0:T(8,128)}, f32[8,256]{1,0:T(8,128)S(1)}, bf16[4,768,768]{2,1,0:T(8,128)(2,1)}) custom-call(s32[64,128]{1,0:T(8,128)S(1)} %bitcast.332, bf16[4,384,128]{2,1,0:T(8,128)(2,1)S(1)} %slice.293.rows, bf16[192,6400]{1,0:T(8,128)(2,1)S(1)} %copy-done.10, bf16[768,768]{1,0:T(8,128)(2,1)S(1)} %bitcast.318, ...), custom_call_target="tpu_custom_call" | custom-call | tf_op jit(solution)/shard_map/scatter_rows/pallas_call | solution.py:988
  715.0 47.0 %exchange.16 = (bf16[8,96,768]{2,1,0:T(8,128)(2,1)}, bf16[8,48,768]{2,1,0:T(8,128)(2,1)}, bf16[8,64,128]{2,1,0:T(8,128)(2,1)}) custom-call(bf16[8,96,768]{2,1,0:T(8,128)(2,1)} %bitcast.372, bf16[8,48,768]{2,1,0:T(8,128)(2,1)} %bitcast.388, bf16[8,64,128]{2,1,0:T(8,128)(2,1)} %bitcast.394, f32[6400,256]{1,0:T(8,128)} %get-tuple-element.92.refs_3_.grad), custom_call_target="tpu_custom_call" | custom-call | tf_op jit(solution)/shard_map/exchange/pallas_call | solution.py:383
  772.5 33.4 %gather_seq.7 = (bf16[8,2,48,768]{3,2,1,0:T(8,128)(2,1)}, bf16[8,1,48,768]{3,2,1,0:T(8,128)(2,1)}, f32[8,2,32,128]{3,2,1,0:T(8,128)}, f32[8,1,8,128]{3,2,1,0:T(8...) custom-call(bf16[2,48,768]{2,1,0:T(8,128)(2,1)} %bitcast.390, ...), custom_call_target="tpu_custom_call" | custom-call | tf_op jit(solution)/shard_map/gather_seq/pallas_call | solution.py:641
  807.3 13.5 %exchange.17 = f32[4,8,128]{2,1,0:T(8,128)} custom-call(f32[8,128]{1,0:T(8,128)} %reduce_sum.431.refs_0_), custom_call_target="tpu_custom_call" | custom-call | tf_op jit(solution)/shard_map/exchange/pallas_call | solution.py:383
  827.5 77.9 %orthogonalize.1._ahead = bf16[4,768,768]{2,1,0:T(8,128)(2,1)} custom-call(s32[1]{0:T(128)} %bitcast.108.place, f32[1]{0:T(128)} %bitcast.104.scale, bf16[4,256,768]{2,1,0:T(8,128)(2,1)} %get-tuple-element.98.moment_a, bf16[4,256,768]{2,1,0:T(8,128)(2,1)} %get-tuple-element.99.moment_b, bf16[4,256,768]{2,1,0:T(8,128)(2,1)} %get-tuple-element.100.moment_c, ...), custom_call_target="tpu_custom_call" | custom-call | tf_op jit(solution)/shard_map/orthogonalize/pallas_call | solution.py:1474
  915.9 16.2 %update_table.1 = (f32[192,6288]{1,0:T(8,128)}, f32[192,6288]{1,0:T(8,128)}, f32[192,6288]{1,0:T(8,128)}) custom-call(f32[1]{0:T(128)} %bitcast.104.scale, f32[6400,256]{1,0:T(8,128)} %get-tuple-element.92.refs_3_.grad, f32[192,6288]{1,0:T(8,128)} %bitcast.333, f32[192,6288]{1,0:T(8,128)} %bitcast.343, f32[192,6288]{1,0:T(8,128)} %bitcast.344, ...), custom_call_target="tpu_custom_call" | custom-call | flops 32194560 | bytes 45072384 | tf_op jit(solution)/shard_map/update_table/pallas_call | solution.py:1514
  944.7 19.8 %all-to-all-done.1 = bf16[4,768,768]{2,1,0:T(8,128)(2,1)} async-done(((bf16[4,768,768]{2,1,0:T(8,128)(2,1)}), bf16[4,768,768]{2,1,0:T(8,128)(2,1)}, u32[]{:S(2)}, u32[]{:S(2)}) %all-to-all-start.1) | async-done | bytes 4718624 | tf_op jit(solution)/shard_map/all_to_all | solution.py:1714
  (616 shorter events, 255.0 us)
Async XLA Ops:
  7.2 107.0 %all-gather.6.cloned.1.call-start = ((), (), s32[]{:S(2)}) async-start(), calls=%async_computation.7 | async-start | bytes 5898240 | tf_op jit(solution)/shard_map/all_gather | solution.py:1593
  10.1 206.2 %all-gather.8.cloned.1.call-start = ((), (), s32[]{:S(2)}) async-start(), calls=%async_computation.8 | async-start | bytes 2949120 | tf_op jit(solution)/shard_map/all_gather | solution.py:1594
  92.8 170.0 %all-gather.10.cloned.1.call-start = ((), (), s32[]{:S(2)}) async-start(), calls=%async_computation.9 | async-start | bytes 5898240 | tf_op jit(solution)/shard_map/all_gather | solution.py:1595
  93.6 188.1 %all-gather.12.cloned.1.call-start = ((), (), s32[]{:S(2)}) async-start(), calls=%async_computation.10 | async-start | bytes 5898240 | tf_op jit(solution)/shard_map/all_gather | solution.py:1596
  94.1 241.3 %all-gather.14.cloned.1.call-start = ((), (), s32[]{:S(2)}) async-start(), calls=%async_computation.11 | async-start | bytes 12288000 | tf_op jit(solution)/shard_map/all_gather | solution.py:1592
  97.3 369.6 %reduce-scatter.6.cloned.1.call-start = ((), (), s32[]{:S(2)}) async-start(), calls=%async_computation.12 | async-start | bytes 12288000 | tf_op jit(solution)/shard_map/reduce_scatter | solution.py:1325
  114.2 18.3 %copy-start.67 = (bf16[1,4,64,1024]{3,1,2,0:T(4,128)(2,1)S(1)}, bf16[1,4,64,1024]{3,1,2,0:T(4,128)(2,1)}, u32[]{:S(2)}) copy-start(bf16[1,4,64,1024]{3,1,2,0:T(4,128)(2,1)} %copy-done.66) | copy-start | bytes 1572868
  118.2 34.3 %copy-start.24 = (f32[2,128,3072]{2,1,0:T(8,128)}, f32[2,128,3072]{2,1,0:T(8,128)S(1)}, u32[]{:S(2)}) copy-start(f32[2,128,3072]{2,1,0:T(8,128)S(1)} %fusion.18) | copy-start | bytes 9437188
  118.9 33.8 %collective-permute-start = (f32[2,3,1536]{2,1,0:T(4,128)}, f32[2,3,1536]{2,1,0:T(4,128)}, u32[]{:S(2)}, u32[]{:S(2)}) collective-permute-start(f32[2,3,1536]{2,1,0:T(4,128)} %slice.263), channel_id=1, source_target_pairs={{0,4},{4,8},{8,12},{12,16},{16,20},{20,24},{24,28},{1,5},{5,9},{9,... | collective-permute-start | bytes 110600 | tf_op jit(solution)/shard_map/ppermute | solution.py:1018
  156.1 358.6 %copy-start = (f32[2,128,1536]{2,1,0:T(8,128)}, f32[2,128,1536]{2,1,0:T(8,128)S(1)}, u32[]{:S(2)}) copy-start(f32[2,128,1536]{2,1,0:T(8,128)S(1)} %get-tuple-element.348.act.refs_3_) | copy-start | bytes 4718596
  160.9 356.1 %copy-start.4 = (f32[2,128,1536]{2,1,0:T(8,128)}, f32[2,128,1536]{2,1,0:T(8,128)S(1)}, u32[]{:S(2)}) copy-start(f32[2,128,1536]{2,1,0:T(8,128)S(1)} %get-tuple-element.363.dt.refs_2_) | copy-start | bytes 4718596
  195.8 19.0 %copy-start.25 = (f32[2,128,3072]{2,1,0:T(8,128)S(1)}, f32[2,128,3072]{2,1,0:T(8,128)}, u32[]{:S(2)}) copy-start(f32[2,128,3072]{2,1,0:T(8,128)} %copy-done.24) | copy-start | bytes 9437188
  219.2 43.6 %copy-start.118 = (f32[256]{0:T(256)}, f32[256]{0:T(256)S(1)}, u32[]{:S(2)}) copy-start(f32[256]{0:T(256)S(1)} %add_rsqrt_fusion.1) | copy-start | bytes 3076
  314.8 30.0 %copy-start.114 = (f32[256]{0:T(256)}, f32[256]{0:T(256)S(1)}, u32[]{:S(2)}) copy-start(f32[256]{0:T(256)S(1)} %add_rsqrt_fusion) | copy-start | bytes 3076
  379.6 261.4 %reduce-scatter.12.cloned.1.call-start = ((), (), s32[]{:S(2)}) async-start(), calls=%async_computation.15 | async-start | bytes 5898240 | tf_op jit(solution)/shard_map/reduce_scatter | solution.py:1325
  391.2 31.9 %copy-start.123 = (s32[2,1,32]{2,1,0:T(1,128)S(1)}, s32[2,1,32]{2,1,0:T(1,128)}, u32[]{:S(2)}) copy-start(s32[2,1,32]{2,1,0:T(1,128)} %broadcast_subtract_fusion) | copy-start | bytes 772
  391.2 32.5 %copy-start.115 = (f32[256]{0:T(256)S(1)}, f32[256]{0:T(256)}, u32[]{:S(2)}) copy-start(f32[256]{0:T(256)} %copy-done.114) | copy-start | bytes 3076
  466.9 176.7 %reduce-scatter.14.cloned.1.call-start = ((), (), s32[]{:S(2)}) async-start(), calls=%async_computation.16 | async-start | bytes 5898240 | tf_op jit(solution)/shard_map/reduce_scatter | solution.py:1325
  467.6 247.4 %reduce-scatter.10.cloned.1.call-start = ((), (), s32[]{:S(2)}) async-start(), calls=%async_computation.14 | async-start | bytes 2949120 | tf_op jit(solution)/shard_map/reduce_scatter | solution.py:1325
  525.3 22.1 %copy-start.15 = (f32[8,1,8,1536]{3,2,1,0:T(8,128)S(1)}, f32[8,1,8,1536]{3,2,1,0:T(8,128)}, u32[]{:S(2)}) copy-start(f32[8,1,8,1536]{3,2,1,0:T(8,128)} %get-tuple-element.74) | copy-start | bytes 1179652
  547.4 167.6 %reduce-scatter.8.cloned.1.call-start = ((), (), s32[]{:S(2)}) async-start(), calls=%async_computation.13 | async-start | bytes 5898240 | tf_op jit(solution)/shard_map/reduce_scatter | solution.py:1325
  548.5 30.7 %copy-start.69 = (f32[2,128,1536]{2,1,0:T(8,128)S(1)}, f32[2,128,1536]{2,1,0:T(8,128)}, u32[]{:S(2)}) copy-start(f32[2,128,1536]{2,1,0:T(8,128)} %get-tuple-element.385) | copy-start | bytes 4718596
  598.0 8.9 collective-permute-start.1
  620.3 20.0 %all-to-all-start = ((bf16[4,896,128]{2,1,0:T(8,128)(2,1)}), bf16[4,896,128]{2,1,0:T(8,128)(2,1)S(1)}, u32[]{:S(2)}, u32[]{:S(2)}) async-start(bf16[4,896,128]{2,1,0:T(8,128)(2,1)} %pad_maximum_fusion.3), calls=%async_computation.3 | async-start | bytes 1835008 | tf_op jit(solution)/shard_map/all_to_all | solution.py:1645
  805.8 21.5 %copy-start.73 = (f32[8,2,32,128]{3,2,1,0:T(8,128)S(1)}, f32[8,2,32,128]{3,2,1,0:T(8,128)}, u32[]{:S(2)}) copy-start(f32[8,2,32,128]{3,2,1,0:T(8,128)} %get-tuple-element.109) | copy-start | bytes 786436
  905.4 59.1 %all-to-all-start.1 = ((bf16[4,768,768]{2,1,0:T(8,128)(2,1)}), bf16[4,768,768]{2,1,0:T(8,128)(2,1)}, u32[]{:S(2)}, u32[]{:S(2)}) async-start(bf16[4,768,768]{2,1,0:T(8,128)(2,1)} %orthogonalize.1._ahead), calls=%async_computation.6 | async-start | bytes 9437184 | tf_op jit(solution)/shard_map/all_to_all | solution.py:1714
  915.8 17.6 %copy-start.91 = (f32[23,384]{1,0:T(8,128)S(1)}, f32[23,384]{1,0:T(8,128)}, u32[]{:S(2)}) copy-start(f32[23,384]{1,0:T(8,128)} %param.58) | copy-start | bytes 105988
  915.9 18.2 %copy-start.88 = (f32[48,384]{1,0:T(8,128)S(1)}, f32[48,384]{1,0:T(8,128)}, u32[]{:S(2)}) copy-start(f32[48,384]{1,0:T(8,128)} %param.52) | copy-start | bytes 221188
  915.9 18.2 %copy-start.95 = (f32[48,384]{1,0:T(8,128)S(1)}, f32[48,384]{1,0:T(8,128)}, u32[]{:S(2)}) copy-start(f32[48,384]{1,0:T(8,128)} %param.53) | copy-start | bytes 221188
  915.9 18.2 %copy-start.96 = (f32[48,384]{1,0:T(8,128)S(1)}, f32[48,384]{1,0:T(8,128)}, u32[]{:S(2)}) copy-start(f32[48,384]{1,0:T(8,128)} %param.54) | copy-start | bytes 221188
  915.9 18.9 %copy-start.80 = (bf16[8,1,48,768]{3,2,1,0:T(8,128)(2,1)S(1)}, bf16[8,1,48,768]{3,2,1,0:T(8,128)(2,1)}, u32[]{:S(2)}) copy-start(bf16[8,1,48,768]{3,2,1,0:T(8,128)(2,1)} %get-tuple-element.108) | copy-start | bytes 1769476
  944.7 23.1 %copy-start.41 = (f32[1,768,768]{2,1,0:T(8,128)S(1)}, f32[1,768,768]{2,1,0:T(8,128)}, u32[]{:S(2)}) copy-start(f32[1,768,768]{2,1,0:T(8,128)} %param.45) | copy-start | bytes 7077892
  (137 other events, 672.8 us)
Sparse Core Ops, SparseCore 0:
  10.2 41.5 all-gather.5
  92.9 27.7 all-gather.7
  122.9 37.4 all-gather.9
  161.8 37.5 all-gather.11
  201.4 83.3 all-gather.13
  379.7 87.1 reduce-scatter.5
  470.0 47.8 reduce-scatter.11
  521.1 47.8 reduce-scatter.13
  572.1 33.0 reduce-scatter.9
  612.6 56.4 reduce-scatter.7

commit v2 on v1

--- a/solution.py
+++ b/solution.py
@@ -33,10 +33,11 @@
 LANES = 512
 UNROLL = 8
 TILE = 256
-CUT = 256
 VOCAB_TILE = 640
 UP_PLACE, IN_PLACE, DOWN_PLACE, OUT_PLACE = 0, 1, 2, 3
 TOTAL_ROWS = 8
+PAD = 8
+HIDDEN = 512
 MESH = pl.DeviceIdType.MESH
 
 
@@ -50,21 +51,111 @@
     return jnp.concatenate([values] * (width // 128), axis=1)
 
 
-def end_kernel(keep, dt, act, inject, rate, out):
-    micro = pl.program_id(0)
-    tokens, width = dt.shape[1], dt.shape[2]
-    rates = rate[...]
-
-    def block(step, state):
+def same_document(lengths, place, micro, tokens, width):
+    position = place[0] * tokens + lax.broadcasted_iota(jnp.int32, (tokens, 128), 0)
+    bounds, bound = [], 0
+    for index in range(lengths.shape[1] - 1):
+        bound = bound + lengths[micro, index]
+        bounds.append(bound)
+    masks = []
+    for tap in range(CONV):
+        source = position - (CONV - 1) + tap
+        inside = source >= 0
+        for bound in bounds:
+            inside = jnp.logical_and(inside, (source >= bound) == (position >= bound))
+        masks.append(spread(jnp.where(inside, 1.0, 0.0), width))
+    return masks
+
+
+def fill_padded(padded, edge, raw):
+    padded[PAD - (CONV - 1) : PAD, :] = edge[0]
+    padded[PAD:, :] = raw[0]
+
+
+def conv_kernel(lengths, place, raw, edge, channel, w_x, conv_out, act_out, projected, padded):
+    micro, group = pl.program_id(0), pl.program_id(1)
+    tokens, width = raw.shape[1], raw.shape[2]
+    fill_padded(padded, edge, raw)
+    masks = same_document(lengths, place, micro, tokens, width)
+    conv = jnp.broadcast_to(channel[CONV : CONV + 1, :], (tokens, width))
+    for tap in range(CONV):
+        shifted = padded[pl.ds(PAD - (CONV - 1) + tap, tokens), :]
+        conv = conv + channel[tap : tap + 1, :] * shifted * masks[tap]
+    act = conv * lax.logistic(conv)
+    conv_out[0] = conv
+    act_out[0] = act
+
+    @pl.when(group == 0)
+    def _():
+        projected[...] = jnp.zeros_like(projected)
+
+    projected[0] += dot(act.astype(BF16), w_x[...], 1, 0)
+
+
+def conv_back_kernel(
+    lengths, place, raw, edge, channel, w_x, conv, act, act_grad, y_grad, projected_grad,
+    raw_out, head_out, x_out, rows_out, padded, total,
+):
+    micro = pl.program_id(1)
+    tokens, width = raw.shape[1], raw.shape[2]
+    fill_padded(padded, edge, raw)
+    masks = same_document(lengths, place, micro, tokens, width)
+    grad = act_grad[0] + y_grad[0] * channel[CONV + 2 : CONV + 3, :]
+    grad = grad + dot(projected_grad[0], w_x[...], 1, 1)
+    values = conv[0]
+    sig = lax.logistic(values)
+    grad = grad * (sig * (1.0 + values * (1.0 - sig)))
+
+    @pl.when(micro == 0)
+    def _():
+        x_out[...] = jnp.zeros_like(x_out)
+        rows_out[...] = jnp.zeros_like(rows_out)
+
+    x_out[...] += dot(act[0].astype(BF16), projected_grad[0], 0, 0)
+    total[...] = jnp.zeros_like(total)
+    for tap in range(CONV):
+        span = pl.ds(PAD - (CONV - 1) + tap, tokens)
+        kept = grad * masks[tap]
+        rows_out[tap : tap + 1, :] += jnp.sum(kept * padded[span, :], axis=0, keepdims=True)
+        total[span, :] += channel[tap : tap + 1, :] * kept
+    rows_out[CONV : CONV + 1, :] += jnp.sum(grad, axis=0, keepdims=True)
+    raw_out[0] = total[PAD:, :]
+    head_out[0] = total[PAD - (CONV - 1) : PAD, :]
+
+
+def end_kernel(keep, projected, w_step, channel, act, inject, pre_out, dt_out, out, totals):
+    micro = pl.program_id(1)
+    micros = pl.num_programs(1)
+    tokens, width = act.shape[1], act.shape[2]
+    rates = -jnp.exp(channel[CONV + 3 :, :])
+    pre = dot(projected[0][:, :RANK].astype(BF16), w_step[...], 1, 0)
+    pre = pre + channel[CONV + 1 : CONV + 2, :]
+    step_size = jnp.maximum(pre, 0.0) + jnp.log1p(jnp.exp(-jnp.abs(pre)))
+    pre_out[0] = pre
+    dt_out[0] = step_size
+
+    def block(step, carry):
+        state, alive = carry
         for inner in range(UNROLL):
             t = step * UNROLL + inner
-            d = dt[0, pl.ds(t, 1), :]
+            d = dt_out[0, pl.ds(t, 1), :]
             w = d * act[0, pl.ds(t, 1), :]
-            state = jnp.exp(rates * d) * keep[micro, t] * state + spread(inject[0, t], width) * w
-        return state
-
-    state = lax.fori_loop(0, tokens // UNROLL, block, jnp.zeros((STATES, width), F32))
+            k = keep[micro, t]
+            state = jnp.exp(rates * d) * k * state + spread(inject[0, t], width) * w
+            alive = alive * k
+        return state, alive
+
+    state, alive = lax.fori_loop(
+        0, tokens // UNROLL, block, (jnp.zeros((STATES, width), F32), jnp.float32(1.0))
+    )
     out[...] = state.astype(BF16)
+
+    @pl.when(micro == 0)
+    def _():
+        totals[...] = jnp.zeros_like(totals)
+
+    totals[pl.ds(micro, 1), :] = jnp.sum(step_size, axis=0, keepdims=True)
+    totals[pl.ds(micros + micro, 1), :] = jnp.zeros((1, width), F32) + alive
 
 
 def forward_kernel(
@@ -211,18 +302,100 @@
     return pltpu.CompilerParams(vmem_limit_bytes=48 * 1024 * 1024)
 
 
-def scan_end(keep, dt, act, inject, rate):
-    micros, tokens, inner = dt.shape
-    rows, wide, rated, _, edge, _, _, _, scalars = specs(tokens, 1)
+def convolve(lengths, place, xz, edge, channel, w_x):
+    micros, tokens, inner = xz.shape[0], xz.shape[1], xz.shape[2] // 2
+    scalars = pl.BlockSpec(memory_space=pltpu.SMEM)
+    rows = pl.BlockSpec((1, tokens, LANES), lambda m, g: (m, 0, g))
+    shape = jax.ShapeDtypeStruct((micros, tokens, inner), F32)
+    columns_x = w_x.shape[1]
+    return pl.pallas_call(
+        conv_kernel,
+        grid=(micros, inner // LANES),
+        in_specs=[
+            scalars,
+            scalars,
+            rows,
+            pl.BlockSpec((1, CONV - 1, LANES), lambda m, g: (m, 0, g)),
+            pl.BlockSpec((channel.shape[0], LANES), lambda m, g: (0, g)),
+            pl.BlockSpec((LANES, columns_x), lambda m, g: (g, 0)),
+        ],
+        out_specs=[rows, rows, pl.BlockSpec((1, tokens, columns_x), lambda m, g: (m, 0, 0))],
+        out_shape=[shape, shape, jax.ShapeDtypeStruct((micros, tokens, columns_x), F32)],
+        scratch_shapes=[pltpu.VMEM((PAD + tokens, LANES), F32)],
+        compiler_params=kernel_params(),
+        name="mixer_conv",
+    )(lengths, place, xz, edge, channel, w_x)
+
+
+def convolve_back(
+    lengths, place, xz, edge, channel, w_x, conv, act, act_grad, y_grad, projected_grad
+):
+    micros, tokens, inner = conv.shape
+    scalars = pl.BlockSpec(memory_space=pltpu.SMEM)
+    rows = pl.BlockSpec((1, tokens, LANES), lambda g, m: (m, 0, g))
+    ends = pl.BlockSpec((1, CONV - 1, LANES), lambda g, m: (m, 0, g))
+    columns_x = w_x.shape[1]
+    weight = pl.BlockSpec((LANES, columns_x), lambda g, m: (g, 0))
+    return pl.pallas_call(
+        conv_back_kernel,
+        grid=(inner // LANES, micros),
+        in_specs=[
+            scalars,
+            scalars,
+            rows,
+            ends,
+            pl.BlockSpec((channel.shape[0], LANES), lambda g, m: (0, g)),
+            weight,
+            rows,
+            rows,
+            rows,
+            rows,
+            pl.BlockSpec((1, tokens, columns_x), lambda g, m: (m, 0, 0)),
+        ],
+        out_specs=[rows, ends, weight, pl.BlockSpec((8, LANES), lambda g, m: (0, g))],
+        out_shape=[
+            jax.ShapeDtypeStruct((micros, tokens, inner), F32),
+            jax.ShapeDtypeStruct((micros, CONV - 1, inner), F32),
+            jax.ShapeDtypeStruct((inner, columns_x), F32),
+            jax.ShapeDtypeStruct((8, inner), F32),
+        ],
+        scratch_shapes=[pltpu.VMEM((PAD + tokens, LANES), F32)] * 2,
+        compiler_params=kernel_params(),
+        name="mixer_conv_back",
+    )(lengths, place, xz, edge, channel, w_x, conv, act, act_grad, y_grad, projected_grad)
+
+
+def scan_end(keep, projected, w_step, channel, act, inject):
+    micros, tokens, inner = act.shape
+    rows = pl.BlockSpec((1, tokens, LANES), lambda g, m: (m, 0, g))
+    columns_x = projected.shape[2]
+    shape = jax.ShapeDtypeStruct((micros, tokens, inner), F32)
     return pl.pallas_call(
         end_kernel,
-        grid=(micros, inner // LANES),
-        in_specs=[scalars, rows, rows, wide, rated],
-        out_specs=edge,
-        out_shape=jax.ShapeDtypeStruct((micros * STATES, inner), BF16),
+        grid=(inner // LANES, micros),
+        in_specs=[
+            pl.BlockSpec(memory_space=pltpu.SMEM),
+            pl.BlockSpec((1, tokens, columns_x), lambda g, m: (m, 0, 0)),
+            pl.BlockSpec((RANK, LANES), lambda g, m: (0, g)),
+            pl.BlockSpec((channel.shape[0], LANES), lambda g, m: (0, g)),
+            rows,
+            pl.BlockSpec((1, tokens, STATES, 128), lambda g, m: (m, 0, 0, 0)),
+        ],
+        out_specs=[
+            rows,
+            rows,
+            pl.BlockSpec((STATES, LANES), lambda g, m: (m, g)),
+            pl.BlockSpec((TOTAL_ROWS, LANES), lambda g, m: (0, g)),
+        ],
+        out_shape=[
+            shape,
+            shape,
+            jax.ShapeDtypeStruct((micros * STATES, inner), BF16),
+            jax.ShapeDtypeStruct((TOTAL_ROWS, inner), F32),
+        ],
         compiler_params=kernel_params(),
         name="scan_end",
-    )(keep, dt, act, inject, rate)
+    )(keep, projected, w_step, channel, act, inject)
 
 
 def scan_forward(place, keep, dt, act, inject, readout, rate, ends_all, totals_all):
@@ -292,10 +465,211 @@
     )(place, keep, dt, act, dy, inject, readout, rate, totals_all, starts_all, start, hs, *ahead)
 
 
-def exchange_kernel(groups, gathers, ahead, through, *refs):
+def expert_kernel(taken, w_up, w_down, hidden_out, slope_out, out, total):
+    step = pl.program_id(1)
+    values = dot(taken[0], w_up[0], 1, 0)
+    below = 0.5 + 0.5 * lax.erf(values * math.sqrt(0.5))
+    hidden = (values * below).astype(BF16)
+    density = jnp.exp(-0.5 * values * values) * (1.0 / math.sqrt(2.0 * math.pi))
+    hidden_out[0] = hidden
+    slope_out[0] = below + values * density
+
+    @pl.when(step == 0)
+    def _():
+        total[...] = jnp.zeros_like(total)
+
+    total[...] += dot(hidden, w_down[0], 1, 0)
+
+    @pl.when(step == pl.num_programs(1) - 1)
+    def _():
+        out[0] = total[...].astype(BF16)
+
+
+def expert_back_kernel(
+    taken, grad, w_up, w_down, hidden, slope, up_out, down_out, taken_out, total
+):
+    step = pl.program_id(1)
+    pre_grad = (dot(grad[0], w_down[0], 1, 1) * slope[0]).astype(BF16)
+    down_out[0] = dot(hidden[0], grad[0], 0, 0).astype(BF16)
+    up_out[0] = dot(taken[0], pre_grad, 0, 0).astype(BF16)
+
+    @pl.when(step == 0)
+    def _():
+        total[...] = jnp.zeros_like(total)
+
+    total[...] += dot(pre_grad, w_up[0], 1, 1)
+
+    @pl.when(step == pl.num_programs(1) - 1)
+    def _():
+        taken_out[0] = total[...].astype(BF16)
+
+
+def expert_specs(rows, width):
+    whole = pl.BlockSpec((1, rows, width), lambda e, j: (e, 0, 0))
+    up = pl.BlockSpec((1, width, HIDDEN), lambda e, j: (e, 0, j))
+    down = pl.BlockSpec((1, HIDDEN, width), lambda e, j: (e, j, 0))
+    units = pl.BlockSpec((1, rows, HIDDEN), lambda e, j: (e, 0, j))
+    return whole, up, down, units
+
+
+def run_experts(taken, w_up, w_down):
+    experts, rows, width = taken.shape
+    hidden = w_up.shape[2]
+    whole, up, down, units = expert_specs(rows, width)
+    return pl.pallas_call(
+        expert_kernel,
+        grid=(experts, hidden // HIDDEN),
+        in_specs=[whole, up, down],
+        out_specs=[units, units, whole],
+        out_shape=[
+            jax.ShapeDtypeStruct((experts, rows, hidden), BF16),
+            jax.ShapeDtypeStruct((experts, rows, hidden), F32),
+            jax.ShapeDtypeStruct(taken.shape, BF16),
+        ],
+        scratch_shapes=[pltpu.VMEM((rows, width), F32)],
+        compiler_params=kernel_params(),
+        name="experts",
+    )(taken, w_up, w_down)
+
+
+def run_experts_back(taken, grad, w_up, w_down, hidden, slope):
+    experts, rows, width = taken.shape
+    whole, up, down, units = expert_specs(rows, width)
+    return pl.pallas_call(
+        expert_back_kernel,
+        grid=(experts, hidden.shape[2] // HIDDEN),
+        in_specs=[whole, whole, up, down, units, units],
+        out_specs=[up, down, whole],
+        out_shape=[
+            jax.ShapeDtypeStruct(w_up.shape, BF16),
+            jax.ShapeDtypeStruct(w_down.shape, BF16),
+            jax.ShapeDtypeStruct(taken.shape, BF16),
+        ],
+        scratch_shapes=[pltpu.VMEM((rows, width), F32)],
+        compiler_params=kernel_params(),
+        name="experts_back",
+    )(taken, grad, w_up, w_down, hidden, slope)
+
+
+def head_columns(width):
+    return lax.broadcasted_iota(jnp.int32, (1, width), 1) + pl.program_id(0) * width
+
+
+def head_kernel(limits, rows, table, targets, logits_out, stats, largest, summed, wanted):
+    step = pl.program_id(0)
+    tile = table.shape[1]
+    column = head_columns(tile)
+    logits = dot(rows[...], table[...], 1, 0)
+    logits = jnp.where(column < limits[1], logits, -1e30)
+    logits_out[...] = logits
+    named = targets[...] - limits[0]
+    named = jnp.where(named < limits[1], named, -1)
+
+    @pl.when(step == 0)
+    def _():
+        largest[...] = jnp.full_like(largest, -1e30)
+        summed[...] = jnp.zeros_like(summed)
+        wanted[...] = jnp.zeros_like(wanted)
+
+    parts = [logits[:, first : first + 128] for first in range(0, tile, 128)]
+    before = largest[...]
+    top = functools.reduce(jnp.maximum, parts, before)
+    total = summed[...] * jnp.exp(before - top)
+    found = wanted[...]
+    for index, part in enumerate(parts):
+        total = total + jnp.exp(part - top)
+        spot = column[:, index * 128 : (index + 1) * 128]
+        found = found + jnp.where(spot == named, part, 0.0)
+    largest[...], summed[...], wanted[...] = top, total, found
+
+    @pl.when(step == pl.num_programs(0) - 1)
+    def _():
+        most = jnp.max(top, axis=1, keepdims=True)
+        stats[...] = jnp.zeros_like(stats)
+        stats[:, 0:1] = most
+        stats[:, 1:2] = jnp.sum(total * jnp.exp(top - most), axis=1, keepdims=True)
+        stats[:, 2:3] = jnp.sum(found, axis=1, keepdims=True)
+
+
+def head_back_kernel(
+    limits, rows, table, targets, scalars, logits, table_out, rows_out, total
+):
+    step = pl.program_id(0)
+    column = head_columns(table.shape[1])
+    inside = column < limits[1]
+    probability = jnp.exp(logits[...] - scalars[:, 0:1])
+    hit = jnp.where(column == targets[...] - limits[0], 1.0, 0.0)
+    grad = scalars[:, 1:2] * (probability - hit)
+    grad = jnp.where(inside, grad, 0.0).astype(BF16)
+
+    @pl.when(step == 0)
+    def _():
+        total[...] = jnp.zeros_like(total)
+
+    table_out[...] = dot(rows[...], grad, 1, 0).astype(BF16)
+
+    @pl.when(step < pl.num_programs(0) - 1)
+    def _():
+        total[...] += dot(grad, table[...], 1, 1)
+
+    @pl.when(step == pl.num_programs(0) - 1)
+    def _():
+        weight = jnp.where(inside, table[...].astype(F32), 0.0).astype(BF16)
+        rows_out[...] = (total[...] + dot(grad, weight, 1, 1)).astype(BF16)
+
+
+def head_specs(rows, table):
+    count, width = rows.shape
+    tile = 1280 if count <= 512 else 640
+    whole = pl.BlockSpec((count, width), lambda j: (0, 0))
+    part = pl.BlockSpec((width, tile), lambda j: (0, j))
+    column = pl.BlockSpec((count, 1), lambda j: (0, 0))
+    few = pl.BlockSpec((count, 8), lambda j: (0, 0))
+    logits = pl.BlockSpec((count, tile), lambda j: (0, j))
+    return whole, part, column, few, logits, (-(-table.shape[1] // tile),)
+
+
+def head(limits, rows, table, targets):
+    whole, part, column, few, logits, grid = head_specs(rows, table)
+    return pl.pallas_call(
+        head_kernel,
+        grid=grid,
+        in_specs=[pl.BlockSpec(memory_space=pltpu.SMEM), whole, part, column],
+        out_specs=[logits, few],
+        out_shape=[
+            jax.ShapeDtypeStruct((rows.shape[0], table.shape[1]), F32),
+            jax.ShapeDtypeStruct((rows.shape[0], 8), F32),
+        ],
+        scratch_shapes=[pltpu.VMEM((rows.shape[0], 128), F32)] * 3,
+        compiler_params=kernel_params(),
+        name="head",
+    )(limits, rows, table, targets)
+
+
+def head_back(limits, rows, table, targets, scalars, logits):
+    whole, part, column, few, logit, grid = head_specs(rows, table)
+    turned = pl.BlockSpec((rows.shape[1], rows.shape[0]), lambda j: (0, 0))
+    return pl.pallas_call(
+        head_back_kernel,
+        grid=grid,
+        in_specs=[
+            pl.BlockSpec(memory_space=pltpu.SMEM), turned, part, column, few, logit,
+        ],
+        out_specs=[part, whole],
+        out_shape=[
+            jax.ShapeDtypeStruct(table.shape, BF16),
+            jax.ShapeDtypeStruct(rows.shape, BF16),
+        ],
+        scratch_shapes=[pltpu.VMEM(rows.shape, F32)],
+        compiler_params=kernel_params(),
+        name="head_back",
+    )(limits, rows.T, table, targets, scalars, logits)
+
+
+def exchange_kernel(groups, gathers, ahead, *refs):
     arrays = len(groups)
     inputs, outputs = refs[:arrays], refs[arrays + ahead : 2 * arrays + ahead]
-    sends, receives, own_sem = refs[2 * arrays + ahead + through :]
+    sends, receives, own_sem = refs[2 * arrays + ahead :]
 
     def place_of(axes):
         if len(axes) == 1:
@@ -362,30 +736,21 @@
         lax.fori_loop(1, peers, end, 0)
 
 
-def exchange(
-    values, gathers, identity, axes=("seq",), space=pltpu.VMEM, ahead=(), riders=(), through=()
-):
-    groups = [axes] * len(values) + [("mat",)] * len(riders)
-    gathers = list(gathers) + [False] * len(riders)
+def exchange(values, gathers, identity, axes=("seq",), space=pltpu.VMEM, ahead=()):
+    groups = [axes] * len(values)
     peers = [math.prod(lax.axis_size(axis) for axis in group) for group in groups]
     place = pl.BlockSpec(memory_space=space)
     unread = pl.BlockSpec(memory_space=pl.ANY)
-    places = [place] * len(values) + [unread] * len(riders)
-    values = list(values) + list(riders)
     shapes = [
         jax.ShapeDtypeStruct(((count,) if gather else ()) + value.shape, value.dtype)
         for value, gather, count in zip(values, gathers, peers)
     ]
     arrays = len(values)
-    ahead = list(ahead) + list(through)
-    first = arrays + len(ahead) - len(through)
-    shapes += [jax.ShapeDtypeStruct(value.shape, value.dtype) for value in through]
     return pl.pallas_call(
-        functools.partial(exchange_kernel, tuple(groups), tuple(gathers), len(ahead), len(through)),
+        functools.partial(exchange_kernel, tuple(groups), tuple(gathers), len(ahead)),
         out_shape=shapes,
-        in_specs=places + [unread] * len(ahead),
-        out_specs=places + [unread] * len(through),
-        input_output_aliases={first + index: arrays + index for index in range(len(through))},
+        in_specs=[place] * arrays + [unread] * len(ahead),
+        out_specs=[place] * arrays,
         scratch_shapes=[
             pltpu.SemaphoreType.DMA((arrays, max(peers))),
             pltpu.SemaphoreType.DMA((arrays, max(peers))),
@@ -401,11 +766,11 @@
     return pl.pallas_call(
         lambda *refs: None,
         out_shape=[jax.ShapeDtypeStruct(value.shape, value.dtype) for value in values],
-        in_specs=[unread] * (len(values) + 1),
+        in_specs=[unread] * (len(values) + len(ahead)),
         out_specs=[unread] * len(values),
         input_output_aliases={index: index for index in range(len(values))},
         name="hold",
-    )(*values, ahead)
+    )(*values, *ahead)
 
 
 class Line:
@@ -492,15 +857,17 @@
         for index, piece in self.pieces():
             self.copy(2, index, outer, piece, self.across(outer)).wait_recv()
 
-    def each(self, lap, use):
+    def each(self, lap, use, partners=None):
         for way in range(2):
             outer = self.outer + (-lap, lap)[way]
 
             @pl.when(jnp.logical_and(outer >= 0, outer < self.outers))
             def _():
-                use(self.block(outer))
-                self.take(outer)
-                use(self.across(outer))
+                if partners is not True:
+                    use(self.block(outer))
+                if partners is not False:
+                    self.take(outer)
+                    use(self.across(outer))
 
     def end(self):
         def one(outer, _):
@@ -661,6 +1028,116 @@
     return gathered + relayed
 
 
+def reduce_kernel(arrays, *refs):
+    inputs, outputs = refs[:arrays], refs[arrays : 2 * arrays]
+    got, keep = refs[2 * arrays : 3 * arrays], refs[3 * arrays : 4 * arrays]
+    passes, arrivals, sends, receives = refs[4 * arrays :]
+    outers = lax.axis_size("seq") // 2
+    me = lax.axis_index("seq")
+    outer, inner = me // 2, me % 2
+    partner = {"seq": outer * 2 + 1 - inner}
+
+    def hand(index, place):
+        return pltpu.make_async_remote_copy(
+            src_ref=inputs[index].at[place * 2 + 1 - inner],
+            dst_ref=got[index].at[place],
+            send_sem=passes.at[index, place],
+            recv_sem=arrivals.at[index, place],
+            device_id=partner,
+            device_id_type=MESH,
+        )
+
+    def send(index, place, origin):
+        return pltpu.make_async_remote_copy(
+            src_ref=keep[index].at[place],
+            dst_ref=outputs[index].at[origin],
+            send_sem=sends.at[index, place],
+            recv_sem=receives.at[index, origin],
+            device_id={"seq": place * 2 + inner},
+            device_id_type=MESH,
+        )
+
+    barrier = pltpu.get_barrier_semaphore()
+
+    def greet(lap, _):
+        pl.semaphore_signal(
+            barrier,
+            inc=1,
+            device_id={"seq": ((outer + lap) % outers) * 2 + inner},
+            device_id_type=MESH,
+        )
+        return 0
+
+    pl.semaphore_signal(barrier, inc=1, device_id=partner, device_id_type=MESH)
+    lax.fori_loop(1, outers, greet, 0)
+    pl.semaphore_wait(barrier, outers)
+
+    def begin(lap, _):
+        for index in range(arrays):
+            hand(index, (outer + 1 + lap) % outers).start()
+        return 0
+
+    lax.fori_loop(0, outers, begin, 0)
+
+    def add(lap, _):
+        place = (outer + 1 + lap) % outers
+        for index in range(arrays):
+            hand(index, place).wait_recv()
+            total = inputs[index][place * 2 + inner].astype(F32) + got[index][place].astype(F32)
+            keep[index][place] = total.astype(BF16)
+
+            @pl.when(place != outer)
+            def _():
+                send(index, place, outer).start()
+
+            @pl.when(place == outer)
+            def _():
+                outputs[index][outer] = total.astype(BF16)
+
+        return 0
+
+    lax.fori_loop(0, outers, add, 0)
+
+    def end(lap, _):
+        place = (outer + lap) % outers
+        for index in range(arrays):
+            hand(index, place).wait_send()
+
+            @pl.when(place != outer)
+            def _():
+                send(index, place, place).wait_recv()
+                send(index, place, outer).wait_send()
+
+        return 0
+
+    lax.fori_loop(0, outers, end, 0)
+
+
+def reduce_seq(values, identity, ahead=()):
+    outers = lax.axis_size("seq") // 2
+    arrays = len(values)
+    shapes = [(outers,) + value.shape[1:] for value in values]
+    place = pl.BlockSpec(memory_space=pltpu.VMEM)
+    unread = pl.BlockSpec(memory_space=pl.ANY)
+
+    def body(*refs):
+        reduce_kernel(arrays, *refs[:arrays], *refs[arrays + len(ahead) :])
+
+    results = pl.pallas_call(
+        body,
+        out_shape=[jax.ShapeDtypeStruct(shape, BF16) for shape in shapes],
+        in_specs=[place] * arrays + [unread] * len(ahead),
+        out_specs=[place] * arrays,
+        scratch_shapes=[pltpu.VMEM(shape, BF16) for shape in shapes * 2]
+        + [pltpu.SemaphoreType.DMA((arrays, outers))] * 4,
+        compiler_params=pltpu.CompilerParams(
+            collective_id=identity, has_side_effects=True, vmem_limit_bytes=48 * 1024 * 1024
+        ),
+        name="reduce_seq",
+    )(*values, *ahead)
+    return [jnp.sum(result.astype(F32), axis=0) for result in results]
+
+
 def lookup_kernel(
     ids, table, small, out, smalls, found, give, got, keep, taken, passes, arrivals, sends,
     receives, small_sends, small_receives, small_own,
@@ -850,10 +1327,10 @@
 
 
 def scatter_rows_kernel(
-    entries, ids, rows, others, first_rider, second_rider, out, squares, whole, buffer, *rest
+    entries, ids, rows, others, first_rider, second_rider, out, squares, whole, buffer, near, *rest
 ):
     line = Line([rows], [buffer], rest[: Line.SEMAPHORES])
-    rider_sends, rider_receives, rider_own = rest[Line.SEMAPHORES :]
+    rider_sends, rider_receives, rider_own, near_own = rest[Line.SEMAPHORES :]
     places = lax.axis_size("mat")
     here = lax.axis_index("mat")
     riders = ((first_rider, UP_PLACE), (second_rider, DOWN_PLACE))
@@ -875,6 +1352,12 @@
 
     mats = rows.shape[0]
     lanes = lax.broadcasted_iota(jnp.int32, (128, 128), 1)
+    nears = [
+        pltpu.make_async_copy(source, near.at[rider], near_own.at[rider])
+        for rider, (source, _) in enumerate(riders)
+    ]
+    for copy in nears:
+        copy.start()
 
     def add(block, source):
         parts = []
@@ -915,7 +1398,6 @@
         return _
 
     lax.fori_loop(1, places, greet_mat, 0)
-    out[...] = jnp.zeros_like(out)
     pl.semaphore_wait(barrier, greeted + places - 1)
     line.begin()
     for rider, (_, place) in enumerate(riders):
@@ -931,7 +1413,31 @@
     def use(block):
         add(block, buffer.at[block])
 
+    part = others.shape[0]
+
+    def fill(index, _):
+        cut = pl.ds(pl.multiple_of(index * VOCAB_TILE, VOCAB_TILE), VOCAB_TILE)
+        more = others[:, cut].astype(F32).T
+        out[cut, :] = jnp.concatenate(
+            [more, jnp.zeros((VOCAB_TILE, 256 - part), F32)], axis=1
+        )
+        return 0
+
+    lax.fori_loop(0, out.shape[0] // VOCAB_TILE, fill, 0)
     add(line.block(line.outer), rows)
+
+    def square(index, total):
+        cut = pl.ds(pl.multiple_of(index * 64, 64), 64)
+        for rider in range(len(riders)):
+            values = near[rider, cut, :].astype(F32)
+            values = jnp.sum(values * values, axis=0, keepdims=True)
+            for lane in range(0, values.shape[1], 256):
+                total = total + values[:, lane : lane + 256]
+        return total
+
+    for copy in nears:
+        copy.wait()
+    total = lax.fori_loop(0, near.shape[1] // 64, square, jnp.zeros((1, 256), F32))
 
     def step(lap, _):
         line.forward(lap)
@@ -963,19 +1469,14 @@
                 if origin != place:
                     ride(rider, origin).wait_recv()
 
-    part = others.shape[0]
-
     def finish(index, total):
         cut = pl.ds(pl.multiple_of(index * VOCAB_TILE, VOCAB_TILE), VOCAB_TILE)
-        more = others[:, cut].astype(F32).T
-        more = jnp.concatenate([more, jnp.zeros((VOCAB_TILE, 256 - part), F32)], axis=1)
-        values = out[cut, :] + more
-        out[cut, :] = values
+        values = out[cut, :]
         entry = lax.broadcasted_iota(jnp.int32, values.shape, 0) + index * VOCAB_TILE
         values = jnp.where(entry < entries, values, 0.0)
         return total + jnp.sum(values * values, axis=0, keepdims=True)
 
-    total = lax.fori_loop(0, out.shape[0] // VOCAB_TILE, finish, jnp.zeros((1, 256), F32))
+    total = lax.fori_loop(0, out.shape[0] // VOCAB_TILE, finish, total)
     squares[...] = jnp.broadcast_to(total, (8, 256))
 
 
@@ -996,10 +1497,12 @@
         out_specs=[place, place, unread],
         scratch_shapes=[
             pltpu.VMEM((peers,) + rows.shape, BF16),
+            pltpu.VMEM((2,) + riders[0].shape, BF16),
             *line_semaphores([rows]),
             pltpu.SemaphoreType.DMA((2,)),
             pltpu.SemaphoreType.DMA((mats,)),
             pltpu.SemaphoreType.DMA,
+            pltpu.SemaphoreType.DMA((2,)),
         ],
         compiler_params=pltpu.CompilerParams(
             collective_id=identity, has_side_effects=True, vmem_limit_bytes=48 * 1024 * 1024
@@ -1061,7 +1564,7 @@
     return stacked.transpose(1, 0, 2).reshape(rows, count * width)
 
 
-def step_grads(weights, moments, embedded, route, lengths, slots, weight_mask, targets, loss_all):
+def step_grads(weights, embedded, route, lengths, slots, weight_mask, targets, loss_all):
     table, w_in, w_out, w_up, w_down, w_x, w_step, w_route, chan_low, gains_low = weights
     channel = chan_low.astype(F32)
     gains = gains_low.astype(F32)
@@ -1069,21 +1572,15 @@
     count = lax.axis_size("seq")
     micros, tokens = route.shape
     inner = w_in.shape[1] // 2
-    vocab_part = table.shape[0]
+    vocab_part = table.shape[1]
     first_pos = me * tokens
     vocab_start = me * vocab_part
-    ext_pos = first_pos - (CONV - 1) + jnp.arange(tokens + CONV - 1, dtype=jnp.int32)
     bounds = jnp.cumsum(lengths, axis=1)
-    ext_doc = jnp.sum((ext_pos[None, :, None] >= bounds[:, None, :-1]).astype(jnp.int32), axis=2)
-    ext_doc = jnp.where(ext_pos[None] >= 0, ext_doc, -1)
-    starts = jnp.concatenate([jnp.zeros((micros, 1), jnp.int32), bounds[:, :-1]], axis=1)
-    keeping = 1.0 - jnp.any(
-        ext_pos[None, CONV - 1 :, None] == starts[:, None, :], axis=2
+    position = first_pos + jnp.arange(tokens, dtype=jnp.int32)
+    opening = position[None, :, None] == bounds[:, None, :-1]
+    keeping = 1.0 - jnp.logical_or(
+        jnp.any(opening, axis=2), position[None] == 0
     ).astype(F32)
-    own_doc = ext_doc[:, CONV - 1 :]
-    same = [
-        (ext_doc[:, tap : tap + tokens] == own_doc).astype(F32)[:, :, None] for tap in range(CONV)
-    ]
     place = me.astype(jnp.int32).reshape(1)
 
     x0 = embedded.astype(F32)
@@ -1091,33 +1588,17 @@
     u, hat0, scale0 = normalize(x0, gains[0])
     u_low = u.astype(BF16)
     xz = dot(u_low, w_in, 1, 0).reshape(micros, tokens, 2 * inner)
-    raw, z = xz[:, :, :inner], xz[:, :, inner:]
-    edge = move_rows(raw[:, tokens - (CONV - 1) :], 1)
-    padded = jnp.concatenate([edge, raw], axis=1)
-    conv = channel[CONV] + jnp.zeros((micros, tokens, inner), F32)
-    for tap in range(CONV):
-        conv = conv + channel[tap] * padded[:, tap : tap + tokens] * same[tap]
-    act = jax.nn.silu(conv)
-    act_low = act.reshape(-1, inner).astype(BF16)
-    projected = dot(act_low, w_x, 1, 0)
-    rank_low = projected[:, :RANK].astype(BF16)
-    pre = dot(rank_low, w_step, 1, 0).reshape(micros, tokens, inner) + channel[CONV + 1]
-    dt = jax.nn.softplus(pre)
+    z = xz[:, :, inner:]
+    edge = move_rows(xz[:, tokens - (CONV - 1) :, :inner], 1)
+    conv, act, projected = convolve(lengths, place, xz, edge, channel, w_x)
+    rank_low = projected[:, :, :RANK].reshape(-1, RANK).astype(BF16)
     rate = -jnp.exp(channel[CONV + 3 :])
-    wide = projected.reshape(micros, tokens, -1)[:, :, :, None]
+    wide = projected[:, :, :, None]
     wide_shape = (micros, tokens, STATES, 128)
     inject = jnp.broadcast_to(wide[:, :, RANK : RANK + STATES], wide_shape)
     readout = jnp.broadcast_to(wide[:, :, RANK + STATES :], wide_shape)
-    totals = jnp.concatenate(
-        [
-            jnp.sum(dt, axis=1),
-            jnp.broadcast_to(jnp.prod(keeping, axis=1)[:, None], (micros, inner)),
-            jnp.zeros((TOTAL_ROWS - 2 * micros, inner), F32),
-        ]
-    )
-    ends_all, totals_all = gather_seq(
-        [scan_end(keeping, dt, act, inject, rate), totals], 1
-    )
+    pre, dt, ends, totals = scan_end(keeping, projected, w_step, channel, act, inject)
+    ends_all, totals_all = gather_seq([ends, totals], 1)
     y, hs, start = scan_forward(
         place, keeping, dt, act, inject, readout, rate, ends_all, totals_all
     )
@@ -1143,36 +1624,24 @@
         placed[:, None, :] == jnp.arange(all_slots, dtype=jnp.int32)[None, :, None]
     ).astype(BF16)
 
-    moved = []
-
-    def swap_seq(value, identity, ahead=(), riders=(), through=()):
-        result = exchange(
-            [value], [False], identity, ahead=ahead, riders=riders, through=through
-        )
-        moved.extend(result[1:])
-        return result[0]
-
-    def to_experts(rows, identity, ahead=(), riders=()):
+    def to_experts(rows, identity, ahead=()):
         sent = jnp.einsum(
             "mst,mtd->msd", sender, rows.reshape(micros, tokens, D), preferred_element_type=F32
         ).astype(BF16)
         sent = sent.reshape(micros, count, -1, D).transpose(1, 0, 2, 3).reshape(count, -1, D)
-        arrived = swap_seq(sent, identity, ahead, riders).reshape(count, micros, local_experts, capacity, D)
+        arrived = swap_seq(sent, identity, ahead).reshape(count, micros, local_experts, capacity, D)
         return arrived.transpose(2, 0, 1, 3, 4).reshape(local_experts, -1, D)
 
-    def from_experts(rows, identity, ahead=(), riders=(), through=()):
+    def from_experts(rows, identity, ahead=()):
         rows = rows.reshape(local_experts, count, micros, capacity, D).transpose(1, 2, 0, 3, 4)
-        back = swap_seq(rows.reshape(count, -1, D), identity, ahead, riders, through)
+        back = swap_seq(rows.reshape(count, -1, D), identity, ahead)
         back = back.reshape(count, micros, -1, D)
         back = back.transpose(1, 0, 2, 3).reshape(micros, all_slots, D)
         return jnp.einsum("mst,msd->mtd", sender, back, preferred_element_type=F32).reshape(-1, D)
 
-    taken = to_experts(s_low, 2, (), [moments[0]])
-    hidden_pre = jnp.einsum("erk,ekn->ern", taken, w_up, preferred_element_type=F32)
-    gelu = functools.partial(jax.nn.gelu, approximate=False)
-    hidden_low = gelu(hidden_pre).astype(BF16)
-    result = jnp.einsum("erk,ekn->ern", hidden_low, w_down, preferred_element_type=F32)
-    combined = from_experts(result.astype(BF16), 3, (), [moments[1]])
+    taken = to_experts(s_low, 2)
+    hidden, slope, result = run_experts(taken, w_up, w_down)
+    combined = from_experts(result, 3)
     x2 = x1 + gate[:, None] * combined
 
     final, hat2, scale2 = normalize(x2, gains[2])
@@ -1194,17 +1663,11 @@
 
     targets = by_device(targets)
     counted = by_device(weight_mask).astype(F32)
-    logits = dot(rows, table, 1, 1)
-    column = vocab_start + jnp.arange(vocab_part, dtype=jnp.int32)
-    valid = column < VOCAB_REAL
-    masked = jnp.where(valid[None, :], logits, -1e30)
-    largest = jnp.max(masked, axis=1)
-    expsum = jnp.sum(jnp.exp(masked - largest[:, None]), axis=1)
-    hitting = column[None, :] == targets[:, None]
-    target_logit = jnp.sum(jnp.where(hitting, logits, 0.0), axis=1)
-    stats = exchange(
-        [jnp.stack([largest, expsum, target_logit] + [jnp.zeros_like(largest)] * 5)], [True], 5
-    )[0]
+    limits = jnp.stack(
+        [vocab_start, jnp.minimum(VOCAB_REAL - vocab_start, vocab_part), vocab_part]
+    ).astype(jnp.int32)
+    logits, stats = head(limits, rows, table, targets[:, None])
+    stats = exchange([stats.T], [True], 5)[0]
     top = jnp.max(stats[:, 0], axis=0)
     lse = top + jnp.log(jnp.sum(stats[:, 1] * jnp.exp(stats[:, 0] - top[None]), axis=0))
     unweighted = lse - jnp.sum(stats[:, 2], axis=0)
@@ -1218,15 +1681,10 @@
     counted_here = own(counted)
     loss_here = jnp.sum(rows_here * counted_here)
     count_here = jnp.sum(counted_here)
-    probability = jnp.where(valid[None, :], jnp.exp(masked - lse[:, None]), 0.0)
-    logit_grad = (
-        (counted / loss_all)[:, None] * (probability - hitting.astype(F32))
-    ).astype(BF16)
-    rows_grad = swap_seq(
-        dot(logit_grad, table, 1, 0).astype(BF16).reshape(count, -1, D), 6, (), [moments[2]]
-    )
-    rows_grad = jnp.sum(rows_grad.astype(F32), axis=0).reshape(micros, own_count, D)
-    table_grad = dot(rows, logit_grad, 0, 0).astype(BF16)
+    scalars = jnp.pad(jnp.stack([lse, counted / loss_all], axis=1), ((0, 0), (0, 6)))
+    table_grad, rows_grad = head_back(limits, rows, table, targets[:, None], scalars, logits)
+    rows_grad = rows_grad.reshape(count, -1, D)
+    rows_grad = reduce_seq([rows_grad], 6)[0].reshape(micros, own_count, D)
     final_grad = jnp.einsum(
         "mst,msd->mtd",
         select.astype(F32),
@@ -1238,17 +1696,11 @@
 
     gate_grad = jnp.sum(x2_grad * combined, axis=1)
     out_grad = to_experts((gate[:, None] * x2_grad).astype(BF16), 7, [table_grad])
-    hidden_grad = jnp.einsum("ern,ekn->erk", out_grad, w_down, preferred_element_type=F32)
-    down_grad = jnp.einsum("erk,ern->ekn", hidden_low, out_grad, preferred_element_type=F32)
-    _, gelu_back = jax.vjp(gelu, hidden_pre)
-    pre_grad = gelu_back(hidden_grad)[0].astype(BF16)
-    up_grad = jnp.einsum("erk,ern->ekn", taken, pre_grad, preferred_element_type=F32)
-    taken_grad = jnp.einsum("ern,ekn->erk", pre_grad, w_up, preferred_element_type=F32)
+    up_grad, down_grad, taken_grad = run_experts_back(
+        taken, out_grad, w_up, w_down, hidden, slope
+    )
     s_table = scatter_mat(table_grad, 0)
-    up_grad, down_grad = hold([up_grad.astype(BF16), down_grad.astype(BF16)], s_table)
-    s_grad = from_experts(taken_grad.astype(BF16), 8, [up_grad, down_grad])
-    s_up = scatter_mat(up_grad, 2)
-    s_down = scatter_mat(down_grad, 1)
+    s_grad = from_experts(taken_grad, 8, [table_grad])
     score_grad = jnp.where(chosen, (gate_grad * gate * (1.0 - gate))[:, None], 0.0).astype(BF16)
     route_grad = dot(s_low, score_grad, 0, 0)
     s_grad = s_grad + dot(score_grad, w_route, 1, 1)
@@ -1256,6 +1708,9 @@
     x1_grad = x2_grad + more
 
     x1_grad_low = x1_grad.astype(BF16)
+    up_grad, down_grad = hold([up_grad, down_grad], [s_table, x1_grad_low])
+    s_up = scatter_mat(up_grad, 2)
+    s_down = scatter_mat(down_grad, 1)
     mixed_grad = dot(x1_grad_low, w_out, 1, 1).reshape(micros, tokens, inner)
     out_weight_grad = dot(mixed_low, x1_grad_low, 0, 0)
     y_grad = mixed_grad * z_silu
@@ -1263,14 +1718,13 @@
     out_weight_grad = out_weight_grad.astype(BF16)
     s_out = scatter_mat(out_weight_grad, 0)
     starts_all = gather_seq(
-        [scan_start(keeping, dt, y_grad, readout, rate, [out_weight_grad])], 9
+        [scan_start(keeping, dt, y_grad, readout, rate, [out_weight_grad, up_grad, down_grad])], 9
     )[0]
     dt_grad, act_grad, inject_grad, readout_grad, rate_grad = scan_backward(
         place, keeping, dt, act, y_grad, inject, readout, rate, totals_all, starts_all, start, hs,
         [],
     )
     skip_grad = jnp.sum(y_grad * act, axis=(0, 1))
-    act_grad = act_grad + y_grad * skip
     pre_dt = dt_grad * jax.nn.sigmoid(pre)
     pre_dt_low = pre_dt.reshape(-1, inner).astype(BF16)
     step_weight_grad = dot(rank_low, pre_dt_low, 0, 0)
@@ -1282,24 +1736,21 @@
         ],
         axis=1,
     ).astype(BF16)
-    x_weight_grad = dot(act_low, projected_grad, 0, 0)
-    act_grad = act_grad + dot(projected_grad, w_x, 1, 1).reshape(micros, tokens, inner)
-    conv_grad = act_grad * silu_back(conv)
-    chan_rows = [
-        jnp.sum(conv_grad * padded[:, tap : tap + tokens] * same[tap], axis=(0, 1))
-        for tap in range(CONV)
-    ]
-    chan_rows += [jnp.sum(conv_grad, axis=(0, 1)), jnp.sum(pre_dt, axis=(0, 1)), skip_grad]
+    raw_grad, head_grad, x_weight_grad, conv_rows = convolve_back(
+        lengths, place, xz, edge, channel, w_x, conv, act, act_grad, y_grad,
+        projected_grad.reshape(micros, tokens, -1),
+    )
     chan_grad = jnp.concatenate(
-        [jnp.stack(chan_rows), jnp.sum(rate_grad, axis=0) * rate], axis=0
-    )
-    padded_grad = jnp.zeros((micros, tokens + CONV - 1, inner), F32)
-    for tap in range(CONV):
-        padded_grad = padded_grad + jnp.pad(
-            channel[tap] * conv_grad * same[tap], ((0, 0), (tap, CONV - 1 - tap), (0, 0))
-        )
-    edge_grad = move_rows(padded_grad[:, : CONV - 1], -1)
-    raw_grad = padded_grad[:, CONV - 1 :] + jnp.pad(
+        [
+            conv_rows[: CONV + 1],
+            jnp.sum(pre_dt, axis=(0, 1))[None],
+            skip_grad[None],
+            jnp.sum(rate_grad, axis=0) * rate,
+        ],
+        axis=0,
+    )
+    edge_grad = move_rows(head_grad, -1)
+    raw_grad = raw_grad + jnp.pad(
         edge_grad, ((0, 0), (tokens - (CONV - 1), 0), (0, 0))
     )
     xz_grad = jnp.concatenate([raw_grad, z_grad], axis=2).reshape(-1, 2 * inner).astype(BF16)
@@ -1318,7 +1769,7 @@
         chan_grad,
         jnp.stack([gain_zero, gain_one, gain_two]),
     )
-    return grads, moved, x0_grad, loss_here, count_here, rows_here
+    return grads, x0_grad, loss_here, count_here, rows_here
 
 
 def scatter_mat(grad, dim):
@@ -1326,115 +1777,139 @@
 
 
 def ortho_kernel(
-    place, scale, moment_a, moment_b, moment_c, experts, inward, outward, out,
-    current, rounded, gram, low, poly, slope, trace,
+    place, scale, moments, experts, inward, outward, out,
+    moment, grads, current, rounded, gram, low, poly, slope, trace, semaphores,
 ):
     blocks, size, _ = experts.shape
     tile = TILE
     tiles = size // tile
-    cuts = size // CUT
-    row = lax.broadcasted_iota(jnp.int32, (tile, size), 0)
-    column = lax.broadcasted_iota(jnp.int32, (tile, size), 1)
+    eye = lax.broadcasted_iota(jnp.int32, (tile, tile), 0) == lax.broadcasted_iota(
+        jnp.int32, (tile, tile), 1
+    )
     turned = jnp.logical_or(place[0] == DOWN_PLACE, place[0] == OUT_PLACE)
 
     def band(index):
-        return pl.ds(pl.multiple_of(index * tile, tile), tile)
-
-    def load(block, index, moment, grad, turn):
-        values = MOMENTUM * moment.astype(F32) + scale[0] * grad.astype(F32)
+        return pl.ds(index * tile, tile)
+
+    fetch = pltpu.make_async_copy(moments, moment, semaphores.at[0])
+    fetch.start()
+
+    @pl.when(jnp.logical_or(place[0] == UP_PLACE, place[0] == DOWN_PLACE))
+    def _():
+        copy = pltpu.make_async_copy(experts, grads, semaphores.at[1])
+        copy.start()
+        copy.wait()
+
+    @pl.when(place[0] == IN_PLACE)
+    def _():
+        copy = pltpu.make_async_copy(inward, grads, semaphores.at[1])
+        copy.start()
+        copy.wait()
+
+    @pl.when(place[0] == OUT_PLACE)
+    def _():
+        rows = outward.shape[1]
+        grads[:, rows:, :] = jnp.zeros((blocks, size - rows, size), BF16)
+        copies = [
+            pltpu.make_async_copy(
+                outward.at[block], grads.at[block, pl.ds(0, rows)], semaphores.at[1 + block]
+            )
+            for block in range(blocks)
+        ]
+        for copy in copies:
+            copy.start()
+        for copy in copies:
+            copy.wait()
+
+    fetch.wait()
+    trace[...] = jnp.zeros_like(trace)
+
+    def load(lap, _):
+        block, index = lap // tiles, lap % tiles
+        rows = pl.ds(pl.multiple_of(index * tile, tile), tile)
+        values = MOMENTUM * moment[block, rows, :].astype(F32)
+        values = values + scale[0] * grads[block, rows, :].astype(F32)
         values = values.astype(BF16).astype(F32)
         trace[...] += jnp.sum(values * values, axis=0, keepdims=True)
-        if turn:
-            values = values.T
-            current[block, :, pl.ds(index * CUT, CUT)] = values
-            rounded[0, block, :, pl.ds(index * CUT, CUT)] = values.astype(BF16)
-        else:
-            current[block, pl.ds(index * CUT, CUT), :] = values
-            rounded[0, block, pl.ds(index * CUT, CUT), :] = values.astype(BF16)
-
-    moments = (moment_a, moment_b, moment_c)
-    trace[...] = jnp.zeros_like(trace)
-
-    def load_block(block, _):
-        for index in range(cuts):
-            rows = pl.ds(index * CUT, CUT)
-
-            @pl.when(place[0] == UP_PLACE)
-            def _():
-                load(block, index, moments[index][block], experts[block, rows, :], False)
-
-            @pl.when(place[0] == DOWN_PLACE)
-            def _():
-                load(block, index, moments[index][block], experts[block, rows, :], True)
-
-            @pl.when(place[0] == IN_PLACE)
-            def _():
-                load(block, index, moments[index][block], inward[block, rows, :], False)
-
-            @pl.when(place[0] == OUT_PLACE)
-            def _():
-                room = outward.shape[1] - index * CUT
-                if room >= CUT:
-                    grad = outward[block, rows, :].astype(F32)
-                elif room > 0:
-                    grad = outward[block, pl.ds(index * CUT, room), :].astype(F32)
-                    grad = jnp.concatenate([grad, jnp.zeros((CUT - room, size), F32)], axis=0)
-                else:
-                    grad = jnp.zeros((CUT, size), F32)
-                load(block, index, moments[index][block], grad, True)
+
+        @pl.when(turned)
+        def _():
+            flipped = values.T
+            current[block, :, rows] = flipped
+            rounded[0, block, :, rows] = flipped.astype(BF16)
+
+        @pl.when(jnp.logical_not(turned))
+        def _():
+            current[block, rows, :] = values
+            rounded[0, block, rows, :] = values.astype(BF16)
 
         return 0
 
-    lax.fori_loop(0, blocks, load_block, 0)
+    lax.fori_loop(0, blocks * tiles, load, 0)
     total = jnp.sum(trace[...])
     factor = 1.0 / (jnp.sqrt(total + jnp.zeros((8, 128), F32)) + 1e-07)[0:1, 0:1]
 
     def sweep(step, gain):
         now = step % 2
 
-        def make_gram(index, diagonal):
-            total = jnp.zeros((tile, size), F32)
+        diagonal = []
+        for index in range(tiles):
+            total = jnp.zeros((tile, size - index * tile), F32)
             for block in range(blocks):
                 total = total + dot(
-                    rounded[now, block, band(index), :], rounded[now, block], 1, 1
+                    rounded[now, block, band(index), :],
+                    rounded[now, block, index * tile :, :],
+                    1,
+                    1,
                 )
             total = total * gain
-            mask = column == row + index * tile
-            gram[band(index), :] = total
-            low[band(index), :] = jnp.where(mask, 0.0, total).astype(BF16)
-            return diagonal + jnp.sum(jnp.where(mask, total, 0.0), axis=0, keepdims=True)
-
-        diagonal = lax.fori_loop(0, tiles, make_gram, jnp.zeros((1, size), F32))
-
-        def make_poly(index, _):
-            mask = column == row + index * tile
-            values = gram[band(index), :]
-            own = jnp.sum(jnp.where(mask, values, 0.0), axis=1, keepdims=True)
-            rest = jnp.where(mask, own * own, (own + diagonal) * values)
-            total = COEF_B * values + COEF_C * (dot(low[band(index), :], low[...], 1, 0) + rest)
-            poly[band(index), :] = jnp.where(mask, 0.0, total).astype(BF16)
-            part = jnp.sum(jnp.where(mask, total, 0.0), axis=1, keepdims=True)
+            corner = total[:, :tile]
+            own = jnp.where(eye, corner, 0.0)
+            diagonal.append(jnp.sum(own, axis=0, keepdims=True))
+            slope[band(index), :] = jnp.broadcast_to(
+                jnp.sum(own, axis=1, keepdims=True), (tile, 128)
+            )
+            gram[band(index), index * tile :] = total
+            low[band(index), band(index)] = (corner - own).astype(BF16)
+            for other in range(index + 1, tiles):
+                part = total[:, (other - index) * tile : (other - index + 1) * tile]
+                flipped = part.T
+                low[band(index), band(other)] = part.astype(BF16)
+                gram[band(other), band(index)] = flipped
+                low[band(other), band(index)] = flipped.astype(BF16)
+
+        for index in range(tiles):
+            product = dot(low[band(index), :], low[...], 1, 0)
+            own = spread(slope[band(index), :], tile)
+            for other in range(tiles):
+                values = gram[band(index), band(other)]
+                sums = own + diagonal[other]
+                total = (COEF_B + COEF_C * sums) * values
+                total = total + COEF_C * product[:, other * tile : (other + 1) * tile]
+                if other == index:
+                    total = jnp.where(eye, total - COEF_C * values * values, total)
+                    part = jnp.sum(jnp.where(eye, total, 0.0), axis=1, keepdims=True)
+                    total = jnp.where(eye, 0.0, total)
+                poly[band(index), band(other)] = total.astype(BF16)
             slope[band(index), :] = jnp.broadcast_to(part + COEF_A, (tile, 128))
-            return _
-
-        lax.fori_loop(0, tiles, make_poly, 0)
 
         def advance(lap, _):
             block, index = lap // tiles, lap % tiles
-            scaled = spread(slope[band(index), :], size) * current[block, band(index), :]
-            values = scaled + dot(poly[band(index), :], rounded[now, block], 1, 0)
-            current[block, band(index), :] = values
-            rounded[1 - now, block, band(index), :] = values.astype(BF16)
-            return _
+            rows = pl.ds(pl.multiple_of(index * tile, tile), tile)
+            scaled = spread(slope[rows, :], size) * current[block, rows, :]
+            values = scaled + dot(poly[rows, :], rounded[now, block], 1, 0)
+            current[block, rows, :] = values
+            rounded[1 - now, block, rows, :] = values.astype(BF16)
+            return 0
 
         def advance_first(lap, _):
             block, index = lap // tiles, lap % tiles
-            scaled = spread(slope[band(index), :], size) * current[block, band(index), :]
-            product = dot(poly[band(index), :], rounded[now, block], 1, 0)
-            values = (scaled + product) * factor
-            current[block, band(index), :] = values
-            rounded[1 - now, block, band(index), :] = values.astype(BF16)
-            return _
+            rows = pl.ds(pl.multiple_of(index * tile, tile), tile)
+            scaled = spread(slope[rows, :], size) * current[block, rows, :]
+            values = (scaled + dot(poly[rows, :], rounded[now, block], 1, 0)) * factor
+            current[block, rows, :] = values
+            rounded[1 - now, block, rows, :] = values.astype(BF16)
+            return 0
 
         @pl.when(step == 0)
         def _():
@@ -1448,35 +1923,37 @@
 
     lax.fori_loop(0, ORTHO_STEPS, sweep, factor * factor)
 
-    def store(block, _):
+    def store(lap, _):
+        block, index = lap // tiles, lap % tiles
+        rows = pl.ds(pl.multiple_of(index * tile, tile), tile)
+
         @pl.when(turned)
         def _():
-            for index in range(cuts):
-                cut = pl.ds(index * CUT, CUT)
-                out[block, :, cut] = current[block, cut, :].T.astype(BF16)
+            out[block, :, rows] = current[block, rows, :].T.astype(BF16)
 
         @pl.when(jnp.logical_not(turned))
         def _():
-            for index in range(cuts):
-                cut = pl.ds(index * CUT, CUT)
-                out[block, cut, :] = current[block, cut, :].astype(BF16)
+            out[block, rows, :] = current[block, rows, :].astype(BF16)
 
         return 0
 
-    lax.fori_loop(0, blocks, store, 0)
+    lax.fori_loop(0, blocks * tiles, store, 0)
 
 
 def orthogonalize(scale, moments, experts, inward, outward):
     blocks, size, width = experts.shape
     vmem = pl.BlockSpec(memory_space=pltpu.VMEM)
     smem = pl.BlockSpec(memory_space=pltpu.SMEM)
+    unread = pl.BlockSpec(memory_space=pl.ANY)
     place = lax.axis_index("mat").astype(jnp.int32).reshape(1)
     return pl.pallas_call(
         ortho_kernel,
         out_shape=jax.ShapeDtypeStruct(experts.shape, BF16),
-        in_specs=[smem, smem] + [vmem] * 6,
+        in_specs=[smem, smem] + [unread] * 4,
         out_specs=vmem,
         scratch_shapes=[
+            pltpu.VMEM((blocks, size, width), BF16),
+            pltpu.VMEM((blocks, size, width), BF16),
             pltpu.VMEM((blocks, size, width), F32),
             pltpu.VMEM((2, blocks, size, width), BF16),
             pltpu.VMEM((size, size), F32),
@@ -1484,10 +1961,11 @@
             pltpu.VMEM((size, size), BF16),
             pltpu.VMEM((size, 128), F32),
             pltpu.VMEM((1, size), F32),
+            pltpu.SemaphoreType.DMA((1 + blocks,)),
         ],
         compiler_params=pltpu.CompilerParams(vmem_limit_bytes=56 * 1024 * 1024),
         name="orthogonalize",
-    )(place, scale.reshape(1), *moments, experts, inward, outward)
+    )(place, scale.reshape(1), moments, experts, inward, outward)
 
 
 def adamw_update(weight, mean, square, grad, rate, decay):
@@ -1581,7 +2059,7 @@
     found, w_table, w_out, w_up, w_down = lax.optimization_barrier(
         (
             found,
-            embedding.astype(BF16),
+            embedding.T.astype(BF16),
             out_project.astype(BF16),
             expert_up.astype(BF16),
             expert_down.astype(BF16),
@@ -1589,7 +2067,7 @@
     )
     small = unpack_small(small, parts)
     weights = (
-        lax.all_gather(w_table, "mat", axis=1, tiled=True),
+        lax.all_gather(w_table, "mat", axis=0, tiled=True),
         lax.all_gather(in_project.astype(BF16), "mat", axis=1, tiled=True),
         lax.all_gather(w_out, "mat", axis=0, tiled=True),
         lax.all_gather(w_up, "mat", axis=2, tiled=True),
@@ -1614,9 +2092,9 @@
             jnp.pad(out_project_mom, ((0, D - out_project_mom.shape[0]), (0, 0))),
         ]
     ).astype(BF16)
-    grads, moved, x0_grad, loss_part, count_part, rows_here = step_grads(
+    moments = lax.all_to_all(moments, "mat", split_axis=0, concat_axis=0, tiled=True)
+    grads, x0_grad, loss_part, count_part, rows_here = step_grads(
         weights,
-        jnp.split(moments, 3, axis=1),
         embedded,
         expert_route[:, 0, :, 0],
         doc_lengths[:, 0],
@@ -1641,6 +2119,7 @@
     x0_parts = x0_grad.reshape(2, -1, mats, part).transpose(2, 0, 1, 3)
     x0_heads = x0_parts[..., :128].reshape(mats, -1, 128)
     x0_tails = jnp.concatenate([x0_parts[:, 0, :, 128:], x0_parts[:, 1, :, 128:]], axis=2)
+    x0_heads, moments = lax.optimization_barrier((x0_heads, moments))
     x0_rows = 3 * micros * tokens // 2
     mixed = lax.all_to_all(
         jnp.concatenate([x0_heads, x0_tails, packed], axis=1),
@@ -1658,22 +2137,18 @@
         13,
         [s_up[0], s_down[0]],
     )
-    s_in, s_out, packed = exchange(
+    s_in, s_out, packed = reduce_seq(
         [
             s_in.reshape(seq_count, -1, D),
             s_out.reshape(seq_count, -1, D),
             packed.reshape(seq_count, -1, 128),
         ],
-        [False, False, False],
         14,
-        ahead=[g_table],
-    )
-    s_in = jnp.sum(s_in.astype(F32), axis=0)
-    s_out = jnp.sum(s_out.astype(F32), axis=0)
-    packed = jnp.sum(packed.astype(F32), axis=0)
+        [g_table],
+    )
     s_up = s_up.astype(F32)
     s_down = s_down.astype(F32)
-    squares = sum(jnp.sum(g * g) for g in (s_up, s_down, s_in, s_out, packed))
+    squares = sum(jnp.sum(g * g) for g in (s_in, s_out, packed))
     squares = squares + jnp.sum(table_squares[0])
     tallies = jnp.stack([squares, loss_part, count_part])
     tallies = jnp.broadcast_to(jnp.pad(tallies, (0, 5))[:, None], (8, 128))
@@ -1686,13 +2161,6 @@
     g_out = g_out.reshape(-1, D).astype(F32)
     totals = exchange([jnp.sum(totals, axis=0)], [True], 11, ("mat",))[0]
     totals = jnp.sum(totals[:, :, 0], axis=0)
-    packed = packed.reshape(-1)
-    shards, offset = [], 0
-    for piece, like in zip(
-        pieces, (x_project, step_project, router_weight, channel_param, norm_gains)
-    ):
-        shards.append(packed[offset : offset + piece.shape[1]].reshape(like.shape))
-        offset += piece.shape[1]
     squares, loss_total, loss_count = totals[0], totals[1], totals[2]
     grad_norm = jnp.sqrt(squares)
     scale = jnp.minimum(1.0, CLIP_NORM / (grad_norm + 1e-06))
@@ -1702,11 +2170,19 @@
     mom_down = MOMENTUM * expert_down_mom + s_down * scale
     ortho = orthogonalize(
         scale,
-        moved,
+        moments,
         whole_experts,
         whole_in.reshape(mats, D, -1),
         whole_out.reshape(mats, -1, D),
     )
+    packed, ortho = lax.optimization_barrier((packed, ortho))
+    packed = packed.reshape(-1)
+    shards, offset = [], 0
+    for piece, like in zip(
+        pieces, (x_project, step_project, router_weight, channel_param, norm_gains)
+    ):
+        shards.append(packed[offset : offset + piece.shape[1]].reshape(like.shape))
+        offset += piece.shape[1]
     table_new = update_table(
         scale, g_table, embedding.T, embedding_mom.T, embedding_sq.T, ortho
     )

time: 986 us -> 881 us (0.89)
  matrix products: 121 us -> 27.8 us
  other arithmetic: 100 us -> 77.9 us
  waiting for transfers between devices: 30.8 us -> 42.6 us
    pallas_call x1 -> x9, Pallas kernels: 8.02 us -> 135 us  [the longest x2 42.2 us: reduce_seq(): pl.pallas_call(body, out_shape=[jax.ShapeDtypeStruct(shape, BF16) for sha...]
    pallas_call x9 -> x7, Pallas kernels: 209 us -> 96.4 us  [exchange(): pl.pallas_call(functools.partial(exchange_kernel, tuple(groups), tuple(ga...]
    dot_general x6 -> x0, matrix products: 53.3 us -> none  [the longest x1 18.8 us: step_grads(): jnp.einsum('erk,ekn->ern', taken, w_up, preferred_element_type=F32)]
    dot_general x18 -> x11, matrix products: 65.1 us -> 24.1 us  [dot(): lax.dot_general(left, right, (((left_dim,), (right_dim,)), ((), ())), pre...]
    pallas_call x1, Pallas kernels: 77.9 us -> 60.9 us  [orthogonalize(): pl.pallas_call(ortho_kernel, out_shape=jax.ShapeDtypeStruct(experts.shape...]
    reduce_sum x12 -> x8, other arithmetic: 19.4 us -> 3.74 us  [the longest x3 3.12 us: local(): squares = sum((jnp.sum(g * g) for g in (s_in, s_out, packed)))]
    ppermute x2, starting transfers between devices: 15.2 us -> 3.79 us  [move_rows(): lax.ppermute(value, 'seq', [(source, source + steps) for source in range(...]
    reduce_scatter x5, waiting for transfers between devices: 0.52 us -> 10.5 us  [scatter_mat(): lax.psum_scatter(grad.astype(BF16), 'mat', scatter_dimension=dim, tiled=T...]
  transfers between devices with their start and end apart: 14 -> 15, of which waited for: 3 -> 3; matrix products, arithmetic and copies ran while one was open for 23% -> 16% of each run, Pallas kernels for 41% -> 46%
where the time goes in v2:
time: 881 us; the launch traced here: 869 us
  Pallas kernels  580 us (66%)
  local copies, waits for them, and re-layouts  100 us (11%)
  other arithmetic  77.9 us (9%)
  waiting for transfers between devices  42.6 us (5%)
  matrix products  27.8 us (3%)
  between operations  21.4 us (2%)
  starting transfers between devices  19.3 us (2%)
    pallas_call x4, Pallas kernels, gather_seq(): pl.pallas_call(functools.partial(gather_kernel, arrays, len(ahead), tuple...  97.4 us
    pallas_call x7, Pallas kernels, exchange(): pl.pallas_call(functools.partial(exchange_kernel, tuple(groups), tuple(ga...  96.4 us
    pallas_call x1, Pallas kernels, scatter_rows(): pl.pallas_call(functools.partial(scatter_rows_kernel, entries), out_shape...  62.4 us
    pallas_call x1, Pallas kernels, orthogonalize(): pl.pallas_call(ortho_kernel, out_shape=jax.ShapeDtypeStruct(experts.shape...  60.9 us
    pallas_call x1, Pallas kernels, lookup(): pl.pallas_call(lookup_kernel, out_shape=[jax.ShapeDtypeStruct((mats, 384,...  55.3 us
    unnamed x339, local copies, waits for them, and re-layouts  53.3 us
    pallas_call x2, Pallas kernels, reduce_seq(): pl.pallas_call(body, out_shape=[jax.ShapeDtypeStruct(shape, BF16) for sha...  42.2 us
    pallas_call x1, Pallas kernels, scan_backward(): pl.pallas_call(body, grid=(micros, inner // LANES), in_specs=[scalars, sc...  30.6 us
  transfers between devices with their start and end apart: 15, of which 3 were waited for; matrix products, arithmetic and copies ran while one was open for 16% of the time, Pallas kernels for 46%

profile of v2, /device:TPU:0, one launch (start us, length us, event | category | flops | bytes accessed | tf_op | source)
XLA Modules:
  0.0 869.3 jit_solution(4970340060871342445)
XLA Ops:
  10.1 6.0 exchange.7
  16.9 7.3 bitcast_convert_fusion
  44.0 55.3 %lookup.1 = (bf16[4,384,128]{2,1,0:T(8,128)(2,1)}, bf16[4,64,1024]{2,1,0:T(8,128)(2,1)}) custom-call(s32[8192]{0:T(1024)} %and_select_fusion.ids, f32[6296,256]{1,0:T(8,128)} %pad_convert_fusion.table, bf16[64,1024]{1,0:T(8,128)(2,1)} %reshape.518.small), custom_call_target="tpu_custom_call" | custom-call | tf_op jit(solution)/shard_map/lookup/pallas_call | solution.py:1303
  121.1 5.8 mixer_conv.1
  130.7 14.6 %scan_end.1 = (f32[2,128,1536]{2,1,0:T(8,128)S(1)}, f32[2,128,1536]{2,1,0:T(8,128)S(1)}, bf16[32,1536]{1,0:T(8,128)(2,1)S(1)}, f32[8,1536]{1,0:T(8,128)S(1)}) custom-call(f32[2,128]{1,0:T(2,128)S(1)} %fusion.50.keep.refs_1_, f32[2,128,80]{2,1,0:T(8,128)S(1)} %get-tuple-element.94.projected, bf16[48,1536]{1,0:T(8,128)(2,1)S(1)} %bitcast.280, ...), custom_call_target="tpu_custom_call" | custom-call | tf_op jit(solution)/shard_map/scan_end/pallas_call | solution.py:373
  147.7 24.0 %gather_seq.4 = (bf16[8,2,16,1536]{3,2,1,0:T(8,128)(2,1)}, f32[8,1,8,1536]{3,2,1,0:T(8,128)}) custom-call(bf16[2,16,1536]{2,1,0:T(8,128)(2,1)} %bitcast.285, f32[1,8,1536]{2,1,0:T(8,128)} %bitcast.286), custom_call_target="tpu_custom_call" | custom-call | tf_op jit(solution)/shard_map/gather_seq/pallas_call | solution.py:1008
  175.6 18.0 %scan_forward.1 = (f32[2,128,1536]{2,1,0:T(8,128)S(1)}, f32[2,128,16,1536]{3,2,1,0:T(8,128)}, f32[2,16,1536]{2,1,0:T(8,128)S(1)}) custom-call(s32[1]{0:T(128)} %bitcast.12.place.refs_0_, f32[2,128]{1,0:T(2,128)S(1)} %fusion.50.keep.refs_1_, f32[2,128,1536]{2,1,0:T(8,128)S(1)} %get-tuple-element.95.dt.refs_2_, ...), custom_call_target="tpu_custom_call" | custom-call | tf_op jit(solution)/shard_map/scan_forward/pallas_call | solution.py:404
  201.3 16.6 %exchange.8 = bf16[8,64,768]{2,1,0:T(8,128)(2,1)} custom-call(bf16[8,64,768]{2,1,0:T(8,128)(2,1)} %bitcast.304), custom_call_target="tpu_custom_call" | custom-call | tf_op jit(solution)/shard_map/exchange/pallas_call | solution.py:749
  219.3 13.0 %experts.1 = (bf16[1,512,3072]{2,1,0:T(8,128)(2,1)S(1)}, f32[1,512,3072]{2,1,0:T(8,128)}, bf16[1,512,768]{2,1,0:T(8,128)(2,1)S(1)}) custom-call(bf16[1,512,768]{2,1,0:T(8,128)(2,1)S(1)} %bitcast.255, bf16[1,768,3072]{2,1,0:T(8,128)(2,1)} %all-gather.10.cloned.1.call-done.w_up, bf16[1,3072,768]{2,1,0:T(8,128)(2,1)} %all-gather.12.cloned.1.call-done.w_down), custom_call_target="tpu_custom_call" | custom-call | tf_op jit(solution)/shard_map/experts/pallas_call | solution.py:519
  234.8 20.3 %exchange.9 = bf16[8,64,768]{2,1,0:T(8,128)(2,1)} custom-call(bf16[8,64,768]{2,1,0:T(8,128)(2,1)} %bitcast.278), custom_call_target="tpu_custom_call" | custom-call | tf_op jit(solution)/shard_map/exchange/pallas_call | solution.py:749
  259.8 21.2 %gather_seq.5 = bf16[8,2,32,768]{3,2,1,0:T(8,128)(2,1)} custom-call(bf16[2,32,768]{2,1,0:T(8,128)(2,1)} %convolution_convert_fusion.5.refs_0_), custom_call_target="tpu_custom_call" | custom-call | tf_op jit(solution)/shard_map/gather_seq/pallas_call | solution.py:1008
  283.5 15.4 %head.1 = (f32[512,6288]{1,0:T(8,128)}, f32[512,8]{1,0:T(8,128)S(1)}) custom-call(s32[3]{0:T(128)S(1)} %pad_add_fusion.limits, bf16[512,768]{1,0:T(8,128)(2,1)S(1)} %bitcast.258, bf16[768,6288]{1,0:T(8,128)(2,1)} %all-gather.14.cloned.1.call-done.table, s32[512,1]{1,0:T(8,128)S(1)} %copy-done.21), custom_call_target="tpu_custom_call" | custom-call | tf_op jit(solution)/shard_map/head/pallas_call | solution.py:634
  299.6 8.5 exchange.10
  310.1 20.1 %head_back.1 = (bf16[768,6288]{1,0:T(8,128)(2,1)}, bf16[512,768]{1,0:T(8,128)(2,1)S(1)}) custom-call(s32[3]{0:T(128)S(1)} %pad_add_fusion.limits, bf16[768,512]{1,0:T(8,128)(2,1)S(1)} %bitcast.262, bf16[768,6288]{1,0:T(8,128)(2,1)} %all-gather.14.cloned.1.call-done.table, s32[512,1]{1,0:T(8,128)S(1)} %copy-done.21, f32[512,8]{1,0:T(8,128)S(1)} %pad.39.scalars, ...), custom_call_target="tpu_custom_call" | custom-call | tf_op jit(solution)/shard_map/head_back/pallas_call | solution.py:652
  332.2 12.9 %reduce_seq.2 = bf16[4,64,768]{2,1,0:T(8,128)(2,1)S(1)} custom-call(bf16[8,64,768]{2,1,0:T(8,128)(2,1)S(1)} %bitcast.277), custom_call_target="tpu_custom_call" | custom-call | tf_op jit(solution)/shard_map/reduce_seq/pallas_call | solution.py:1126
  349.8 14.4 %exchange.11 = bf16[8,64,768]{2,1,0:T(8,128)(2,1)} custom-call(bf16[8,64,768]{2,1,0:T(8,128)(2,1)} %bitcast.301, bf16[768,6288]{1,0:T(8,128)(2,1)} %get-tuple-element.109.refs_1_), custom_call_target="tpu_custom_call" | custom-call | tf_op jit(solution)/shard_map/exchange/pallas_call | solution.py:749
  367.3 17.1 %experts_back.1 = (bf16[1,768,3072]{2,1,0:T(8,128)(2,1)}, bf16[1,3072,768]{2,1,0:T(8,128)(2,1)}, bf16[1,512,768]{2,1,0:T(8,128)(2,1)S(1)}) custom-call(bf16[1,512,768]{2,1,0:T(8,128)(2,1)S(1)} %bitcast.256, bf16[1,512,768]{2,1,0:T(8,128)(2,1)S(1)} %bitcast.261, bf16[1,768,3072]{2,1,0:T(8,128)(2,1)} %all-gather.10.cloned.1.call-done.w_up, ...), custom_call_target="tpu_custom_call" | custom-call | tf_op jit(solution)/shard_map/experts_back/pallas_call | solution.py:538
  385.2 16.7 %exchange.12 = bf16[8,64,768]{2,1,0:T(8,128)(2,1)} custom-call(bf16[8,64,768]{2,1,0:T(8,128)(2,1)} %bitcast.276, bf16[768,6288]{1,0:T(8,128)(2,1)} %get-tuple-element.109.refs_1_), custom_call_target="tpu_custom_call" | custom-call | tf_op jit(solution)/shard_map/exchange/pallas_call | solution.py:749
  405.7 10.5 %reduce-scatter.6.cloned.1.call-done.refs_2_ = bf16[192,6288]{1,0:T(8,128)(2,1)} async-done(((bf16[768,6288]{1,0:T(8,128)(2,1)}), bf16[192,6288]{1,0:T(8,128)(2,1)}) %reduce-scatter.6.cloned.1.call-update) | async-done | bytes 2414608 | tf_op jit(solution)/shard_map/reduce_scatter | solution.py:1776
  450.7 7.6 scan_start.1
  459.0 18.5 %gather_seq.6 = bf16[8,2,16,1536]{3,2,1,0:T(8,128)(2,1)} custom-call(bf16[2,16,1536]{2,1,0:T(8,128)(2,1)} %bitcast.282), custom_call_target="tpu_custom_call" | custom-call | tf_op jit(solution)/shard_map/gather_seq/pallas_call | solution.py:1008
  479.6 30.6 %scan_backward.1 = (f32[2,128,1536]{2,1,0:T(8,128)S(1)}, f32[2,128,1536]{2,1,0:T(8,128)S(1)}, f32[2,128,16,128]{3,2,1,0:T(8,128)}, f32[2,128,16,128]{3,2,1,0:T(8,128)}, f32[2,16,1536]{2,1,0:T(8,128)S(1)}) custom-call(s32[1]{0:T(128)} %bitcast.12.place.refs_0_, f32[2,128]{1,0:T(2,128)S(1)} %fusion.50.keep.refs_1_, f32[2,128,1536]{2,1,0:T(8,128)} %copy-done.4, ...), custom_call_target="tpu_custom_call" | custom-call | tf_op jit(solution)/shard_map/scan_backward/pallas_call | solution.py:448
  516.7 7.4 mixer_conv_back.1
  558.8 9.3 %all-to-all-done.1 = bf16[4,896,128]{2,1,0:T(8,128)(2,1)} async-done(((bf16[4,896,128]{2,1,0:T(8,128)(2,1)}), bf16[4,896,128]{2,1,0:T(8,128)(2,1)}, u32[]{:S(2)}, u32[]{:S(2)}) %all-to-all-start.1) | async-done | bytes 917536 | tf_op jit(solution)/shard_map/all_to_all | solution.py:2124
  572.9 62.4 %scatter_rows.1 = (f32[6400,256]{1,0:T(8,128)}, f32[8,256]{1,0:T(8,128)S(1)}, bf16[4,768,768]{2,1,0:T(8,128)(2,1)}) custom-call(s32[64,128]{1,0:T(8,128)S(1)} %bitcast.284, bf16[4,384,128]{2,1,0:T(8,128)(2,1)S(1)} %slice.199.rows, bf16[192,6400]{1,0:T(8,128)(2,1)S(1)} %pad.43.others, bf16[768,768]{1,0:T(8,128)(2,1)S(1)} %bitcast.259, ...), custom_call_target="tpu_custom_call" | custom-call | tf_op jit(solution)/shard_map/scatter_rows/pallas_call | solution.py:1489
  638.2 29.3 %reduce_seq.3 = (bf16[4,96,768]{2,1,0:T(8,128)(2,1)S(1)}, bf16[4,48,768]{2,1,0:T(8,128)(2,1)S(1)}, bf16[4,64,128]{2,1,0:T(8,128)(2,1)S(1)}) custom-call(bf16[8,96,768]{2,1,0:T(8,128)(2,1)S(1)} %bitcast.274, bf16[8,48,768]{2,1,0:T(8,128)(2,1)S(1)} %bitcast.279, bf16[8,64,128]{2,1,0:T(8,128)(2,1)S(1)} %bitcast.281, f32[6400,256]{1,0:T(8,128)} %get-tuple-element.130.refs_3_.grad), custom_call_target="tpu_custom_call" | custom-call | tf_op jit(solution)/shard_map/reduce_seq/pallas_call | solution.py:1126
  675.4 33.7 %gather_seq.7 = (bf16[8,2,48,768]{3,2,1,0:T(8,128)(2,1)}, bf16[8,1,48,768]{3,2,1,0:T(8,128)(2,1)}, f32[8,2,32,128]{3,2,1,0:T(8,128)}, f32[8,1,8,128]{3,2,1,0:T(8...) custom-call(bf16[2,48,768]{2,1,0:T(8,128)(2,1)} %bitcast.339, ...), custom_call_target="tpu_custom_call" | custom-call | tf_op jit(solution)/shard_map/gather_seq/pallas_call | solution.py:1008
  710.5 13.9 %exchange.13 = f32[4,8,128]{2,1,0:T(8,128)} custom-call(f32[8,128]{1,0:T(8,128)} %reduce_sum.321.refs_0_), custom_call_target="tpu_custom_call" | custom-call | tf_op jit(solution)/shard_map/exchange/pallas_call | solution.py:749
  726.6 60.9 %orthogonalize.1._ahead = bf16[4,768,768]{2,1,0:T(8,128)(2,1)} custom-call(s32[1]{0:T(128)} %bitcast.107.place, f32[1]{0:T(128)} %bitcast.103.scale, bf16[4,768,768]{2,1,0:T(8,128)(2,1)} %all-to-all-done.moments, bf16[4,768,768]{2,1,0:T(8,128)(2,1)} %get-tuple-element.138.experts, bf16[4,768,768]{2,1,0:T(8,128)(2,1)} %bitcast.299, bf16[4,384,768]{2,1,0:T(8,128)(2,1)} %bitcast.311), custom_call_target="tpu_custom_call" | custom-call | tf_op jit(solution)/shard_map/orthogonalize/pallas_call | solution.py:1949
  792.3 5.4 all-to-all-start.2
  802.8 16.2 %update_table.1 = (f32[192,6288]{1,0:T(8,128)}, f32[192,6288]{1,0:T(8,128)}, f32[192,6288]{1,0:T(8,128)}) custom-call(f32[1]{0:T(128)} %bitcast.103.scale, f32[6400,256]{1,0:T(8,128)} %get-tuple-element.130.refs_3_.grad, f32[192,6288]{1,0:T(8,128)} %bitcast.290, f32[192,6288]{1,0:T(8,128)} %bitcast.297, f32[192,6288]{1,0:T(8,128)} %bitcast.298, ...), custom_call_target="tpu_custom_call" | custom-call | flops 32194560 | bytes 45072384 | tf_op jit(solution)/shard_map/update_table/pallas_call | solution.py:1992
  831.4 20.1 %all-to-all-done.2 = bf16[4,768,768]{2,1,0:T(8,128)(2,1)} async-done(((bf16[4,768,768]{2,1,0:T(8,128)(2,1)}), bf16[4,768,768]{2,1,0:T(8,128)(2,1)}, u32[]{:S(2)}, u32[]{:S(2)}) %all-to-all-start.2) | async-done | bytes 4718624 | tf_op jit(solution)/shard_map/all_to_all | solution.py:2190
  (585 shorter events, 214.9 us)
Async XLA Ops:
  7.2 99.4 %all-gather.6.cloned.1.call-start = ((), (), s32[]{:S(2)}) async-start(), calls=%async_computation.8 | async-start | bytes 5898240 | tf_op jit(solution)/shard_map/all_gather | solution.py:2071
  10.1 186.8 %all-gather.8.cloned.1.call-start = ((), (), s32[]{:S(2)}) async-start(), calls=%async_computation.9 | async-start | bytes 2949120 | tf_op jit(solution)/shard_map/all_gather | solution.py:2072
  16.9 23.3 %copy-start.43 = (s32[4,2,8,128]{3,1,0,2:T(2,128)}, s32[4,2,8,128]{3,1,0,2:T(2,128)S(1)}, u32[]{:S(2)}) copy-start(s32[4,2,8,128]{3,1,0,2:T(2,128)S(1)} %copy.250) | copy-start | bytes 98308
  99.3 118.7 %all-gather.10.cloned.1.call-start = ((), (), s32[]{:S(2)}) async-start(), calls=%async_computation.10 | async-start | bytes 5898240 | tf_op jit(solution)/shard_map/all_gather | solution.py:2073
  100.1 117.9 %all-gather.12.cloned.1.call-start = ((), (), s32[]{:S(2)}) async-start(), calls=%async_computation.11 | async-start | bytes 5898240 | tf_op jit(solution)/shard_map/all_gather | solution.py:2074
  100.7 181.7 %all-gather.14.cloned.1.call-start = ((), (), s32[]{:S(2)}) async-start(), calls=%async_computation.12 | async-start | bytes 12288000 | tf_op jit(solution)/shard_map/all_gather | solution.py:2070
  101.3 314.9 %reduce-scatter.6.cloned.1.call-start = ((), (), s32[]{:S(2)}) async-start(), calls=%async_computation.13 | async-start | bytes 12288000 | tf_op jit(solution)/shard_map/reduce_scatter | solution.py:1776
  110.5 10.6 %collective-permute-start = (f32[2,3,1536]{2,1,0:T(4,128)S(1)}, f32[2,3,1536]{2,1,0:T(4,128)S(1)}, u32[]{:S(2)}, u32[]{:S(2)}) collective-permute-start(f32[2,3,1536]{2,1,0:T(4,128)S(1)} %slice.181), channel_id=1, source_target_pairs={{0,4},{4,8},{8,12},{12,16},{16,20},{20,24},{24,28},{1,5},{5,9},{9,... | collective-permute-start | bytes 110600 | tf_op jit(solution)/shard_map/ppermute | solution.py:1521
  128.0 311.5 %copy-start = (f32[2,128,1536]{2,1,0:T(8,128)}, f32[2,128,1536]{2,1,0:T(8,128)S(1)}, u32[]{:S(2)}) copy-start(f32[2,128,1536]{2,1,0:T(8,128)S(1)} %get-tuple-element.93.act.refs_3_) | copy-start | bytes 4718596
  147.7 45.9 %copy-start.4 = (f32[2,128,1536]{2,1,0:T(8,128)}, f32[2,128,1536]{2,1,0:T(8,128)S(1)}, u32[]{:S(2)}) copy-start(f32[2,128,1536]{2,1,0:T(8,128)S(1)} %get-tuple-element.95.dt.refs_2_) | copy-start | bytes 4718596
  175.6 19.8 %copy-start.53 = (f32[2,128,3072]{2,1,0:T(8,128)S(1)}, f32[2,128,3072]{2,1,0:T(8,128)}, u32[]{:S(2)}) copy-start(f32[2,128,3072]{2,1,0:T(8,128)} %copy-done.52) | copy-start | bytes 9437188
  175.6 19.8 %copy-start.110 = (f32[1536]{0:T(1024)S(1)}, f32[1536]{0:T(1024)}, u32[]{:S(2)}) copy-start(f32[1536]{0:T(1024)} %mul.596) | copy-start | bytes 18436
  199.7 57.8 %copy-start.55 = (f32[256,768]{1,0:T(8,128)}, f32[256,768]{1,0:T(8,128)S(1)}, u32[]{:S(2)}) copy-start(f32[256,768]{1,0:T(8,128)S(1)} %get-tuple-element.362) | copy-start | bytes 2359300
  199.9 56.4 %copy-start.79 = (bf16[256,768]{1,0:T(8,128)(2,1)}, bf16[256,768]{1,0:T(8,128)(2,1)S(1)}, u32[]{:S(2)}) copy-start(bf16[256,768]{1,0:T(8,128)(2,1)S(1)} %multiply_convert_fusion.4) | copy-start | bytes 1179652
  234.8 21.5 %copy-start.86 = (bf16[768,8]{1,0:T(8,128)(2,1)S(1)}, bf16[768,8]{1,0:T(8,128)(2,1)}, u32[]{:S(2)}) copy-start(bf16[768,8]{1,0:T(8,128)(2,1)} %reshape_reshape.18) | copy-start | bytes 36868
  234.8 21.5 %copy-start.118 = (s32[2,1,128,1]{2,3,1,0:T(1,128)S(1)}, s32[2,1,128,1]{2,3,1,0:T(1,128)}, u32[]{:S(2)}) copy-start(s32[2,1,128,1]{2,3,1,0:T(1,128)} %param.33) | copy-start | bytes 3076
  234.8 22.4 %copy-start.126 = (s32[2,128]{1,0:T(2,128)S(1)}, s32[2,128]{1,0:T(2,128)}, u32[]{:S(2)}) copy-start(s32[2,128]{1,0:T(2,128)} %add_add_fusion) | copy-start | bytes 3076
  257.8 24.6 %copy-start.21 = (s32[512,1]{1,0:T(8,128)S(1)}, s32[512,1]{1,0:T(8,128)}, u32[]{:S(2)}) copy-start(s32[512,1]{1,0:T(8,128)} %broadcast_in_dim_reshape.5.targets) | copy-start | bytes 6148
  283.5 26.3 %copy-start.147 = (f32[512,1]{0,1:T(1,128)S(1)}, f32[512,1]{0,1:T(1,128)}, u32[]{:S(2)}) copy-start(f32[512,1]{0,1:T(1,128)} %div.135) | copy-start | bytes 6148
  331.1 239.2 %reduce-scatter.12.cloned.1.call-start = ((), (), s32[]{:S(2)}) async-start(), calls=%async_computation.16 | async-start | bytes 5898240 | tf_op jit(solution)/shard_map/reduce_scatter | solution.py:1776
  416.2 154.1 %reduce-scatter.14.cloned.1.call-start = ((), (), s32[]{:S(2)}) async-start(), calls=%async_computation.17 | async-start | bytes 5898240 | tf_op jit(solution)/shard_map/reduce_scatter | solution.py:1776
  416.9 218.9 %reduce-scatter.10.cloned.1.call-start = ((), (), s32[]{:S(2)}) async-start(), calls=%async_computation.15 | async-start | bytes 2949120 | tf_op jit(solution)/shard_map/reduce_scatter | solution.py:1776
  427.4 118.8 %all-to-all-start = ((bf16[4,768,768]{2,1,0:T(8,128)(2,1)}), bf16[4,768,768]{2,1,0:T(8,128)(2,1)}, u32[]{:S(2)}, u32[]{:S(2)}) async-start(bf16[4,768,768]{2,1,0:T(8,128)(2,1)} %pad_maximum_fusion), calls=%async_computation.3 | async-start | bytes 9437184 | tf_op jit(solution)/shard_map/all_to_all | solution.py:2095
  432.6 203.3 %reduce-scatter.8.cloned.1.call-start = ((), (), s32[]{:S(2)}) async-start(), calls=%async_computation.14 | async-start | bytes 5898240 | tf_op jit(solution)/shard_map/reduce_scatter | solution.py:1776
  450.7 26.8 %copy-start.20 = (f32[4,2,8,384]{3,2,0,1:T(8,128)S(1)}, f32[4,2,8,384]{3,2,0,1:T(8,128)}, u32[]{:S(2)}) copy-start(f32[4,2,8,384]{3,2,0,1:T(8,128)} %copy.311) | copy-start | bytes 294916
  450.7 26.8 %copy-start.28 = (f32[8,1,8,1536]{3,2,1,0:T(8,128)S(1)}, f32[8,1,8,1536]{3,2,1,0:T(8,128)}, u32[]{:S(2)}) copy-start(f32[8,1,8,1536]{3,2,1,0:T(8,128)} %get-tuple-element.99) | copy-start | bytes 1179652
  479.6 30.6 %copy-start.30 = (f32[2,128,1536]{2,1,0:T(8,128)S(1)}, f32[2,128,1536]{2,1,0:T(8,128)}, u32[]{:S(2)}) copy-start(f32[2,128,1536]{2,1,0:T(8,128)} %copy-done.29) | copy-start | bytes 4718596
  524.2 7.4 collective-permute-start.1
  549.6 18.6 %all-to-all-start.1 = ((bf16[4,896,128]{2,1,0:T(8,128)(2,1)}), bf16[4,896,128]{2,1,0:T(8,128)(2,1)}, u32[]{:S(2)}, u32[]{:S(2)}) async-start(bf16[4,896,128]{2,1,0:T(8,128)(2,1)} %pad_maximum_fusion.2), calls=%async_computation.4 | async-start | bytes 1835008 | tf_op jit(solution)/shard_map/all_to_all | solution.py:2124
  726.6 60.9 %copy-start.93 = (f32[8,2,32,128]{3,2,1,0:T(8,128)S(1)}, f32[8,2,32,128]{3,2,1,0:T(8,128)}, u32[]{:S(2)}) copy-start(f32[8,2,32,128]{3,2,1,0:T(8,128)} %get-tuple-element.136) | copy-start | bytes 786436
  792.3 59.3 %all-to-all-start.2 = ((bf16[4,768,768]{2,1,0:T(8,128)(2,1)}), bf16[4,768,768]{2,1,0:T(8,128)(2,1)}, u32[]{:S(2)}, u32[]{:S(2)}) async-start(bf16[4,768,768]{2,1,0:T(8,128)(2,1)} %orthogonalize.1._ahead), calls=%async_computation.7 | async-start | bytes 9437184 | tf_op jit(solution)/shard_map/all_to_all | solution.py:2190
  831.4 23.5 %copy-start.61 = (f32[1,768,768]{2,1,0:T(8,128)S(1)}, f32[1,768,768]{2,1,0:T(8,128)}, u32[]{:S(2)}) copy-start(f32[1,768,768]{2,1,0:T(8,128)} %param.45) | copy-start | bytes 7077892
  (141 other events, 738.0 us)
Sparse Core Ops, SparseCore 0:
  10.2 40.1 all-gather.5
  99.5 27.7 all-gather.7
  129.4 37.4 all-gather.9
  168.9 37.4 all-gather.11
  208.4 66.4 all-gather.13
  331.2 84.9 reduce-scatter.5
  419.3 73.2 reduce-scatter.11
  495.8 47.8 reduce-scatter.13
  546.8 34.2 reduce-scatter.9
  584.3 51.4 reduce-scatter.7

commit v3 on v2

--- a/solution.py
+++ b/solution.py
@@ -893,15 +893,35 @@
     return [pltpu.SemaphoreType.DMA(shape)] * Line.SEMAPHORES
 
 
-def gather_kernel(arrays, ahead, relays, *refs):
+def gather_kernel(arrays, ahead, relays, everyone, *refs):
+    if everyone:
+        tally, tallies = refs[arrays], refs[2 * arrays + 1 + ahead]
+        refs = list(refs)
+        del refs[2 * arrays + 1 + ahead], refs[arrays]
     inputs = refs[:arrays]
     outputs = refs[arrays + ahead : 2 * arrays + ahead]
     wholes = refs[2 * arrays + ahead : 2 * arrays + ahead + len(relays)]
     rest = refs[2 * arrays + ahead + len(relays) :]
     line = Line(inputs, outputs, rest[: Line.SEMAPHORES])
-    own_sem, relay_sends, relay_receives, relay_own = rest[Line.SEMAPHORES :]
+    own_sem, relay_sends, relay_receives, relay_own = rest[Line.SEMAPHORES :][:4]
+    all_sends, all_receives, all_own = rest[Line.SEMAPHORES + 4 :]
     mats, here = lax.axis_size("mat"), lax.axis_index("mat")
     me = lax.axis_index("seq")
+    devices = lax.axis_size("seq") * mats
+    number = me * mats + here
+
+    def device(other):
+        return {"seq": other // mats, "mat": other % mats}
+
+    def report(other, origin):
+        return pltpu.make_async_remote_copy(
+            src_ref=tally,
+            dst_ref=tallies.at[origin],
+            send_sem=all_sends.at[other],
+            recv_sem=all_receives.at[origin],
+            device_id=device(other),
+            device_id_type=MESH,
+        )
 
     def relayed(relay, block, origin):
         index, place = relays[relay]
@@ -948,8 +968,19 @@
         return 0
 
     barrier = pltpu.get_barrier_semaphore()
-    greeted = line.greet(barrier)
-    if relays:
+    if everyone:
+
+        def greet_all(lap, _):
+            pl.semaphore_signal(
+                barrier, inc=1, device_id=device((number + lap) % devices), device_id_type=MESH
+            )
+            return 0
+
+        lax.fori_loop(1, devices, greet_all, 0)
+        greeted = devices - 1
+    else:
+        greeted = line.greet(barrier)
+    if relays and not everyone:
 
         def greet_mat(lap, _):
             pl.semaphore_signal(
@@ -966,6 +997,15 @@
     for copy in own:
         copy.start()
     pl.semaphore_wait(barrier, greeted)
+    if everyone:
+
+        def report_all(lap, _):
+            report((number + lap) % devices, number).start()
+            return 0
+
+        lax.fori_loop(1, devices, report_all, 0)
+        own_tally = pltpu.make_async_copy(tally, tallies.at[number], all_own)
+        own_tally.start()
     line.begin()
     for copy in own:
         copy.wait()
@@ -987,9 +1027,19 @@
     line.end()
     if relays:
         lax.fori_loop(0, lax.axis_size("seq"), relay_end, 0)
-
-
-def gather_seq(values, identity, space=pltpu.VMEM, ahead=(), relays=()):
+    if everyone:
+
+        def report_end(lap, _):
+            before = (number + devices - lap) % devices
+            report(before, before).wait_recv()
+            report((number + lap) % devices, number).wait_send()
+            return 0
+
+        lax.fori_loop(1, devices, report_end, 0)
+        own_tally.wait()
+
+
+def gather_seq(values, identity, space=pltpu.VMEM, ahead=(), relays=(), everyone=()):
     peers = lax.axis_size("seq")
     mats = lax.axis_size("mat")
     plain = [value.shape for value in values]
@@ -1004,28 +1054,37 @@
     ]
     place = pl.BlockSpec(memory_space=space)
     unread = pl.BlockSpec(memory_space=pl.ANY)
-    arrays = len(values)
+    arrays, more = len(values), len(everyone)
+    shapes[arrays:arrays] = [
+        jax.ShapeDtypeStruct((peers * mats,) + value.shape, value.dtype) for value in everyone
+    ]
     results = pl.pallas_call(
-        functools.partial(gather_kernel, arrays, len(ahead), tuple(relays)),
+        functools.partial(gather_kernel, arrays, len(ahead), tuple(relays), bool(more)),
         out_shape=shapes,
-        in_specs=[place] * arrays + [unread] * len(ahead),
-        out_specs=[place] * arrays + [unread] * len(relays),
+        in_specs=[place] * (arrays + more) + [unread] * len(ahead),
+        out_specs=[place] * (arrays + more) + [unread] * len(relays),
         scratch_shapes=line_semaphores(values)
         + [
             pltpu.SemaphoreType.DMA((arrays,)),
             pltpu.SemaphoreType.DMA((max(1, len(relays)), peers)),
             pltpu.SemaphoreType.DMA((max(1, len(relays)), mats, peers)),
             pltpu.SemaphoreType.DMA((max(1, len(relays)), peers)),
+            pltpu.SemaphoreType.DMA((peers * mats,)),
+            pltpu.SemaphoreType.DMA((peers * mats,)),
+            pltpu.SemaphoreType.DMA,
         ],
         compiler_params=pltpu.CompilerParams(collective_id=identity, has_side_effects=True),
         name="gather_seq",
-    )(*values, *ahead)
+    )(*values, *everyone, *ahead)
+    results = list(results)
+    reported = results[arrays : arrays + more]
+    del results[arrays : arrays + more]
     gathered = [result.reshape((peers,) + shape) for result, shape in zip(results, plain)]
     relayed = [
         result.reshape((mats, peers) + plain[index])
         for result, (index, _) in zip(results[arrays:], relays)
     ]
-    return gathered + relayed
+    return gathered + relayed + reported
 
 
 def reduce_kernel(arrays, *refs):
@@ -1139,7 +1198,7 @@
 
 
 def lookup_kernel(
-    ids, table, small, out, smalls, found, give, got, keep, taken, passes, arrivals, sends,
+    ids, turned, small, out, smalls, table, found, give, got, keep, taken, passes, arrivals, sends,
     receives, small_sends, small_receives, small_own,
 ):
     outers, mats = taken.shape[0], taken.shape[1]
@@ -1205,6 +1264,8 @@
         return 0
 
     lax.fori_loop(1, mats, share_start, 0)
+    for first in range(0, table.shape[0], VOCAB_TILE):
+        table[first : first + VOCAB_TILE, :] = turned[:, first : first + VOCAB_TILE].T
 
     def find(block):
         def rows(index, _):
@@ -1293,10 +1354,10 @@
 
 def lookup(ids, table, small, identity):
     outers, mats = lax.axis_size("seq") // 2, lax.axis_size("mat")
-    entries, part = table.shape
-    padded = (entries // 8 + 1) * 8
+    part, entries = table.shape
+    padded = (entries // VOCAB_TILE + 1) * VOCAB_TILE
+    table = jnp.pad(table, ((0, 256 - part), (0, padded - entries)))
     table = table.astype(BF16).astype(F32)
-    table = jnp.pad(table, ((0, padded - entries), (0, 256 - part)))
     ids = jnp.where((ids >= 0) & (ids < entries), ids, entries)
     vmem = pl.BlockSpec(memory_space=pltpu.VMEM)
     blocks = pltpu.VMEM((outers, mats, 384, 128), BF16)
@@ -1309,6 +1370,7 @@
         in_specs=[pl.BlockSpec(memory_space=pltpu.SMEM), vmem, vmem],
         out_specs=[vmem, vmem],
         scratch_shapes=[
+            pltpu.VMEM((padded, 256), F32),
             pltpu.VMEM((mats * 256, 256), F32),
             blocks,
             blocks,
@@ -1708,14 +1770,14 @@
     x1_grad = x2_grad + more
 
     x1_grad_low = x1_grad.astype(BF16)
-    up_grad, down_grad = hold([up_grad, down_grad], [s_table, x1_grad_low])
-    s_up = scatter_mat(up_grad, 2)
-    s_down = scatter_mat(down_grad, 1)
     mixed_grad = dot(x1_grad_low, w_out, 1, 1).reshape(micros, tokens, inner)
     out_weight_grad = dot(mixed_low, x1_grad_low, 0, 0)
     y_grad = mixed_grad * z_silu
     z_grad = mixed_grad * core * silu_back(z)
     out_weight_grad = out_weight_grad.astype(BF16)
+    up_grad, down_grad = hold([up_grad, down_grad], [s_table, out_weight_grad])
+    s_up = scatter_mat(up_grad, 2)
+    s_down = scatter_mat(down_grad, 1)
     s_out = scatter_mat(out_weight_grad, 0)
     starts_all = gather_seq(
         [scan_start(keeping, dt, y_grad, readout, rate, [out_weight_grad, up_grad, down_grad])], 9
@@ -2055,7 +2117,7 @@
     ids = ids.reshape(mats, micros, seq_count, tokens)
     ids = ids.transpose(2, 0, 1, 3).reshape(-1) - lax.axis_index("seq") * vocab_part
     parts = [x_project, step_project, router_weight, channel_param, norm_gains]
-    found, small = lookup(ids, embedding, pack_small(parts), 10)
+    found, small = lookup(ids, embedding.T, pack_small(parts), 10)
     found, w_table, w_out, w_up, w_down = lax.optimization_barrier(
         (
             found,
@@ -2152,14 +2214,14 @@
     squares = squares + jnp.sum(table_squares[0])
     tallies = jnp.stack([squares, loss_part, count_part])
     tallies = jnp.broadcast_to(jnp.pad(tallies, (0, 5))[:, None], (8, 128))
-    g_in, g_out, packed, totals, whole_in, whole_out = gather_seq(
-        [s_in.astype(BF16), s_out.astype(BF16), packed, tallies],
+    g_in, g_out, packed, whole_in, whole_out, totals = gather_seq(
+        [s_in.astype(BF16), s_out.astype(BF16), packed.astype(BF16)],
         15,
         relays=[(0, IN_PLACE), (1, OUT_PLACE)],
+        everyone=[tallies],
     )
     g_in = g_in.reshape(-1, D).astype(F32)
     g_out = g_out.reshape(-1, D).astype(F32)
-    totals = exchange([jnp.sum(totals, axis=0)], [True], 11, ("mat",))[0]
     totals = jnp.sum(totals[:, :, 0], axis=0)
     squares, loss_total, loss_count = totals[0], totals[1], totals[2]
     grad_norm = jnp.sqrt(squares)
@@ -2176,7 +2238,7 @@
         whole_out.reshape(mats, -1, D),
     )
     packed, ortho = lax.optimization_barrier((packed, ortho))
-    packed = packed.reshape(-1)
+    packed = packed.reshape(-1).astype(F32)
     shards, offset = [], 0
     for piece, like in zip(
         pieces, (x_project, step_project, router_weight, channel_param, norm_gains)
@@ -2187,16 +2249,16 @@
         scale, g_table, embedding.T, embedding_mom.T, embedding_sq.T, ortho
     )
     table_new = [values.T for values in table_new]
-    ortho = lax.all_to_all(ortho, "mat", split_axis=0, concat_axis=0, tiled=True).astype(F32)
+    ortho = lax.all_to_all(ortho, "mat", split_axis=0, concat_axis=0, tiled=True)
     shrink = 1.0 - LR_MUON * DECAY_MUON
-    new_up = expert_up * shrink - LR_MUON * 0.2 * math.sqrt(max(D, FF)) * ortho[UP_PLACE][None]
-    new_in = in_project * shrink - LR_MUON * 0.2 * math.sqrt(max(D, 2 * DI)) * ortho[IN_PLACE]
+    new_up = expert_up * shrink - LR_MUON * 0.2 * math.sqrt(max(D, FF)) * ortho[UP_PLACE][None].astype(F32)
+    new_in = in_project * shrink - LR_MUON * 0.2 * math.sqrt(max(D, 2 * DI)) * ortho[IN_PLACE].astype(F32)
     new_down = (
-        expert_down * shrink - LR_MUON * 0.2 * math.sqrt(max(D, FF)) * ortho[DOWN_PLACE][None]
+        expert_down * shrink - LR_MUON * 0.2 * math.sqrt(max(D, FF)) * ortho[DOWN_PLACE][None].astype(F32)
     )
     new_out = (
         out_project * shrink
-        - LR_MUON * 0.2 * math.sqrt(max(D, DI)) * ortho[OUT_PLACE, : out_project.shape[0]]
+        - LR_MUON * 0.2 * math.sqrt(max(D, DI)) * ortho[OUT_PLACE, : out_project.shape[0]].astype(F32)
     )
     x_new = adamw_update(x_project, x_project_mom, x_project_sq, shards[0] * scale, 0.06, 0.1)
     step_new = adamw_update(

time: 881 us -> 873 us (level)
    pallas_call x7 -> x6, Pallas kernels: 96.4 us -> 84.2 us  [exchange(): pl.pallas_call(functools.partial(exchange_kernel, tuple(groups), tuple(ga...]
    all_to_all x1, starting transfers between devices: 5.45 us -> 14.3 us  [local(): lax.all_to_all(ortho, 'mat', split_axis=0, concat_axis=0, tiled=True)]
    unnamed x339 -> x347, local copies, waits for them, and re-layouts: 53.3 us -> 53.8 us
  transfers between devices with their start and end apart: 15 -> 15, of which waited for: 3 -> 4; matrix products, arithmetic and copies ran while one was open for 16% -> 15% of each run, Pallas kernels for 46% -> 47%
where the time goes in v3:
time: 873 us; the launch traced here: 864 us
  Pallas kernels  576 us (66%)
  local copies, waits for them, and re-layouts  96.3 us (11%)
  other arithmetic  74.7 us (9%)
  waiting for transfers between devices  39.1 us (4%)
  starting transfers between devices  28.1 us (3%)
  matrix products  28 us (3%)
  between operations  21.4 us (2%)
    pallas_call x4, Pallas kernels, gather_seq(): pl.pallas_call(functools.partial(gather_kernel, arrays, len(ahead), tuple...  101 us
    pallas_call x6, Pallas kernels, exchange(): pl.pallas_call(functools.partial(exchange_kernel, tuple(groups), tuple(ga...  84.2 us
    pallas_call x1, Pallas kernels, scatter_rows(): pl.pallas_call(functools.partial(scatter_rows_kernel, entries), out_shape...  63.6 us
    pallas_call x1, Pallas kernels, orthogonalize(): pl.pallas_call(ortho_kernel, out_shape=jax.ShapeDtypeStruct(experts.shape...  61.7 us
    pallas_call x1, Pallas kernels, lookup(): pl.pallas_call(lookup_kernel, out_shape=[jax.ShapeDtypeStruct((mats, 384,...  56.7 us
    unnamed x347, local copies, waits for them, and re-layouts  53.8 us
    pallas_call x2, Pallas kernels, reduce_seq(): pl.pallas_call(body, out_shape=[jax.ShapeDtypeStruct(shape, BF16) for sha...  42.4 us
    pallas_call x1, Pallas kernels, scan_backward(): pl.pallas_call(body, grid=(micros, inner // LANES), in_specs=[scalars, sc...  30.9 us
  transfers between devices with their start and end apart: 15, of which 4 were waited for; matrix products, arithmetic and copies ran while one was open for 15% of the time, Pallas kernels for 47%

profile of v3, /device:TPU:0, one launch (start us, length us, event | category | flops | bytes accessed | tf_op | source)
XLA Modules:
  0.0 864.0 jit_solution(15607499927559214413)
XLA Ops:
  10.2 6.0 exchange.6
  35.9 56.7 %lookup.1 = (bf16[4,384,128]{2,1,0:T(8,128)(2,1)}, bf16[4,64,1024]{2,1,0:T(8,128)(2,1)}) custom-call(s32[8192]{0:T(1024)} %and_select_fusion.ids, f32[256,6400]{1,0:T(8,128)} %pad_convert_fusion.turned, bf16[64,1024]{1,0:T(8,128)(2,1)} %reshape.522.small), custom_call_target="tpu_custom_call" | custom-call | tf_op jit(solution)/shard_map/lookup/pallas_call | solution.py:1364
  114.7 5.8 mixer_conv.1
  124.3 14.6 %scan_end.1 = (f32[2,128,1536]{2,1,0:T(8,128)S(1)}, f32[2,128,1536]{2,1,0:T(8,128)S(1)}, bf16[32,1536]{1,0:T(8,128)(2,1)S(1)}, f32[8,1536]{1,0:T(8,128)S(1)}) custom-call(f32[2,128]{1,0:T(2,128)S(1)} %fusion.47.keep.refs_1_, f32[2,128,80]{2,1,0:T(8,128)S(1)} %get-tuple-element.94.projected, bf16[48,1536]{1,0:T(8,128)(2,1)S(1)} %bitcast.275, ...), custom_call_target="tpu_custom_call" | custom-call | tf_op jit(solution)/shard_map/scan_end/pallas_call | solution.py:373
  141.4 24.9 %gather_seq.4 = (bf16[8,2,16,1536]{3,2,1,0:T(8,128)(2,1)}, f32[8,1,8,1536]{3,2,1,0:T(8,128)}) custom-call(bf16[2,16,1536]{2,1,0:T(8,128)(2,1)} %bitcast.280, f32[1,8,1536]{2,1,0:T(8,128)} %bitcast.281), custom_call_target="tpu_custom_call" | custom-call | tf_op jit(solution)/shard_map/gather_seq/pallas_call | solution.py:1061
  170.1 18.2 %scan_forward.1 = (f32[2,128,1536]{2,1,0:T(8,128)S(1)}, f32[2,128,16,1536]{3,2,1,0:T(8,128)}, f32[2,16,1536]{2,1,0:T(8,128)S(1)}) custom-call(s32[1]{0:T(128)} %bitcast.12.place.refs_0_, f32[2,128]{1,0:T(2,128)S(1)} %fusion.47.keep.refs_1_, f32[2,128,1536]{2,1,0:T(8,128)S(1)} %get-tuple-element.95.dt.refs_2_, ...), custom_call_target="tpu_custom_call" | custom-call | tf_op jit(solution)/shard_map/scan_forward/pallas_call | solution.py:404
  196.1 15.8 %exchange.7 = bf16[8,64,768]{2,1,0:T(8,128)(2,1)} custom-call(bf16[8,64,768]{2,1,0:T(8,128)(2,1)} %bitcast.299), custom_call_target="tpu_custom_call" | custom-call | tf_op jit(solution)/shard_map/exchange/pallas_call | solution.py:749
  213.1 12.8 %experts.1 = (bf16[1,512,3072]{2,1,0:T(8,128)(2,1)S(1)}, f32[1,512,3072]{2,1,0:T(8,128)}, bf16[1,512,768]{2,1,0:T(8,128)(2,1)S(1)}) custom-call(bf16[1,512,768]{2,1,0:T(8,128)(2,1)S(1)} %bitcast.250, bf16[1,768,3072]{2,1,0:T(8,128)(2,1)} %all-gather.10.cloned.1.call-done.w_up, bf16[1,3072,768]{2,1,0:T(8,128)(2,1)} %all-gather.12.cloned.1.call-done.w_down), custom_call_target="tpu_custom_call" | custom-call | tf_op jit(solution)/shard_map/experts/pallas_call | solution.py:519
  228.4 20.7 %exchange.8 = bf16[8,64,768]{2,1,0:T(8,128)(2,1)} custom-call(bf16[8,64,768]{2,1,0:T(8,128)(2,1)} %bitcast.273), custom_call_target="tpu_custom_call" | custom-call | tf_op jit(solution)/shard_map/exchange/pallas_call | solution.py:749
  253.8 21.6 %gather_seq.5 = bf16[8,2,32,768]{3,2,1,0:T(8,128)(2,1)} custom-call(bf16[2,32,768]{2,1,0:T(8,128)(2,1)} %convolution_convert_fusion.5.refs_0_), custom_call_target="tpu_custom_call" | custom-call | tf_op jit(solution)/shard_map/gather_seq/pallas_call | solution.py:1061
  278.0 15.5 %head.1 = (f32[512,6288]{1,0:T(8,128)}, f32[512,8]{1,0:T(8,128)S(1)}) custom-call(s32[3]{0:T(128)S(1)} %pad_add_fusion.limits, bf16[512,768]{1,0:T(8,128)(2,1)S(1)} %bitcast.253, bf16[768,6288]{1,0:T(8,128)(2,1)} %all-gather.14.cloned.1.call-done.table, s32[512,1]{1,0:T(8,128)S(1)} %copy-done.24), custom_call_target="tpu_custom_call" | custom-call | tf_op jit(solution)/shard_map/head/pallas_call | solution.py:634
  294.2 8.4 exchange.9
  304.6 20.1 %head_back.1 = (bf16[768,6288]{1,0:T(8,128)(2,1)}, bf16[512,768]{1,0:T(8,128)(2,1)S(1)}) custom-call(s32[3]{0:T(128)S(1)} %pad_add_fusion.limits, bf16[768,512]{1,0:T(8,128)(2,1)S(1)} %bitcast.257, bf16[768,6288]{1,0:T(8,128)(2,1)} %all-gather.14.cloned.1.call-done.table, s32[512,1]{1,0:T(8,128)S(1)} %copy-done.24, f32[512,8]{1,0:T(8,128)S(1)} %pad.37.scalars, ...), custom_call_target="tpu_custom_call" | custom-call | tf_op jit(solution)/shard_map/head_back/pallas_call | solution.py:652
  326.8 12.9 %reduce_seq.2 = bf16[4,64,768]{2,1,0:T(8,128)(2,1)S(1)} custom-call(bf16[8,64,768]{2,1,0:T(8,128)(2,1)S(1)} %bitcast.272), custom_call_target="tpu_custom_call" | custom-call | tf_op jit(solution)/shard_map/reduce_seq/pallas_call | solution.py:1185
  344.4 14.3 %exchange.10 = bf16[8,64,768]{2,1,0:T(8,128)(2,1)} custom-call(bf16[8,64,768]{2,1,0:T(8,128)(2,1)} %bitcast.296, bf16[768,6288]{1,0:T(8,128)(2,1)} %get-tuple-element.109.refs_1_), custom_call_target="tpu_custom_call" | custom-call | tf_op jit(solution)/shard_map/exchange/pallas_call | solution.py:749
  361.8 17.3 %experts_back.1 = (bf16[1,768,3072]{2,1,0:T(8,128)(2,1)}, bf16[1,3072,768]{2,1,0:T(8,128)(2,1)}, bf16[1,512,768]{2,1,0:T(8,128)(2,1)S(1)}) custom-call(bf16[1,512,768]{2,1,0:T(8,128)(2,1)S(1)} %bitcast.251, bf16[1,512,768]{2,1,0:T(8,128)(2,1)S(1)} %bitcast.256, bf16[1,768,3072]{2,1,0:T(8,128)(2,1)} %all-gather.10.cloned.1.call-done.w_up, ...), custom_call_target="tpu_custom_call" | custom-call | tf_op jit(solution)/shard_map/experts_back/pallas_call | solution.py:538
  379.9 19.0 %exchange.11 = bf16[8,64,768]{2,1,0:T(8,128)(2,1)} custom-call(bf16[8,64,768]{2,1,0:T(8,128)(2,1)} %bitcast.271, bf16[768,6288]{1,0:T(8,128)(2,1)} %get-tuple-element.109.refs_1_), custom_call_target="tpu_custom_call" | custom-call | tf_op jit(solution)/shard_map/exchange/pallas_call | solution.py:749
  404.1 6.8 reduce-scatter.6.cloned.1.call-done.refs_2_
  420.3 5.4 all-to-all-start
  442.1 7.6 scan_start.1
  450.4 19.2 %gather_seq.6 = bf16[8,2,16,1536]{3,2,1,0:T(8,128)(2,1)} custom-call(bf16[2,16,1536]{2,1,0:T(8,128)(2,1)} %bitcast.277), custom_call_target="tpu_custom_call" | custom-call | tf_op jit(solution)/shard_map/gather_seq/pallas_call | solution.py:1061
  473.5 30.9 %scan_backward.1 = (f32[2,128,1536]{2,1,0:T(8,128)S(1)}, f32[2,128,1536]{2,1,0:T(8,128)S(1)}, f32[2,128,16,128]{3,2,1,0:T(8,128)}, f32[2,128,16,128]{3,2,1,0:T(8,128)}, f32[2,16,1536]{2,1,0:T(8,128)S(1)}) custom-call(s32[1]{0:T(128)} %bitcast.12.place.refs_0_, f32[2,128]{1,0:T(2,128)S(1)} %fusion.47.keep.refs_1_, f32[2,128,1536]{2,1,0:T(8,128)} %copy-done.4, ...), custom_call_target="tpu_custom_call" | custom-call | tf_op jit(solution)/shard_map/scan_backward/pallas_call | solution.py:448
  511.2 7.4 mixer_conv_back.1
  553.9 7.7 all-to-all-done.1
  566.0 63.6 %scatter_rows.1 = (f32[6400,256]{1,0:T(8,128)}, f32[8,256]{1,0:T(8,128)S(1)}, bf16[4,768,768]{2,1,0:T(8,128)(2,1)}) custom-call(s32[64,128]{1,0:T(8,128)S(1)} %bitcast.279, bf16[4,384,128]{2,1,0:T(8,128)(2,1)S(1)} %slice.200.rows, bf16[192,6400]{1,0:T(8,128)(2,1)S(1)} %copy-done.6, bf16[768,768]{1,0:T(8,128)(2,1)S(1)} %bitcast.254, ...), custom_call_target="tpu_custom_call" | custom-call | tf_op jit(solution)/shard_map/scatter_rows/pallas_call | solution.py:1551
  633.7 29.5 %reduce_seq.3 = (bf16[4,96,768]{2,1,0:T(8,128)(2,1)S(1)}, bf16[4,48,768]{2,1,0:T(8,128)(2,1)S(1)}, bf16[4,64,128]{2,1,0:T(8,128)(2,1)S(1)}) custom-call(bf16[8,96,768]{2,1,0:T(8,128)(2,1)S(1)} %bitcast.269, bf16[8,48,768]{2,1,0:T(8,128)(2,1)S(1)} %bitcast.274, bf16[8,64,128]{2,1,0:T(8,128)(2,1)S(1)} %bitcast.276, f32[6400,256]{1,0:T(8,128)} %get-tuple-element.130.refs_3_.grad), custom_call_target="tpu_custom_call" | custom-call | tf_op jit(solution)/shard_map/reduce_seq/pallas_call | solution.py:1185
  671.7 35.7 %gather_seq.7 = (bf16[8,2,48,768]{3,2,1,0:T(8,128)(2,1)}, bf16[8,1,48,768]{3,2,1,0:T(8,128)(2,1)}, bf16[8,2,32,128]{3,2,1,0:T(8,128)(2,1)}, f32[32,8,128]{2,1,0:...) custom-call(bf16[2,48,768]{2,1,0:T(8,128)(2,1)} %bitcast.329, ...), custom_call_target="tpu_custom_call" | custom-call | tf_op jit(solution)/shard_map/gather_seq/pallas_call | solution.py:1061
  709.8 61.7 %orthogonalize.1._ahead = bf16[4,768,768]{2,1,0:T(8,128)(2,1)} custom-call(s32[1]{0:T(128)} %bitcast.107.place, f32[1]{0:T(128)} %bitcast.103.scale, bf16[4,768,768]{2,1,0:T(8,128)(2,1)} %all-to-all-done.moments, bf16[4,768,768]{2,1,0:T(8,128)(2,1)} %get-tuple-element.138.experts, bf16[4,768,768]{2,1,0:T(8,128)(2,1)} %bitcast.294, bf16[4,384,768]{2,1,0:T(8,128)(2,1)} %bitcast.306), custom_call_target="tpu_custom_call" | custom-call | tf_op jit(solution)/shard_map/orthogonalize/pallas_call | solution.py:2011
  775.9 14.3 %all-to-all-start.2 = ((bf16[4,768,768]{2,1,0:T(8,128)(2,1)}), bf16[4,768,768]{2,1,0:T(8,128)(2,1)}, u32[]{:S(2)}, u32[]{:S(2)}) async-start(bf16[4,768,768]{2,1,0:T(8,128)(2,1)} %orthogonalize.1._ahead), calls=%async_computation.7 | async-start | bytes 9437184 | tf_op jit(solution)/shard_map/all_to_all | solution.py:2252
  795.3 16.2 %update_table.1 = (f32[192,6288]{1,0:T(8,128)}, f32[192,6288]{1,0:T(8,128)}, f32[192,6288]{1,0:T(8,128)}) custom-call(f32[1]{0:T(128)} %bitcast.103.scale, f32[6400,256]{1,0:T(8,128)} %get-tuple-element.130.refs_3_.grad, f32[192,6288]{1,0:T(8,128)} %bitcast.285, f32[192,6288]{1,0:T(8,128)} %bitcast.292, f32[192,6288]{1,0:T(8,128)} %bitcast.293, ...), custom_call_target="tpu_custom_call" | custom-call | flops 32194560 | bytes 45072384 | tf_op jit(solution)/shard_map/update_table/pallas_call | solution.py:2054
  823.9 20.2 %all-to-all-done.2 = bf16[4,768,768]{2,1,0:T(8,128)(2,1)} async-done(((bf16[4,768,768]{2,1,0:T(8,128)(2,1)}), bf16[4,768,768]{2,1,0:T(8,128)(2,1)}, u32[]{:S(2)}, u32[]{:S(2)}) %all-to-all-start.2) | async-done | bytes 4718624 | tf_op jit(solution)/shard_map/all_to_all | solution.py:2252
  844.1 6.1 multiply_subtract_fusion
  (590 shorter events, 205.7 us)
Async XLA Ops:
  7.3 92.7 %all-gather.6.cloned.1.call-start = ((), (), s32[]{:S(2)}) async-start(), calls=%async_computation.8 | async-start | bytes 5898240 | tf_op jit(solution)/shard_map/all_gather | solution.py:2133
  10.2 181.4 %all-gather.8.cloned.1.call-start = ((), (), s32[]{:S(2)}) async-start(), calls=%async_computation.9 | async-start | bytes 2949120 | tf_op jit(solution)/shard_map/all_gather | solution.py:2134
  92.7 119.2 %all-gather.10.cloned.1.call-start = ((), (), s32[]{:S(2)}) async-start(), calls=%async_computation.10 | async-start | bytes 5898240 | tf_op jit(solution)/shard_map/all_gather | solution.py:2135
  93.4 118.5 %all-gather.12.cloned.1.call-start = ((), (), s32[]{:S(2)}) async-start(), calls=%async_computation.11 | async-start | bytes 5898240 | tf_op jit(solution)/shard_map/all_gather | solution.py:2136
  94.0 182.8 %all-gather.14.cloned.1.call-start = ((), (), s32[]{:S(2)}) async-start(), calls=%async_computation.12 | async-start | bytes 12288000 | tf_op jit(solution)/shard_map/all_gather | solution.py:2132
  94.6 316.3 %reduce-scatter.6.cloned.1.call-start = ((), (), s32[]{:S(2)}) async-start(), calls=%async_computation.13 | async-start | bytes 12288000 | tf_op jit(solution)/shard_map/reduce_scatter | solution.py:1838
  103.8 10.9 %collective-permute-start = (f32[2,3,1536]{2,1,0:T(4,128)S(1)}, f32[2,3,1536]{2,1,0:T(4,128)S(1)}, u32[]{:S(2)}, u32[]{:S(2)}) collective-permute-start(f32[2,3,1536]{2,1,0:T(4,128)S(1)} %slice.182), channel_id=1, source_target_pairs={{0,4},{4,8},{8,12},{12,16},{16,20},{20,24},{24,28},{1,5},{5,9},{9,... | collective-permute-start | bytes 110600 | tf_op jit(solution)/shard_map/ppermute | solution.py:1583
  121.6 310.8 %copy-start = (f32[2,128,1536]{2,1,0:T(8,128)}, f32[2,128,1536]{2,1,0:T(8,128)S(1)}, u32[]{:S(2)}) copy-start(f32[2,128,1536]{2,1,0:T(8,128)S(1)} %get-tuple-element.93.act.refs_3_) | copy-start | bytes 4718596
  141.4 47.0 %copy-start.4 = (f32[2,128,1536]{2,1,0:T(8,128)}, f32[2,128,1536]{2,1,0:T(8,128)S(1)}, u32[]{:S(2)}) copy-start(f32[2,128,1536]{2,1,0:T(8,128)S(1)} %get-tuple-element.95.dt.refs_2_) | copy-start | bytes 4718596
  170.1 20.0 %copy-start.58 = (f32[2,128,3072]{2,1,0:T(8,128)S(1)}, f32[2,128,3072]{2,1,0:T(8,128)}, u32[]{:S(2)}) copy-start(f32[2,128,3072]{2,1,0:T(8,128)} %copy-done.57) | copy-start | bytes 9437188
  170.1 20.0 %copy-start.113 = (f32[1536]{0:T(1024)S(1)}, f32[1536]{0:T(1024)}, u32[]{:S(2)}) copy-start(f32[1536]{0:T(1024)} %mul.596) | copy-start | bytes 18436
  194.5 57.0 %copy-start.60 = (f32[256,768]{1,0:T(8,128)}, f32[256,768]{1,0:T(8,128)S(1)}, u32[]{:S(2)}) copy-start(f32[256,768]{1,0:T(8,128)S(1)} %get-tuple-element.360) | copy-start | bytes 2359300
  194.6 55.7 %copy-start.85 = (bf16[256,768]{1,0:T(8,128)(2,1)}, bf16[256,768]{1,0:T(8,128)(2,1)S(1)}, u32[]{:S(2)}) copy-start(bf16[256,768]{1,0:T(8,128)(2,1)S(1)} %multiply_convert_fusion.4) | copy-start | bytes 1179652
  228.4 21.9 %copy-start.91 = (bf16[768,8]{1,0:T(8,128)(2,1)S(1)}, bf16[768,8]{1,0:T(8,128)(2,1)}, u32[]{:S(2)}) copy-start(bf16[768,8]{1,0:T(8,128)(2,1)} %reshape_reshape.18) | copy-start | bytes 36868
  228.4 21.9 %copy-start.120 = (s32[2,1,128,1]{2,3,1,0:T(1,128)S(1)}, s32[2,1,128,1]{2,3,1,0:T(1,128)}, u32[]{:S(2)}) copy-start(s32[2,1,128,1]{2,3,1,0:T(1,128)} %param.33) | copy-start | bytes 3076
  228.4 22.8 %copy-start.129 = (s32[2,128]{1,0:T(2,128)S(1)}, s32[2,128]{1,0:T(2,128)}, u32[]{:S(2)}) copy-start(s32[2,128]{1,0:T(2,128)} %add_add_fusion) | copy-start | bytes 3076
  251.8 25.0 %copy-start.24 = (s32[512,1]{1,0:T(8,128)S(1)}, s32[512,1]{1,0:T(8,128)}, u32[]{:S(2)}) copy-start(s32[512,1]{1,0:T(8,128)} %broadcast_in_dim_reshape.5.targets) | copy-start | bytes 6148
  278.0 26.4 %copy-start.149 = (f32[512,1]{0,1:T(1,128)S(1)}, f32[512,1]{0,1:T(1,128)}, u32[]{:S(2)}) copy-start(f32[512,1]{0,1:T(1,128)} %div.135) | copy-start | bytes 6148
  325.7 236.0 %reduce-scatter.12.cloned.1.call-start = ((), (), s32[]{:S(2)}) async-start(), calls=%async_computation.16 | async-start | bytes 5898240 | tf_op jit(solution)/shard_map/reduce_scatter | solution.py:1838
  379.9 20.3 %copy-start.143 = (f32[256]{0:T(256)S(1)}, f32[256]{0:T(256)}, u32[]{:S(2)}) copy-start(f32[256]{0:T(256)} %copy-done.142) | copy-start | bytes 3076
  379.9 20.3 %copy-start.155 = (f32[256]{0:T(256)S(1)}, f32[256]{0:T(256)}, u32[]{:S(2)}) copy-start(f32[256]{0:T(256)} %get-tuple-element.332) | copy-start | bytes 3076
  379.9 20.4 %copy-start.131 = (s32[2,128]{1,0:T(2,128)S(1)}, s32[2,128]{1,0:T(2,128)}, u32[]{:S(2)}) copy-start(s32[2,128]{1,0:T(2,128)} %add_add_fusion) | copy-start | bytes 3076
  401.9 27.9 %copy-start.62 = (f32[256,768]{1,0:T(8,128)}, f32[256,768]{1,0:T(8,128)S(1)}, u32[]{:S(2)}) copy-start(f32[256,768]{1,0:T(8,128)S(1)} %multiply_add_fusion.3) | copy-start | bytes 2359300
  410.9 150.8 %reduce-scatter.14.cloned.1.call-start = ((), (), s32[]{:S(2)}) async-start(), calls=%async_computation.17 | async-start | bytes 5898240 | tf_op jit(solution)/shard_map/reduce_scatter | solution.py:1838
  411.7 218.6 %reduce-scatter.10.cloned.1.call-start = ((), (), s32[]{:S(2)}) async-start(), calls=%async_computation.15 | async-start | bytes 2949120 | tf_op jit(solution)/shard_map/reduce_scatter | solution.py:1838
  420.3 121.1 %all-to-all-start = ((bf16[4,768,768]{2,1,0:T(8,128)(2,1)}), bf16[4,768,768]{2,1,0:T(8,128)(2,1)}, u32[]{:S(2)}, u32[]{:S(2)}) async-start(bf16[4,768,768]{2,1,0:T(8,128)(2,1)} %pad_maximum_fusion), calls=%async_computation.3 | async-start | bytes 9437184 | tf_op jit(solution)/shard_map/all_to_all | solution.py:2157
  425.6 205.7 %reduce-scatter.8.cloned.1.call-start = ((), (), s32[]{:S(2)}) async-start(), calls=%async_computation.14 | async-start | bytes 5898240 | tf_op jit(solution)/shard_map/reduce_scatter | solution.py:1838
  473.5 30.9 %copy-start.33 = (f32[2,128,1536]{2,1,0:T(8,128)S(1)}, f32[2,128,1536]{2,1,0:T(8,128)}, u32[]{:S(2)}) copy-start(f32[2,128,1536]{2,1,0:T(8,128)} %copy-done.32) | copy-start | bytes 4718596
  519.8 7.3 collective-permute-start.1
  544.6 17.0 %all-to-all-start.1 = ((bf16[4,896,128]{2,1,0:T(8,128)(2,1)}), bf16[4,896,128]{2,1,0:T(8,128)(2,1)S(1)}, u32[]{:S(2)}, u32[]{:S(2)}) async-start(bf16[4,896,128]{2,1,0:T(8,128)(2,1)} %pad_maximum_fusion.2), calls=%async_computation.4 | async-start | bytes 1835008 | tf_op jit(solution)/shard_map/all_to_all | solution.py:2186
  709.8 61.7 %copy-start.101 = (bf16[8,2,32,128]{3,2,1,0:T(8,128)(2,1)S(1)}, bf16[8,2,32,128]{3,2,1,0:T(8,128)(2,1)}, u32[]{:S(2)}) copy-start(bf16[8,2,32,128]{3,2,1,0:T(8,128)(2,1)} %get-tuple-element.136) | copy-start | bytes 393220
  775.9 68.2 %all-to-all-start.2 = ((bf16[4,768,768]{2,1,0:T(8,128)(2,1)}), bf16[4,768,768]{2,1,0:T(8,128)(2,1)}, u32[]{:S(2)}, u32[]{:S(2)}) async-start(bf16[4,768,768]{2,1,0:T(8,128)(2,1)} %orthogonalize.1._ahead), calls=%async_computation.7 | async-start | bytes 9437184 | tf_op jit(solution)/shard_map/all_to_all | solution.py:2252
  (145 other events, 757.1 us)
Sparse Core Ops, SparseCore 0:
  10.3 43.4 all-gather.5
  92.8 27.7 all-gather.7
  122.7 37.4 all-gather.9
  162.2 37.4 all-gather.11
  201.7 66.4 all-gather.13
  325.8 85.0 reduce-scatter.5
  414.0 73.2 reduce-scatter.11
  490.6 47.8 reduce-scatter.13
  541.5 33.9 reduce-scatter.9
  578.6 52.6 reduce-scatter.7

commit v4 on v3

--- a/solution.py
+++ b/solution.py
@@ -1087,7 +1087,26 @@
     return gathered + relayed + reported
 
 
-def reduce_kernel(arrays, *refs):
+def reduce_kernel(arrays, riders, *refs):
+    rides = [refs[index : index + 5] for index in range(0, 5 * riders, 5)]
+    refs = refs[5 * riders :]
+    mats, here = lax.axis_size("mat"), lax.axis_index("mat")
+
+    def ride(refs, place, origin):
+        source, target, ride_sends, ride_receives, _ = refs
+        return pltpu.make_async_remote_copy(
+            src_ref=source.at[place],
+            dst_ref=target.at[origin],
+            send_sem=ride_sends.at[place],
+            recv_sem=ride_receives.at[origin],
+            device_id={"mat": place},
+            device_id_type=MESH,
+        )
+
+    def stay(refs):
+        source, target, _, _, ride_own = refs
+        return pltpu.make_async_copy(source.at[here], target.at[here], ride_own)
+
     inputs, outputs = refs[:arrays], refs[arrays : 2 * arrays]
     got, keep = refs[2 * arrays : 3 * arrays], refs[3 * arrays : 4 * arrays]
     passes, arrivals, sends, receives = refs[4 * arrays :]
@@ -1129,7 +1148,23 @@
 
     pl.semaphore_signal(barrier, inc=1, device_id=partner, device_id_type=MESH)
     lax.fori_loop(1, outers, greet, 0)
-    pl.semaphore_wait(barrier, outers)
+    def greet_mat(lap, _):
+        pl.semaphore_signal(
+            barrier, inc=1, device_id={"mat": (here + lap) % mats}, device_id_type=MESH
+        )
+        return 0
+
+    if riders:
+        lax.fori_loop(1, mats, greet_mat, 0)
+    pl.semaphore_wait(barrier, outers + (mats - 1 if riders else 0))
+    for one in rides:
+        stay(one).start()
+
+        def set_off(lap, _):
+            ride(one, (here + lap) % mats, here).start()
+            return 0
+
+        lax.fori_loop(1, mats, set_off, 0)
 
     def begin(lap, _):
         for index in range(arrays):
@@ -1170,36 +1205,71 @@
         return 0
 
     lax.fori_loop(0, outers, end, 0)
-
-
-def reduce_seq(values, identity, ahead=()):
+    for one in rides:
+        stay(one).wait()
+
+        def arrive(lap, _):
+            before = (here + mats - lap) % mats
+            ride(one, before, before).wait_recv()
+            ride(one, (here + lap) % mats, here).wait_send()
+            return 0
+
+        lax.fori_loop(1, mats, arrive, 0)
+
+
+def reduce_seq(values, identity, ahead=(), riders=()):
     outers = lax.axis_size("seq") // 2
     arrays = len(values)
     shapes = [(outers,) + value.shape[1:] for value in values]
     place = pl.BlockSpec(memory_space=pltpu.VMEM)
     unread = pl.BlockSpec(memory_space=pl.ANY)
 
+    count, mats = len(riders), lax.axis_size("mat")
+    first = arrays + count + len(ahead)
+
     def body(*refs):
-        reduce_kernel(arrays, *refs[:arrays], *refs[arrays + len(ahead) :])
+        sources = refs[arrays : arrays + count]
+        targets = refs[first + arrays : first + arrays + count]
+        rest = refs[first + arrays + count :]
+        rides = []
+        for index in range(count):
+            rides += [sources[index], targets[index], *rest[3 * index : 3 * index + 3]]
+        reduce_kernel(
+            arrays,
+            count,
+            *rides,
+            *refs[:arrays],
+            *refs[first : first + arrays],
+            *rest[3 * count :],
+        )
 
     results = pl.pallas_call(
         body,
-        out_shape=[jax.ShapeDtypeStruct(shape, BF16) for shape in shapes],
-        in_specs=[place] * arrays + [unread] * len(ahead),
-        out_specs=[place] * arrays,
-        scratch_shapes=[pltpu.VMEM(shape, BF16) for shape in shapes * 2]
+        out_shape=[jax.ShapeDtypeStruct(shape, BF16) for shape in shapes]
+        + [jax.ShapeDtypeStruct(rider.shape, rider.dtype) for rider in riders],
+        in_specs=[place] * arrays + [unread] * (count + len(ahead)),
+        out_specs=[place] * arrays + [unread] * count,
+        scratch_shapes=[
+            pltpu.SemaphoreType.DMA((mats,)),
+            pltpu.SemaphoreType.DMA((mats,)),
+            pltpu.SemaphoreType.DMA,
+        ]
+        * count
+        + [pltpu.VMEM(shape, BF16) for shape in shapes * 2]
         + [pltpu.SemaphoreType.DMA((arrays, outers))] * 4,
         compiler_params=pltpu.CompilerParams(
             collective_id=identity, has_side_effects=True, vmem_limit_bytes=48 * 1024 * 1024
         ),
         name="reduce_seq",
-    )(*values, *ahead)
-    return [jnp.sum(result.astype(F32), axis=0) for result in results]
+    )(*values, *riders, *ahead)
+    sums = [jnp.sum(result.astype(F32), axis=0) for result in results[:arrays]]
+    return sums + list(results[arrays:])
 
 
 def lookup_kernel(
-    ids, turned, small, out, smalls, table, found, give, got, keep, taken, passes, arrivals, sends,
-    receives, small_sends, small_receives, small_own,
+    ids, turned, small, up_mom, in_mom, down_mom, out_mom, up, down, outward,
+    out, smalls, moments, up_low, down_low, out_low, table, found, give, got, keep, taken, passes, arrivals, sends,
+    receives, small_sends, small_receives, small_own, near, low, loads, stores,
 ):
     outers, mats = taken.shape[0], taken.shape[1]
     me = lax.axis_index("seq")
@@ -1321,6 +1391,48 @@
     hand_over(0)
     lax.fori_loop(0, outers, compute, 0)
 
+    tasks = (
+        (up, up_low),
+        (down, down_low),
+        (outward, out_low),
+        (up_mom, moments.at[UP_PLACE]),
+        (in_mom, moments.at[IN_PLACE]),
+        (down_mom, moments.at[DOWN_PLACE]),
+        (out_mom, moments.at[OUT_PLACE]),
+    )
+
+    def load(task):
+        source, slot = tasks[task][0], task % 2
+        rows = pl.ds(0, source.shape[0])
+        return pltpu.make_async_copy(source, near.at[slot, rows], loads.at[slot])
+
+    def keep_low(task):
+        target, slot = tasks[task][1], task % 2
+        rows = pl.ds(0, target.shape[0])
+        return pltpu.make_async_copy(low.at[slot, rows], target, stores.at[slot])
+
+    load(0).start()
+    for task, (source, target) in enumerate(tasks):
+        slot = task % 2
+        if task + 1 < len(tasks):
+            load(task + 1).start()
+        load(task).wait()
+        if task > 1:
+            keep_low(task - 2).wait()
+
+        def round_rows(index, _):
+            cut = pl.ds(pl.multiple_of(index * 64, 64), 64)
+            low[slot, cut, :] = near[slot, cut, :].astype(BF16)
+            return 0
+
+        lax.fori_loop(0, source.shape[0] // 64, round_rows, 0)
+        if source.shape[0] < target.shape[0]:
+            missing = target.shape[0] - source.shape[0]
+            low[slot, source.shape[0] :, :] = jnp.zeros((missing, low.shape[2]), BF16)
+        keep_low(task).start()
+    keep_low(len(tasks) - 2).wait()
+    keep_low(len(tasks) - 1).wait()
+
     def finish(lap, _):
         to_outer, to_mat = (outer + lap // mats) % outers, (here + lap % mats) % mats
         send(to_outer, to_mat, to_outer, to_mat).wait_recv()
@@ -1352,13 +1464,14 @@
         out[place] = lax.fori_loop(0, outers, gather, jnp.zeros((384, 128), F32)).astype(BF16)
 
 
-def lookup(ids, table, small, identity):
+def lookup(ids, table, small, wide, identity):
     outers, mats = lax.axis_size("seq") // 2, lax.axis_size("mat")
     part, entries = table.shape
     padded = (entries // VOCAB_TILE + 1) * VOCAB_TILE
     table = jnp.pad(table, ((0, 256 - part), (0, padded - entries)))
     table = table.astype(BF16).astype(F32)
     ids = jnp.where((ids >= 0) & (ids < entries), ids, entries)
+    unread = pl.BlockSpec(memory_space=pl.ANY)
     vmem = pl.BlockSpec(memory_space=pltpu.VMEM)
     blocks = pltpu.VMEM((outers, mats, 384, 128), BF16)
     return pl.pallas_call(
@@ -1366,9 +1479,11 @@
         out_shape=[
             jax.ShapeDtypeStruct((mats, 384, 128), BF16),
             jax.ShapeDtypeStruct((mats,) + small.shape, BF16),
+            jax.ShapeDtypeStruct((mats,) + wide[0].shape, BF16),
+            *[jax.ShapeDtypeStruct(value.shape, BF16) for value in wide[4:]],
         ],
-        in_specs=[pl.BlockSpec(memory_space=pltpu.SMEM), vmem, vmem],
-        out_specs=[vmem, vmem],
+        in_specs=[pl.BlockSpec(memory_space=pltpu.SMEM), vmem, vmem] + [unread] * len(wide),
+        out_specs=[vmem, vmem] + [unread] * 4,
         scratch_shapes=[
             pltpu.VMEM((padded, 256), F32),
             pltpu.VMEM((mats * 256, 256), F32),
@@ -1380,12 +1495,16 @@
             pltpu.SemaphoreType.DMA((mats,)),
             pltpu.SemaphoreType.DMA((mats,)),
             pltpu.SemaphoreType.DMA,
+            pltpu.VMEM((2,) + wide[0].shape, F32),
+            pltpu.VMEM((2,) + wide[0].shape, BF16),
+            pltpu.SemaphoreType.DMA((2,)),
+            pltpu.SemaphoreType.DMA((2,)),
         ],
         compiler_params=pltpu.CompilerParams(
             collective_id=identity, has_side_effects=True, vmem_limit_bytes=56 * 1024 * 1024
         ),
         name="lookup",
-    )(ids, table, small)
+    )(ids, table, small, *wide)
 
 
 def scatter_rows_kernel(
@@ -1839,7 +1958,7 @@
 
 
 def ortho_kernel(
-    place, scale, moments, experts, inward, outward, out,
+    place, scale, moments, later, experts, inward, outward, out,
     moment, grads, current, rounded, gram, low, poly, slope, trace, semaphores,
 ):
     blocks, size, _ = experts.shape
@@ -1853,8 +1972,13 @@
     def band(index):
         return pl.ds(index * tile, tile)
 
-    fetch = pltpu.make_async_copy(moments, moment, semaphores.at[0])
-    fetch.start()
+    half = moments.shape[1]
+    fetches = [
+        pltpu.make_async_copy(moments, moment.at[:, pl.ds(0, half)], semaphores.at[0]),
+        pltpu.make_async_copy(later, moment.at[:, pl.ds(half, half)], semaphores.at[1 + blocks]),
+    ]
+    for fetch in fetches:
+        fetch.start()
 
     @pl.when(jnp.logical_or(place[0] == UP_PLACE, place[0] == DOWN_PLACE))
     def _():
@@ -1883,7 +2007,8 @@
         for copy in copies:
             copy.wait()
 
-    fetch.wait()
+    for fetch in fetches:
+        fetch.wait()
     trace[...] = jnp.zeros_like(trace)
 
     def load(lap, _):
@@ -2002,7 +2127,7 @@
     lax.fori_loop(0, blocks * tiles, store, 0)
 
 
-def orthogonalize(scale, moments, experts, inward, outward):
+def orthogonalize(scale, moments, later, experts, inward, outward):
     blocks, size, width = experts.shape
     vmem = pl.BlockSpec(memory_space=pltpu.VMEM)
     smem = pl.BlockSpec(memory_space=pltpu.SMEM)
@@ -2011,7 +2136,7 @@
     return pl.pallas_call(
         ortho_kernel,
         out_shape=jax.ShapeDtypeStruct(experts.shape, BF16),
-        in_specs=[smem, smem] + [unread] * 4,
+        in_specs=[smem, smem] + [unread] * 5,
         out_specs=vmem,
         scratch_shapes=[
             pltpu.VMEM((blocks, size, width), BF16),
@@ -2023,11 +2148,11 @@
             pltpu.VMEM((size, size), BF16),
             pltpu.VMEM((size, 128), F32),
             pltpu.VMEM((1, size), F32),
-            pltpu.SemaphoreType.DMA((1 + blocks,)),
+            pltpu.SemaphoreType.DMA((2 + blocks,)),
         ],
         compiler_params=pltpu.CompilerParams(vmem_limit_bytes=56 * 1024 * 1024),
         name="orthogonalize",
-    )(place, scale.reshape(1), moments, experts, inward, outward)
+    )(place, scale.reshape(1), moments, later, experts, inward, outward)
 
 
 def adamw_update(weight, mean, square, grad, rate, decay):
@@ -2117,23 +2242,19 @@
     ids = ids.reshape(mats, micros, seq_count, tokens)
     ids = ids.transpose(2, 0, 1, 3).reshape(-1) - lax.axis_index("seq") * vocab_part
     parts = [x_project, step_project, router_weight, channel_param, norm_gains]
-    found, small = lookup(ids, embedding.T, pack_small(parts), 10)
-    found, w_table, w_out, w_up, w_down = lax.optimization_barrier(
-        (
-            found,
-            embedding.T.astype(BF16),
-            out_project.astype(BF16),
-            expert_up.astype(BF16),
-            expert_down.astype(BF16),
-        )
-    )
+    wide = [expert_up_mom[0], in_project_mom, expert_down_mom[0], out_project_mom]
+    wide += [expert_up[0], expert_down[0], out_project]
+    found, small, moments, w_up, w_down, w_out = lookup(
+        ids, embedding.T, pack_small(parts), wide, 10
+    )
+    found, w_table = lax.optimization_barrier((found, embedding.T.astype(BF16)))
     small = unpack_small(small, parts)
     weights = (
         lax.all_gather(w_table, "mat", axis=0, tiled=True),
         lax.all_gather(in_project.astype(BF16), "mat", axis=1, tiled=True),
         lax.all_gather(w_out, "mat", axis=0, tiled=True),
-        lax.all_gather(w_up, "mat", axis=2, tiled=True),
-        lax.all_gather(w_down, "mat", axis=1, tiled=True),
+        lax.all_gather(w_up[None], "mat", axis=2, tiled=True),
+        lax.all_gather(w_down[None], "mat", axis=1, tiled=True),
         small[0].reshape(-1, small[0].shape[2]),
         columns(small[1]),
         small[2].reshape(-1, small[2].shape[2]),
@@ -2146,14 +2267,7 @@
     embedded = jnp.concatenate([heads, tails], axis=3).transpose(1, 2, 0, 3)
     embedded = embedded.reshape(micros * tokens, mats * part)
     loss_all = micros * lax.axis_size("mat") * loss_weight.shape[2]
-    moments = jnp.stack(
-        [
-            expert_up_mom[0],
-            in_project_mom,
-            expert_down_mom[0],
-            jnp.pad(out_project_mom, ((0, D - out_project_mom.shape[0]), (0, 0))),
-        ]
-    ).astype(BF16)
+    moments, later = jnp.split(moments, 2, axis=1)
     moments = lax.all_to_all(moments, "mat", split_axis=0, concat_axis=0, tiled=True)
     grads, x0_grad, loss_part, count_part, rows_here = step_grads(
         weights,
@@ -2199,7 +2313,7 @@
         13,
         [s_up[0], s_down[0]],
     )
-    s_in, s_out, packed = reduce_seq(
+    s_in, s_out, packed, later = reduce_seq(
         [
             s_in.reshape(seq_count, -1, D),
             s_out.reshape(seq_count, -1, D),
@@ -2207,6 +2321,7 @@
         ],
         14,
         [g_table],
+        [later],
     )
     s_up = s_up.astype(F32)
     s_down = s_down.astype(F32)
@@ -2233,17 +2348,18 @@
     ortho = orthogonalize(
         scale,
         moments,
+        later,
         whole_experts,
         whole_in.reshape(mats, D, -1),
         whole_out.reshape(mats, -1, D),
     )
     packed, ortho = lax.optimization_barrier((packed, ortho))
-    packed = packed.reshape(-1).astype(F32)
+    packed = packed.reshape(-1)
     shards, offset = [], 0
     for piece, like in zip(
         pieces, (x_project, step_project, router_weight, channel_param, norm_gains)
     ):
-        shards.append(packed[offset : offset + piece.shape[1]].reshape(like.shape))
+        shards.append(packed[offset : offset + piece.shape[1]].reshape(like.shape).astype(F32))
         offset += piece.shape[1]
     table_new = update_table(
         scale, g_table, embedding.T, embedding_mom.T, embedding_sq.T, ortho

time: 873 us -> 862 us (0.987)
  other arithmetic: 74.7 us -> 62.7 us
    unnamed x347 -> x341, local copies, waits for them, and re-layouts: 53.8 us -> 50.5 us
  transfers between devices with their start and end apart: 15 -> 15, of which waited for: 4 -> 3; matrix products, arithmetic and copies ran while one was open for 15% -> 13% of each run, Pallas kernels for 47% -> 48%
where the time goes in v4:
time: 862 us; the launch traced here: 852 us
  Pallas kernels  577 us (67%)
  local copies, waits for them, and re-layouts  96.6 us (11%)
  other arithmetic  62.7 us (7%)
  waiting for transfers between devices  39.2 us (5%)
  starting transfers between devices  27.9 us (3%)
  matrix products  27.9 us (3%)
  between operations  21.4 us (2%)
    pallas_call x4, Pallas kernels, gather_seq(): pl.pallas_call(functools.partial(gather_kernel, arrays, len(ahead), tuple...  96.7 us
    pallas_call x6, Pallas kernels, exchange(): pl.pallas_call(functools.partial(exchange_kernel, tuple(groups), tuple(ga...  84.9 us
    pallas_call x1, Pallas kernels, scatter_rows(): pl.pallas_call(functools.partial(scatter_rows_kernel, entries), out_shape...  62.6 us
    pallas_call x1, Pallas kernels, lookup(): pl.pallas_call(lookup_kernel, out_shape=[jax.ShapeDtypeStruct((mats, 384,...  62.2 us
    pallas_call x1, Pallas kernels, orthogonalize(): pl.pallas_call(ortho_kernel, out_shape=jax.ShapeDtypeStruct(experts.shape...  61.7 us
    unnamed x341, local copies, waits for them, and re-layouts  50.5 us
    pallas_call x2, Pallas kernels, reduce_seq(): pl.pallas_call(body, out_shape=[jax.ShapeDtypeStruct(shape, BF16) for sha...  42.9 us
    pallas_call x1, Pallas kernels, scan_backward(): pl.pallas_call(body, grid=(micros, inner // LANES), in_specs=[scalars, sc...  30.9 us
  transfers between devices with their start and end apart: 15, of which 3 were waited for; matrix products, arithmetic and copies ran while one was open for 13% of the time, Pallas kernels for 48%

profile of v4, /device:TPU:0, one launch (start us, length us, event | category | flops | bytes accessed | tf_op | source)
XLA Modules:
  0.0 852.3 jit_solution(1546066038630236264)
XLA Ops:
  10.2 6.0 exchange.6
  29.7 62.2 %lookup.1 = (bf16[4,384,128]{2,1,0:T(8,128)(2,1)}, bf16[4,64,1024]{2,1,0:T(8,128)(2,1)}, bf16[4,768,768]{2,1,0:T(8,128)(2,1)}, bf16[768,768]{1,0:T(8,128)(2,1)},...) custom-call(s32[8192]{0:T(1024)} %and_select_fusion.ids, f32[256,6400]{1,0:T(8,128)} %pad_convert_fusion.turned, ...), custom_call_target="tpu_custom_call" | custom-call | tf_op jit(solution)/shard_map/lookup/pallas_call | solution.py:1477
  114.3 5.8 mixer_conv.1
  123.9 14.6 %scan_end.1 = (f32[2,128,1536]{2,1,0:T(8,128)S(1)}, f32[2,128,1536]{2,1,0:T(8,128)S(1)}, bf16[32,1536]{1,0:T(8,128)(2,1)S(1)}, f32[8,1536]{1,0:T(8,128)S(1)}) custom-call(f32[2,128]{1,0:T(2,128)S(1)} %fusion.47.keep.refs_1_, f32[2,128,80]{2,1,0:T(8,128)S(1)} %get-tuple-element.96.projected, bf16[48,1536]{1,0:T(8,128)(2,1)S(1)} %bitcast.275, ...), custom_call_target="tpu_custom_call" | custom-call | tf_op jit(solution)/shard_map/scan_end/pallas_call | solution.py:373
  141.0 20.2 %gather_seq.4 = (bf16[8,2,16,1536]{3,2,1,0:T(8,128)(2,1)}, f32[8,1,8,1536]{3,2,1,0:T(8,128)}) custom-call(bf16[2,16,1536]{2,1,0:T(8,128)(2,1)} %bitcast.281, f32[1,8,1536]{2,1,0:T(8,128)} %bitcast.282), custom_call_target="tpu_custom_call" | custom-call | tf_op jit(solution)/shard_map/gather_seq/pallas_call | solution.py:1061
  165.1 17.8 %scan_forward.1 = (f32[2,128,1536]{2,1,0:T(8,128)S(1)}, f32[2,128,16,1536]{3,2,1,0:T(8,128)}, f32[2,16,1536]{2,1,0:T(8,128)S(1)}) custom-call(s32[1]{0:T(128)} %bitcast.16.place.refs_0_, f32[2,128]{1,0:T(2,128)S(1)} %fusion.47.keep.refs_1_, f32[2,128,1536]{2,1,0:T(8,128)S(1)} %get-tuple-element.97.dt.refs_2_, ...), custom_call_target="tpu_custom_call" | custom-call | tf_op jit(solution)/shard_map/scan_forward/pallas_call | solution.py:404
  190.6 16.4 %exchange.7 = bf16[8,64,768]{2,1,0:T(8,128)(2,1)} custom-call(bf16[8,64,768]{2,1,0:T(8,128)(2,1)} %bitcast.308), custom_call_target="tpu_custom_call" | custom-call | tf_op jit(solution)/shard_map/exchange/pallas_call | solution.py:749
  208.3 12.6 %experts.1 = (bf16[1,512,3072]{2,1,0:T(8,128)(2,1)S(1)}, f32[1,512,3072]{2,1,0:T(8,128)}, bf16[1,512,768]{2,1,0:T(8,128)(2,1)S(1)}) custom-call(bf16[1,512,768]{2,1,0:T(8,128)(2,1)S(1)} %bitcast.251, bf16[1,768,3072]{2,1,0:T(8,128)(2,1)} %bitcast.287, bf16[1,3072,768]{2,1,0:T(8,128)(2,1)} %bitcast.289), custom_call_target="tpu_custom_call" | custom-call | tf_op jit(solution)/shard_map/experts/pallas_call | solution.py:519
  223.5 20.7 %exchange.8 = bf16[8,64,768]{2,1,0:T(8,128)(2,1)} custom-call(bf16[8,64,768]{2,1,0:T(8,128)(2,1)} %bitcast.274), custom_call_target="tpu_custom_call" | custom-call | tf_op jit(solution)/shard_map/exchange/pallas_call | solution.py:749
  248.9 21.7 %gather_seq.5 = bf16[8,2,32,768]{3,2,1,0:T(8,128)(2,1)} custom-call(bf16[2,32,768]{2,1,0:T(8,128)(2,1)} %convolution_convert_fusion.5.refs_0_), custom_call_target="tpu_custom_call" | custom-call | tf_op jit(solution)/shard_map/gather_seq/pallas_call | solution.py:1061
  273.2 15.4 %head.1 = (f32[512,6288]{1,0:T(8,128)}, f32[512,8]{1,0:T(8,128)S(1)}) custom-call(s32[3]{0:T(128)S(1)} %pad_add_fusion.limits, bf16[512,768]{1,0:T(8,128)(2,1)S(1)} %bitcast.254, bf16[768,6288]{1,0:T(8,128)(2,1)} %all-gather.12.cloned.1.call-done.table, s32[512,1]{1,0:T(8,128)S(1)} %copy-done.24), custom_call_target="tpu_custom_call" | custom-call | tf_op jit(solution)/shard_map/head/pallas_call | solution.py:634
  289.3 8.5 exchange.9
  299.7 20.1 %head_back.1 = (bf16[768,6288]{1,0:T(8,128)(2,1)}, bf16[512,768]{1,0:T(8,128)(2,1)S(1)}) custom-call(s32[3]{0:T(128)S(1)} %pad_add_fusion.limits, bf16[768,512]{1,0:T(8,128)(2,1)S(1)} %bitcast.258, bf16[768,6288]{1,0:T(8,128)(2,1)} %all-gather.12.cloned.1.call-done.table, s32[512,1]{1,0:T(8,128)S(1)} %copy-done.24, f32[512,8]{1,0:T(8,128)S(1)} %pad.32.scalars, ...), custom_call_target="tpu_custom_call" | custom-call | tf_op jit(solution)/shard_map/head_back/pallas_call | solution.py:652
  321.8 12.9 %reduce_seq.2 = bf16[4,64,768]{2,1,0:T(8,128)(2,1)S(1)} custom-call(bf16[8,64,768]{2,1,0:T(8,128)(2,1)S(1)} %bitcast.273), custom_call_target="tpu_custom_call" | custom-call | tf_op jit(solution)/shard_map/reduce_seq/pallas_call | solution.py:1246
  339.5 14.2 %exchange.10 = bf16[8,64,768]{2,1,0:T(8,128)(2,1)} custom-call(bf16[8,64,768]{2,1,0:T(8,128)(2,1)} %bitcast.305, bf16[768,6288]{1,0:T(8,128)(2,1)} %get-tuple-element.111.refs_1_), custom_call_target="tpu_custom_call" | custom-call | tf_op jit(solution)/shard_map/exchange/pallas_call | solution.py:749
  356.8 17.3 %experts_back.1 = (bf16[1,768,3072]{2,1,0:T(8,128)(2,1)}, bf16[1,3072,768]{2,1,0:T(8,128)(2,1)}, bf16[1,512,768]{2,1,0:T(8,128)(2,1)S(1)}) custom-call(bf16[1,512,768]{2,1,0:T(8,128)(2,1)S(1)} %bitcast.252, bf16[1,512,768]{2,1,0:T(8,128)(2,1)S(1)} %bitcast.257, bf16[1,768,3072]{2,1,0:T(8,128)(2,1)} %bitcast.288, bf16[1,3072,768]{2,1,0:T(8,128)(2,1)} %bitcast.290, ...), custom_call_target="tpu_custom_call" | custom-call | tf_op jit(solution)/shard_map/experts_back/pallas_call | solution.py:538
  374.9 19.1 %exchange.11 = bf16[8,64,768]{2,1,0:T(8,128)(2,1)} custom-call(bf16[8,64,768]{2,1,0:T(8,128)(2,1)} %bitcast.272, bf16[768,6288]{1,0:T(8,128)(2,1)} %get-tuple-element.111.refs_1_), custom_call_target="tpu_custom_call" | custom-call | tf_op jit(solution)/shard_map/exchange/pallas_call | solution.py:749
  399.2 5.4 reduce-scatter.6.cloned.1.call-done.refs_2_
  432.2 7.6 scan_start.1
  440.5 19.3 %gather_seq.6 = bf16[8,2,16,1536]{3,2,1,0:T(8,128)(2,1)} custom-call(bf16[2,16,1536]{2,1,0:T(8,128)(2,1)} %bitcast.278), custom_call_target="tpu_custom_call" | custom-call | tf_op jit(solution)/shard_map/gather_seq/pallas_call | solution.py:1061
  463.7 30.9 %scan_backward.1 = (f32[2,128,1536]{2,1,0:T(8,128)S(1)}, f32[2,128,1536]{2,1,0:T(8,128)S(1)}, f32[2,128,16,128]{3,2,1,0:T(8,128)}, f32[2,128,16,128]{3,2,1,0:T(8,128)}, f32[2,16,1536]{2,1,0:T(8,128)S(1)}) custom-call(s32[1]{0:T(128)} %bitcast.16.place.refs_0_, f32[2,128]{1,0:T(2,128)S(1)} %fusion.47.keep.refs_1_, f32[2,128,1536]{2,1,0:T(8,128)} %copy-done.4, ...), custom_call_target="tpu_custom_call" | custom-call | tf_op jit(solution)/shard_map/scan_backward/pallas_call | solution.py:448
  501.0 7.4 mixer_conv_back.1
  517.4 5.0 convolution_convert_fusion
  539.9 10.3 %all-to-all-done.1 = bf16[4,896,128]{2,1,0:T(8,128)(2,1)S(1)} async-done(((bf16[4,896,128]{2,1,0:T(8,128)(2,1)}), bf16[4,896,128]{2,1,0:T(8,128)(2,1)S(1)}, u32[]{:S(2)}, u32[]{:S(2)}) %all-to-all-start.1) | async-done | bytes 917536 | tf_op jit(solution)/shard_map/all_to_all | solution.py:2300
  554.6 62.6 %scatter_rows.1 = (f32[6400,256]{1,0:T(8,128)}, f32[8,256]{1,0:T(8,128)S(1)}, bf16[4,768,768]{2,1,0:T(8,128)(2,1)}) custom-call(s32[64,128]{1,0:T(8,128)S(1)} %bitcast.280, bf16[4,384,128]{2,1,0:T(8,128)(2,1)S(1)} %slice.199.rows, bf16[192,6400]{1,0:T(8,128)(2,1)S(1)} %copy-done.6, bf16[768,768]{1,0:T(8,128)(2,1)S(1)} %bitcast.255, ...), custom_call_target="tpu_custom_call" | custom-call | tf_op jit(solution)/shard_map/scatter_rows/pallas_call | solution.py:1670
  620.2 30.0 %reduce_seq.3 = (bf16[4,96,768]{2,1,0:T(8,128)(2,1)S(1)}, bf16[4,48,768]{2,1,0:T(8,128)(2,1)S(1)}, bf16[4,64,128]{2,1,0:T(8,128)(2,1)S(1)}, bf16[4,384,768]{2,1,0:T(8,128)(2,1)S(1)}) custom-call(bf16[8,96,768]{2,1,0:T(8,128)(2,1)S(1)} %bitcast.270, bf16[8,48,768]{2,1,0:T(8,128)(2,1)S(1)} %bitcast.276, bf16[8,64,128]{2,1,0:T(8,128)(2,1)S(1)} %bitcast.277, ...), custom_call_target="tpu_custom_call" | custom-call | tf_op jit(solution)/shard_map/reduce_seq/pallas_call | solution.py:1246
  660.0 35.6 %gather_seq.7 = (bf16[8,2,48,768]{3,2,1,0:T(8,128)(2,1)}, bf16[8,1,48,768]{3,2,1,0:T(8,128)(2,1)}, bf16[8,2,32,128]{3,2,1,0:T(8,128)(2,1)}, f32[32,8,128]{2,1,0:...) custom-call(bf16[2,48,768]{2,1,0:T(8,128)(2,1)} %bitcast.338, ...), custom_call_target="tpu_custom_call" | custom-call | tf_op jit(solution)/shard_map/gather_seq/pallas_call | solution.py:1061
  698.0 61.7 %orthogonalize.1._ahead = bf16[4,768,768]{2,1,0:T(8,128)(2,1)} custom-call(s32[1]{0:T(128)} %bitcast.111.place, f32[1]{0:T(128)} %bitcast.107.scale, bf16[4,384,768]{2,1,0:T(8,128)(2,1)} %all-to-all-done.moments, bf16[4,384,768]{2,1,0:T(8,128)(2,1)} %copy-done.25, bf16[4,768,768]{2,1,0:T(8,128)(2,1)} %get-tuple-element.142.experts, ...), custom_call_target="tpu_custom_call" | custom-call | tf_op jit(solution)/shard_map/orthogonalize/pallas_call | solution.py:2136
  764.1 14.3 %all-to-all-start.2 = ((bf16[4,768,768]{2,1,0:T(8,128)(2,1)}), bf16[4,768,768]{2,1,0:T(8,128)(2,1)}, u32[]{:S(2)}, u32[]{:S(2)}) async-start(bf16[4,768,768]{2,1,0:T(8,128)(2,1)} %orthogonalize.1._ahead), calls=%async_computation.7 | async-start | bytes 9437184 | tf_op jit(solution)/shard_map/all_to_all | solution.py:2368
  783.5 16.2 %update_table.1 = (f32[192,6288]{1,0:T(8,128)}, f32[192,6288]{1,0:T(8,128)}, f32[192,6288]{1,0:T(8,128)}) custom-call(f32[1]{0:T(128)} %bitcast.107.scale, f32[6400,256]{1,0:T(8,128)} %get-tuple-element.133.refs_4_.grad, f32[192,6288]{1,0:T(8,128)} %bitcast.286, f32[192,6288]{1,0:T(8,128)} %bitcast.301, f32[192,6288]{1,0:T(8,128)} %bitcast.302, ...), custom_call_target="tpu_custom_call" | custom-call | flops 32194560 | bytes 45072384 | tf_op jit(solution)/shard_map/update_table/pallas_call | solution.py:2179
  812.2 20.2 %all-to-all-done.2 = bf16[4,768,768]{2,1,0:T(8,128)(2,1)} async-done(((bf16[4,768,768]{2,1,0:T(8,128)(2,1)}), bf16[4,768,768]{2,1,0:T(8,128)(2,1)}, u32[]{:S(2)}, u32[]{:S(2)}) %all-to-all-start.2) | async-done | bytes 4718624 | tf_op jit(solution)/shard_map/all_to_all | solution.py:2368
  832.4 6.1 multiply_subtract_fusion
  (575 shorter events, 192.9 us)
Async XLA Ops:
  7.3 91.9 %all-gather.8.cloned.1.call-start = ((), (), s32[]{:S(2)}) async-start(), calls=%async_computation.8 | async-start | bytes 5898240 | tf_op jit(solution)/shard_map/all_gather | solution.py:2254
  10.2 176.0 %all-gather.10.cloned.1.call-start = ((), (), s32[]{:S(2)}) async-start(), calls=%async_computation.9 | async-start | bytes 2949120 | tf_op jit(solution)/shard_map/all_gather | solution.py:2255
  91.9 115.2 %all-gather.14.cloned.1.call-start = ((), (), s32[]{:S(2)}) async-start(), calls=%async_computation.16 | async-start | bytes 5898240 | tf_op jit(solution)/shard_map/all_gather | solution.py:2256
  92.6 114.5 %all-gather.16.cloned.1.call-start = ((), (), s32[]{:S(2)}) async-start(), calls=%async_computation.17 | async-start | bytes 5898240 | tf_op jit(solution)/shard_map/all_gather | solution.py:2257
  93.2 178.8 %all-gather.12.cloned.1.call-start = ((), (), s32[]{:S(2)}) async-start(), calls=%async_computation.10 | async-start | bytes 12288000 | tf_op jit(solution)/shard_map/all_gather | solution.py:2253
  93.8 310.8 %reduce-scatter.6.cloned.1.call-start = ((), (), s32[]{:S(2)}) async-start(), calls=%async_computation.11 | async-start | bytes 12288000 | tf_op jit(solution)/shard_map/reduce_scatter | solution.py:1957
  102.9 11.3 %collective-permute-start = (f32[2,3,1536]{2,1,0:T(4,128)S(1)}, f32[2,3,1536]{2,1,0:T(4,128)S(1)}, u32[]{:S(2)}, u32[]{:S(2)}) collective-permute-start(f32[2,3,1536]{2,1,0:T(4,128)S(1)} %slice.181), channel_id=1, source_target_pairs={{0,4},{4,8},{8,12},{12,16},{16,20},{20,24},{24,28},{1,5},{5,9},{9,... | collective-permute-start | bytes 110600 | tf_op jit(solution)/shard_map/ppermute | solution.py:1702
  121.2 301.3 %copy-start = (f32[2,128,1536]{2,1,0:T(8,128)}, f32[2,128,1536]{2,1,0:T(8,128)S(1)}, u32[]{:S(2)}) copy-start(f32[2,128,1536]{2,1,0:T(8,128)S(1)} %get-tuple-element.95.act.refs_3_) | copy-start | bytes 4718596
  141.0 41.9 %copy-start.4 = (f32[2,128,1536]{2,1,0:T(8,128)}, f32[2,128,1536]{2,1,0:T(8,128)S(1)}, u32[]{:S(2)}) copy-start(f32[2,128,1536]{2,1,0:T(8,128)S(1)} %get-tuple-element.97.dt.refs_2_) | copy-start | bytes 4718596
  165.1 19.7 %copy-start.59 = (f32[2,128,3072]{2,1,0:T(8,128)S(1)}, f32[2,128,3072]{2,1,0:T(8,128)}, u32[]{:S(2)}) copy-start(f32[2,128,3072]{2,1,0:T(8,128)} %copy-done.58) | copy-start | bytes 9437188
  165.1 19.7 %copy-start.110 = (f32[1536]{0:T(1024)S(1)}, f32[1536]{0:T(1024)}, u32[]{:S(2)}) copy-start(f32[1536]{0:T(1024)} %mul.596) | copy-start | bytes 18436
  189.0 57.6 %copy-start.61 = (f32[256,768]{1,0:T(8,128)}, f32[256,768]{1,0:T(8,128)S(1)}, u32[]{:S(2)}) copy-start(f32[256,768]{1,0:T(8,128)S(1)} %get-tuple-element.366) | copy-start | bytes 2359300
  189.2 56.2 %copy-start.84 = (bf16[256,768]{1,0:T(8,128)(2,1)}, bf16[256,768]{1,0:T(8,128)(2,1)S(1)}, u32[]{:S(2)}) copy-start(bf16[256,768]{1,0:T(8,128)(2,1)S(1)} %multiply_convert_fusion.4) | copy-start | bytes 1179652
  223.5 21.9 %copy-start.89 = (bf16[768,8]{1,0:T(8,128)(2,1)S(1)}, bf16[768,8]{1,0:T(8,128)(2,1)}, u32[]{:S(2)}) copy-start(bf16[768,8]{1,0:T(8,128)(2,1)} %reshape_reshape.18) | copy-start | bytes 36868
  223.5 21.9 %copy-start.117 = (s32[2,1,128,1]{2,3,1,0:T(1,128)S(1)}, s32[2,1,128,1]{2,3,1,0:T(1,128)}, u32[]{:S(2)}) copy-start(s32[2,1,128,1]{2,3,1,0:T(1,128)} %param.33) | copy-start | bytes 3076
  223.5 22.8 %copy-start.126 = (s32[2,128]{1,0:T(2,128)S(1)}, s32[2,128]{1,0:T(2,128)}, u32[]{:S(2)}) copy-start(s32[2,128]{1,0:T(2,128)} %add_add_fusion) | copy-start | bytes 3076
  246.9 25.1 %copy-start.24 = (s32[512,1]{1,0:T(8,128)S(1)}, s32[512,1]{1,0:T(8,128)}, u32[]{:S(2)}) copy-start(s32[512,1]{1,0:T(8,128)} %broadcast_in_dim_reshape.5.targets) | copy-start | bytes 6148
  273.2 26.4 %copy-start.146 = (f32[512,1]{0,1:T(1,128)S(1)}, f32[512,1]{0,1:T(1,128)}, u32[]{:S(2)}) copy-start(f32[512,1]{0,1:T(1,128)} %div.135) | copy-start | bytes 6148
  320.7 229.6 %reduce-scatter.12.cloned.1.call-start = ((), (), s32[]{:S(2)}) async-start(), calls=%async_computation.14 | async-start | bytes 5898240 | tf_op jit(solution)/shard_map/reduce_scatter | solution.py:1957
  374.9 20.5 %copy-start.140 = (f32[256]{0:T(256)S(1)}, f32[256]{0:T(256)}, u32[]{:S(2)}) copy-start(f32[256]{0:T(256)} %copy-done.139) | copy-start | bytes 3076
  374.9 20.5 %copy-start.152 = (f32[256]{0:T(256)S(1)}, f32[256]{0:T(256)}, u32[]{:S(2)}) copy-start(f32[256]{0:T(256)} %get-tuple-element.336) | copy-start | bytes 3076
  374.9 20.5 %copy-start.128 = (s32[2,128]{1,0:T(2,128)S(1)}, s32[2,128]{1,0:T(2,128)}, u32[]{:S(2)}) copy-start(s32[2,128]{1,0:T(2,128)} %add_add_fusion) | copy-start | bytes 3076
  396.9 22.9 %copy-start.63 = (f32[256,768]{1,0:T(8,128)}, f32[256,768]{1,0:T(8,128)S(1)}, u32[]{:S(2)}) copy-start(f32[256,768]{1,0:T(8,128)S(1)} %multiply_add_fusion.3) | copy-start | bytes 2359300
  404.6 145.7 %reduce-scatter.14.cloned.1.call-start = ((), (), s32[]{:S(2)}) async-start(), calls=%async_computation.15 | async-start | bytes 5898240 | tf_op jit(solution)/shard_map/reduce_scatter | solution.py:1957
  405.4 212.4 %reduce-scatter.10.cloned.1.call-start = ((), (), s32[]{:S(2)}) async-start(), calls=%async_computation.13 | async-start | bytes 2949120 | tf_op jit(solution)/shard_map/reduce_scatter | solution.py:1957
  411.0 117.9 %all-to-all-start = ((bf16[4,384,768]{2,1,0:T(8,128)(2,1)}), bf16[4,384,768]{2,1,0:T(8,128)(2,1)}, u32[]{:S(2)}, u32[]{:S(2)}) async-start(bf16[4,384,768]{2,1,0:T(8,128)(2,1)} %get-tuple-element.344), calls=%async_computation.3 | async-start | bytes 4718592 | tf_op jit(solution)/shard_map/all_to_all | solution.py:2271
  415.7 202.1 %reduce-scatter.8.cloned.1.call-start = ((), (), s32[]{:S(2)}) async-start(), calls=%async_computation.12 | async-start | bytes 5898240 | tf_op jit(solution)/shard_map/reduce_scatter | solution.py:1957
  463.7 30.9 %copy-start.34 = (f32[2,128,1536]{2,1,0:T(8,128)S(1)}, f32[2,128,1536]{2,1,0:T(8,128)}, u32[]{:S(2)}) copy-start(f32[2,128,1536]{2,1,0:T(8,128)} %copy-done.33) | copy-start | bytes 4718596
  509.5 6.9 collective-permute-start.1
  530.7 19.5 %all-to-all-start.1 = ((bf16[4,896,128]{2,1,0:T(8,128)(2,1)}), bf16[4,896,128]{2,1,0:T(8,128)(2,1)S(1)}, u32[]{:S(2)}, u32[]{:S(2)}) async-start(bf16[4,896,128]{2,1,0:T(8,128)(2,1)} %pad_maximum_fusion.1), calls=%async_computation.4 | async-start | bytes 1835008 | tf_op jit(solution)/shard_map/all_to_all | solution.py:2300
  698.0 61.7 %copy-start.101 = (bf16[8,2,32,128]{3,2,1,0:T(8,128)(2,1)S(1)}, bf16[8,2,32,128]{3,2,1,0:T(8,128)(2,1)}, u32[]{:S(2)}) copy-start(bf16[8,2,32,128]{3,2,1,0:T(8,128)(2,1)} %get-tuple-element.139) | copy-start | bytes 393220
  764.1 68.2 %all-to-all-start.2 = ((bf16[4,768,768]{2,1,0:T(8,128)(2,1)}), bf16[4,768,768]{2,1,0:T(8,128)(2,1)}, u32[]{:S(2)}, u32[]{:S(2)}) async-start(bf16[4,768,768]{2,1,0:T(8,128)(2,1)} %orthogonalize.1._ahead), calls=%async_computation.7 | async-start | bytes 9437184 | tf_op jit(solution)/shard_map/all_to_all | solution.py:2368
  (142 other events, 732.0 us)
Sparse Core Ops, SparseCore 0:
  10.3 49.2 all-gather.7
  92.0 22.8 all-gather.9
  116.5 37.4 all-gather.13
  155.4 37.5 all-gather.15
  194.9 66.4 all-gather.11
  320.8 83.7 reduce-scatter.5
  407.7 63.1 reduce-scatter.11
  474.2 47.9 reduce-scatter.13
  525.3 35.6 reduce-scatter.9
  564.2 49.1 reduce-scatter.7
